TPU v7x, 32 devices: a whole 2x2x4 slice. The times are simulated.
32 devices in a mesh: dp: 4 (over z), rows: 8 (over y, x, core).
Axes of the slice: x: 2, y: 2, z: 4, core: 2. Of those that a mesh axis runs over, the one named last changes fastest.
Arguments:
- item_ids: int32 [2, 32, 512], P(None, ('dp', 'rows')), may hold values from 0 to 200703, as said below
- targets: int32 [2, 32, 512], P(None, ('dp', 'rows')), may hold values from 0 to 200703, as said below
- lengths: int32 [2, 32], P(None, ('dp', 'rows')), may hold values from 1 to 512, as said below
- correction: float32 [2, 32, 512], P(None, ('dp', 'rows')), may hold values from -9 to -6
- item_row: int32 [200704], replicated, may hold values from 0 to 200703, as said below
- item_table: float32 [200704, 256], P(('dp', 'rows')), may hold values from -0.6 to 0.6
- qkv_weight: float32 [256, 1536], replicated, may hold values from -0.375 to 0.375
- out_weight: float32 [512, 256], replicated, may hold values from -1 to 1
- up_weight: float32 [256, 1024], replicated, may hold values from -0.375 to 0.375
- down_weight: float32 [1024, 256], replicated, may hold values from -0.1875 to 0.1875
- positions: float32 [512, 256], replicated, may hold values from -0.6 to 0.6
- gains: float32 [3, 256], replicated, may hold values from 0.5 to 1.5
- item_table_first: float32 [200704, 256], P(('dp', 'rows')), may hold values from -0.00015258789 to 0.00015258789
- qkv_weight_first: float32 [256, 1536], replicated, may hold values from -0.0004272461 to 0.0004272461
- out_weight_first: float32 [512, 256], replicated, may hold values from -0.0004272461 to 0.0004272461
- up_weight_first: float32 [256, 1024], replicated, may hold values from -0.0004272461 to 0.0004272461
- down_weight_first: float32 [1024, 256], replicated, may hold values from -0.0004272461 to 0.0004272461
- positions_first: float32 [512, 256], replicated, may hold values from -7.6293945e-05 to 7.6293945e-05
- gains_first: float32 [3, 256], replicated, may hold values from -0.0017089844 to 0.0017089844
- item_table_second: float32 [200704, 256], P(('dp', 'rows')), may hold values from 5.960465e-11 to 2.384186e-10
- qkv_weight_second: float32 [256, 1536], replicated, may hold values from 4.2385526e-10 to 1.695421e-09
- out_weight_second: float32 [512, 256], replicated, may hold values from 4.2385526e-10 to 1.695421e-09
- up_weight_second: float32 [256, 1024], replicated, may hold values from 4.2385526e-10 to 1.695421e-09
- down_weight_second: float32 [1024, 256], replicated, may hold values from 4.2385526e-10 to 1.695421e-09
- positions_second: float32 [512, 256], replicated, may hold values from 1.4901162e-11 to 5.960465e-11
- gains_second: float32 [3, 256], replicated, may hold values from 6.781684e-09 to 2.7126736e-08
Outputs:
- new_item_table: float32 [200704, 256], P(('dp', 'rows'))
- new_qkv_weight: float32 [256, 1536], replicated
- new_out_weight: float32 [512, 256], replicated
- new_up_weight: float32 [256, 1024], replicated
- new_down_weight: float32 [1024, 256], replicated
- new_positions: float32 [512, 256], replicated
- new_gains: float32 [3, 256], replicated
- new_item_table_first: float32 [200704, 256], P(('dp', 'rows'))
- new_qkv_weight_first: float32 [256, 1536], replicated
- new_out_weight_first: float32 [512, 256], replicated
- new_up_weight_first: float32 [256, 1024], replicated
- new_down_weight_first: float32 [1024, 256], replicated
- new_positions_first: float32 [512, 256], replicated
- new_gains_first: float32 [3, 256], replicated
- new_item_table_second: float32 [200704, 256], P(('dp', 'rows'))
- new_qkv_weight_second: float32 [256, 1536], replicated
- new_out_weight_second: float32 [512, 256], replicated
- new_up_weight_second: float32 [256, 1024], replicated
- new_down_weight_second: float32 [1024, 256], replicated
- new_positions_second: float32 [512, 256], replicated
- new_gains_second: float32 [3, 256], replicated
- loss_sum: float32 [], replicated
- valid_count: float32 [], replicated
- grad_norm: float32 [], replicated
Inputs may be any that keep to these rules, and one draw needn't show every extreme that they name: Owner block o holds table rows o * 6272 to (o + 1) * 6272 - 1, and device o in the order dp then rows holds it. Among the item_ids and targets of the histories of one device (both micro-batches), the entries at positions below their history's length whose table row lies in one owner block number at most 98; in every draw some owner block gets exactly 98 from every device. `targets`: counted together with item_ids in the bound stated there. `lengths`: some history has all 512 positions. A permutation: item i is stored in table row item_row[i].
All inputs are finite; a program needn't handle non-finite values.
Results may differ from a plain program's by a relative error of at most 0.012.
The roundings to bfloat16 on the way count: a program that leaves them out, or rounds other values in their place, can miss the bound.
Values may be sent and summed in bfloat16 or wider, within the bound.
A program may use at most 256 MiB of HBM per device.

v0:
```python
import math

import jax
import jax.numpy as jnp
from jax import lax
from jax.sharding import PartitionSpec as P

HEADS = 8
STEP = 10


NORM_EPS = 1e-06
MASKED = -1e30
BETA_ONE = 0.9
BETA_TWO = 0.999
ADAM_EPS = 1e-08
DECAY = 0.01
RATE = 0.1
GAIN_RATE = 1.0
CLIP = 1.0


def rounded(values):
    return values.astype(jnp.bfloat16)


def matmul(first_op, second_op):
    return jnp.dot(first_op, second_op, preferred_element_type=jnp.float32)


def inner_rows(first_op, second_op):
    return lax.dot_general(
        first_op, second_op, (((0,), (0,)), ((), ())), preferred_element_type=jnp.float32
    )


def inner_cols(first_op, second_op):
    return lax.dot_general(
        first_op, second_op, (((1,), (1,)), ((), ())), preferred_element_type=jnp.float32
    )


def rms_norm(values, gain_row):
    return (
        values * lax.rsqrt(jnp.mean(values * values, axis=-1, keepdims=True) + NORM_EPS) * gain_row
    )


def gelu_tanh(values):
    return jax.nn.gelu(values)


def split_heads(joined, histories, head_count):
    pieces = joined.reshape(histories, joined.shape[0] // histories, 3, head_count, -1)
    return (pieces[:, :, 0], pieces[:, :, 1], pieces[:, :, 2])


def masked_scores(queries, key_rows, lengths_here):
    length = queries.shape[1]
    scaling = queries.shape[-1] ** (-0.5)
    scores = (
        jnp.einsum("sqhe,skhe->shqk", queries, key_rows, preferred_element_type=jnp.float32)
        * scaling
    )
    position = jnp.arange(length, dtype=jnp.int32)
    allowed = (position[None, :] <= position[:, None])[None, None] & (
        position[None, None, None, :] < lengths_here[:, None, None, None]
    )
    return jnp.where(allowed, scores, MASKED)


def attention_forward(joined, lengths_here, head_count):
    queries, key_rows, value_rows = split_heads(joined, lengths_here.shape[0], head_count)
    scores = masked_scores(queries, key_rows, lengths_here)
    highest = jnp.max(scores, axis=-1, keepdims=True)
    log_total = highest + jnp.log(jnp.sum(jnp.exp(scores - highest), axis=-1, keepdims=True))
    probabilities = rounded(jnp.exp(scores - log_total))
    attended = jnp.einsum(
        "shqk,skhe->sqhe", probabilities, value_rows, preferred_element_type=jnp.float32
    )
    return (attended.reshape(joined.shape[0], -1), log_total)


def attention_backward(joined, log_total, lengths_here, grad_attended, head_count):
    queries, key_rows, value_rows = split_heads(joined, lengths_here.shape[0], head_count)
    probabilities = jnp.exp(masked_scores(queries, key_rows, lengths_here) - log_total)
    grad_heads = grad_attended.reshape(queries.shape)
    grad_probs = jnp.einsum(
        "sqhe,skhe->shqk", grad_heads, value_rows, preferred_element_type=jnp.float32
    )
    grad_values = jnp.einsum(
        "shqk,sqhe->skhe", rounded(probabilities), grad_heads, preferred_element_type=jnp.float32
    )
    row_inner = jnp.sum(probabilities * grad_probs, axis=-1, keepdims=True)
    grad_scores = rounded(probabilities * (grad_probs - row_inner))
    scaling = queries.shape[-1] ** (-0.5)
    grad_queries = (
        jnp.einsum("shqk,skhe->sqhe", grad_scores, key_rows, preferred_element_type=jnp.float32)
        * scaling
    )
    grad_keys = (
        jnp.einsum("shqk,sqhe->skhe", grad_scores, queries, preferred_element_type=jnp.float32)
        * scaling
    )
    stacked = jnp.stack([grad_queries, grad_keys, grad_values], axis=2)
    return stacked.reshape(joined.shape[0], -1)


def layer_forward(embedded, lengths_here, matrices, gains, head_count):
    qkv_low, out_low, up_low, down_low = matrices
    normed_one, back_one = jax.vjp(rms_norm, embedded, gains[0])
    hidden_one = rounded(normed_one)
    joined = rounded(matmul(hidden_one, qkv_low))
    attended, log_total = attention_forward(joined, lengths_here, head_count)
    attended_low = rounded(attended)
    middle = embedded + matmul(attended_low, out_low)
    normed_two, back_two = jax.vjp(rms_norm, middle, gains[1])
    hidden_two = rounded(normed_two)
    upward = matmul(hidden_two, up_low)
    active, back_active = jax.vjp(gelu_tanh, upward)
    active_low = rounded(active)
    output = middle + matmul(active_low, down_low)
    return (
        output,
        (
            back_one,
            hidden_one,
            joined,
            log_total,
            attended_low,
            back_two,
            hidden_two,
            back_active,
            active_low,
        ),
    )


def layer_backward(grad_output, saved_state, lengths_here, matrices, head_count):
    (
        back_one,
        hidden_one,
        joined,
        log_total,
        attended_low,
        back_two,
        hidden_two,
        back_active,
        active_low,
    ) = saved_state
    qkv_low, out_low, up_low, down_low = matrices
    grad_branch = rounded(grad_output)
    grad_down = inner_rows(active_low, grad_branch)
    grad_upward = rounded(back_active(inner_cols(grad_branch, down_low))[0])
    grad_up = inner_rows(hidden_two, grad_upward)
    grad_middle, gain_two = back_two(inner_cols(grad_upward, up_low))
    grad_middle = grad_middle + grad_output
    grad_attn = rounded(grad_middle)
    grad_out = inner_rows(attended_low, grad_attn)
    grad_attended = rounded(inner_cols(grad_attn, out_low))
    grad_joined = rounded(
        attention_backward(joined, log_total, lengths_here, grad_attended, head_count)
    )
    grad_qkv = inner_rows(hidden_one, grad_joined)
    grad_embedded, gain_one = back_one(inner_cols(grad_joined, qkv_low))
    return (
        grad_embedded + grad_middle,
        (grad_qkv, grad_out, grad_up, grad_down),
        (gain_one, gain_two),
    )


def candidate_loss(query_low, candidates, cand_bias, valid_here, offset):
    tokens, width = query_low.shape
    block_rows = min(512, tokens)
    blocks = tokens // block_rows
    column = jnp.arange(candidates.shape[0], dtype=jnp.int32)
    bias_wide = cand_bias.astype(jnp.float32)

    def one_block(running, block_pieces):
        query_block, valid_block, start_row = block_pieces
        logits = inner_cols(query_block, candidates) + bias_wide[None]
        highest = jnp.max(logits, axis=1, keepdims=True)
        log_total = highest + jnp.log(jnp.sum(jnp.exp(logits - highest), axis=1, keepdims=True))
        target_hit = (
            column[None, :]
            == (offset + start_row + jnp.arange(block_rows, dtype=jnp.int32))[:, None]
        )
        own_logit = jnp.sum(jnp.where(target_hit, logits, 0.0), axis=1)
        grad_logits = rounded(
            (jnp.exp(logits - log_total) - target_hit.astype(jnp.float32)) * valid_block[:, None]
        )
        return (
            running + jnp.sum(valid_block * (log_total[:, 0] - own_logit)),
            (grad_logits, log_total[:, 0]),
        )

    loss_part, block_out = lax.scan(
        one_block,
        jnp.zeros((), jnp.float32),
        (
            query_low.reshape(blocks, block_rows, width),
            valid_here.reshape(blocks, block_rows),
            jnp.arange(blocks, dtype=jnp.int32) * block_rows,
        ),
    )
    return (loss_part, block_out[0].reshape(tokens, -1), block_out[1].reshape(tokens))


def send_requests(asked_rows):
    moved = lax.all_to_all(asked_rows, ("dp", "rows"), split_axis=0, concat_axis=0, tiled=True)
    return moved


def send_replies(found_rows):
    moved = lax.all_to_all(found_rows, ("dp", "rows"), split_axis=0, concat_axis=0, tiled=True)
    return moved


def send_grads(row_terms):
    moved = lax.all_to_all(row_terms, ("dp", "rows"), split_axis=0, concat_axis=0, tiled=True)
    return moved


def adam_step(weight, gradient, first, second, rate, decay):
    first_new = BETA_ONE * first + (1.0 - BETA_ONE) * gradient
    second_new = BETA_TWO * second + (1.0 - BETA_TWO) * gradient * gradient
    stepped = (
        first_new
        / (1.0 - BETA_ONE**STEP)
        / (jnp.sqrt(second_new / (1.0 - BETA_TWO**STEP)) + ADAM_EPS)
    )
    return (weight - rate * (stepped + decay * weight), first_new, second_new)


def local(
    item_ids,
    targets,
    lengths,
    correction,
    item_row,
    item_table,
    qkv_weight,
    out_weight,
    up_weight,
    down_weight,
    positions,
    gains,
    item_table_first,
    qkv_weight_first,
    out_weight_first,
    up_weight_first,
    down_weight_first,
    positions_first,
    gains_first,
    item_table_second,
    qkv_weight_second,
    out_weight_second,
    up_weight_second,
    down_weight_second,
    positions_second,
    gains_second,
):
    micro, histories, length = item_ids.shape
    rows_here, width = item_table.shape
    devices = lax.axis_size("dp") * lax.axis_size("rows")
    tokens = histories * length
    requests = 2 * micro * tokens
    capacity = 3 * (requests + devices) // (2 * devices) + 1
    position = jnp.arange(length, dtype=jnp.int32)
    valid_pos = (position[None, None, :] < lengths[:, :, None]).reshape(micro, tokens)
    wanted = jnp.stack([item_ids, targets]).reshape(requests)
    live_request = jnp.concatenate([valid_pos.reshape(-1), valid_pos.reshape(-1)])
    table_rows = item_row[wanted]
    owner_of = table_rows // rows_here
    choose = (
        (owner_of[:, None] == jnp.arange(devices, dtype=jnp.int32)[None, :]) & live_request[:, None]
    ).astype(jnp.int32)
    earlier = jnp.sum((jnp.cumsum(choose, axis=0) - choose) * choose, axis=1)
    slot_of = jnp.where(live_request, owner_of * capacity + earlier, devices * capacity)
    asked_rows = (
        jnp.zeros((devices * capacity,), jnp.int32)
        .at[slot_of]
        .set(table_rows % rows_here, mode="drop")
    )
    received = send_requests(asked_rows.reshape(devices, capacity))
    replies = send_replies(rounded(item_table)[received]).reshape(devices * capacity, width)
    fetched = jnp.where(
        live_request[:, None],
        replies[jnp.minimum(slot_of, devices * capacity - 1)],
        jnp.zeros((), jnp.bfloat16),
    )
    fetched = fetched.reshape(2, micro, tokens, width)
    matrices = (rounded(qkv_weight), rounded(out_weight), rounded(up_weight), rounded(down_weight))
    scaling = math.sqrt(width)
    offset = lax.axis_index("rows") * tokens
    running = [
        jnp.zeros_like(qkv_weight),
        jnp.zeros_like(out_weight),
        jnp.zeros_like(up_weight),
        jnp.zeros_like(down_weight),
    ]
    grad_positions = jnp.zeros_like(positions)
    grad_gains = jnp.zeros_like(gains)
    loss_local = jnp.zeros((), jnp.float32)
    embed_grads = []
    target_grads = []
    for micro_index in range(micro):
        lengths_here = lengths[micro_index]
        valid_here = valid_pos[micro_index].astype(jnp.float32)
        embedded = scaling * fetched[0, micro_index].astype(jnp.float32) + jnp.tile(
            positions, (histories, 1)
        )
        output, saved_state = layer_forward(embedded, lengths_here, matrices, gains, HEADS)
        normed_three, back_three = jax.vjp(rms_norm, output, gains[2])
        query_low = rounded(normed_three)
        bias_low = jnp.where(
            valid_pos[micro_index],
            rounded(-correction[micro_index].reshape(-1)),
            jnp.asarray(MASKED, jnp.bfloat16),
        )
        candidates, cand_bias = (
            lax.all_gather(fetched[1, micro_index], "rows", axis=0, tiled=True),
            lax.all_gather(bias_low, "rows", axis=0, tiled=True),
        )
        loss_part, grad_logits, log_total = candidate_loss(
            query_low, candidates, cand_bias, valid_here, offset
        )
        loss_local = loss_local + loss_part
        grad_output, gain_three = back_three(matmul(grad_logits, candidates))
        target_grads.append(
            lax.psum_scatter(
                inner_rows(grad_logits, query_low).astype(jnp.bfloat16),
                "rows",
                scatter_dimension=0,
                tiled=True,
            ).astype(jnp.float32)
        )
        grad_embedded, grad_layer, gain_pair = layer_backward(
            grad_output, saved_state, lengths_here, matrices, HEADS
        )
        for which_one in range(4):
            running[which_one] = running[which_one] + grad_layer[which_one]
        grad_positions = grad_positions + jnp.sum(
            grad_embedded.reshape(histories, length, width), axis=0
        )
        grad_gains = grad_gains + jnp.stack([gain_pair[0], gain_pair[1], gain_three])
        embed_grads.append(scaling * grad_embedded)
    target_part = jnp.stack(target_grads)
    row_grads = jnp.concatenate([jnp.stack(embed_grads), target_part]).reshape(requests, width)
    outgoing = (
        jnp.zeros((devices * capacity, width), jnp.float32).at[slot_of].set(row_grads, mode="drop")
    )
    incoming = send_grads(outgoing.reshape(devices, capacity, width))
    table_grad = (
        jnp.zeros((rows_here, width), jnp.float32)
        .at[received.reshape(-1)]
        .add(incoming.reshape(-1, width))
    )
    summed = lax.psum(
        (
            running[0],
            running[1],
            running[2],
            running[3],
            grad_positions,
            grad_gains,
            loss_local,
            jnp.sum(valid_pos.astype(jnp.float32)),
        ),
        ("dp", "rows"),
    )
    table_square = lax.psum(jnp.sum(table_grad * table_grad), ("dp", "rows"))
    gradients = (table_grad, summed[0], summed[1], summed[2], summed[3], summed[4], summed[5])
    square_total = table_square
    for which_one in range(1, 7):
        square_total = square_total + jnp.sum(gradients[which_one] * gradients[which_one])
    grad_norm = jnp.sqrt(square_total)
    factor = CLIP / jnp.maximum(grad_norm, CLIP)
    weights = (item_table, qkv_weight, out_weight, up_weight, down_weight, positions, gains)
    firsts = (
        item_table_first,
        qkv_weight_first,
        out_weight_first,
        up_weight_first,
        down_weight_first,
        positions_first,
        gains_first,
    )
    seconds = (
        item_table_second,
        qkv_weight_second,
        out_weight_second,
        up_weight_second,
        down_weight_second,
        positions_second,
        gains_second,
    )
    rates = (RATE, RATE, RATE, RATE, RATE, RATE, GAIN_RATE)
    decays = (DECAY, DECAY, DECAY, DECAY, DECAY, DECAY, 0.0)
    updated = [
        adam_step(
            weights[which_one],
            factor * gradients[which_one],
            firsts[which_one],
            seconds[which_one],
            rates[which_one],
            decays[which_one],
        )
        for which_one in range(7)
    ]
    return (
        updated[0][0],
        updated[1][0],
        updated[2][0],
        updated[3][0],
        updated[4][0],
        updated[5][0],
        updated[6][0],
        updated[0][1],
        updated[1][1],
        updated[2][1],
        updated[3][1],
        updated[4][1],
        updated[5][1],
        updated[6][1],
        updated[0][2],
        updated[1][2],
        updated[2][2],
        updated[3][2],
        updated[4][2],
        updated[5][2],
        updated[6][2],
        summed[6],
        summed[7],
        grad_norm,
    )


def solution(mesh):
    placed = (
        P(None, ("dp", "rows"), None),
        P(None, ("dp", "rows"), None),
        P(None, ("dp", "rows")),
        P(None, ("dp", "rows"), None),
        P(),
        P(("dp", "rows"), None),
        P(),
        P(),
        P(),
        P(),
        P(),
        P(),
        P(("dp", "rows"), None),
        P(),
        P(),
        P(),
        P(),
        P(),
        P(),
        P(("dp", "rows"), None),
        P(),
        P(),
        P(),
        P(),
        P(),
        P(),
    )
    return jax.shard_map(
        local,
        mesh=mesh,
        in_specs=placed,
        out_specs=(
            P(("dp", "rows"), None),
            P(),
            P(),
            P(),
            P(),
            P(),
            P(),
            P(("dp", "rows"), None),
            P(),
            P(),
            P(),
            P(),
            P(),
            P(),
            P(("dp", "rows"), None),
            P(),
            P(),
            P(),
            P(),
            P(),
            P(),
            P(),
            P(),
            P(),
        ),
        check_vma=False,
    )
```

profile of v0, /device:TPU:0, one launch (start us, length us, event | category | flops | bytes accessed | tf_op | source)
XLA Modules:
  0.0 669.8 jit_solution(18231010994488937483)
XLA Ops:
  8.8 11.8 %gather_fusion = s32[2048]{0:T(1024)S(1)} fusion(s32[200704]{0:T(1024)S(1)} %copy-done, s32[2048]{0:T(1024)S(1)} %broadcast_clamp_fusion.1), kind=kCustom, calls=%fused_computation | custom fusion | bytes 24576 | tf_op jit(solution)/shard_map/gather | solution.py:274
  20.7 9.1 %reduce-window.6 = s32[32,16,128]{2,1,0:T(8,128)S(1)} reduce-window(s32[32,16,128]{2,1,0:T(8,128)S(1)} %fusion.65, s32[]{:T(128)} %constant.64.clone.1), window={size=1x1x128 pad=0_0x0_0x127_0}, to_apply=%region_0.1 | reduce-window | flops 8323072 | bytes 524292 | tf_op jit(solution)/shard_map/reduce-window
  30.7 8.1 %scatter_custom_fusion = s32[3136]{0:T(1024)S(1)} fusion(s32[2048]{0:T(1024)S(1)} %bitcast.291, s32[2048]{0:T(1024)S(1)} %get-tuple-element.149, s32[]{:T(128)} %constant.64.clone.1), kind=kCustom, calls=%fused_computation.223 | custom fusion | bytes 12548 | tf_op jit(solution)/shard_map/scatter | solution.py:284
  39.5 7.3 %all-to-all-start = ((s32[32,1,98]{2,1,0:T(1,128)}), s32[32,1,98]{2,1,0:T(1,128)S(1)}, u32[]{:S(2)}, u32[]{:S(2)}) async-start(s32[32,1,98]{2,1,0:T(1,128)} %all_to_all.14), calls=%async_computation | async-start | bytes 32768 | tf_op jit(solution)/shard_map/all_to_all | solution.py:211
  46.8 4.8 convert_element_type.193
  54.0 9.8 %gather_fusion.1 = bf16[3136,256]{1,0:T(8,128)(2,1)S(1)} fusion(bf16[6272,256]{1,0:T(8,128)(2,1)} %convert_element_type.193, s32[4096]{0:T(1024)S(1)} %pad_clamp_fusion), kind=kCustom, calls=%fused_computation.1 | custom fusion | bytes 3223808 | tf_op jit(solution)/shard_map/gather | solution.py:287
  65.2 3.7 all-to-all-start.1
  70.3 14.6 %all-gather.2 = bf16[8,1,512]{2,1,0:T(2,128)(2,1)S(1)} all-gather(bf16[1,1,512]{2,1,0:T(2,128)(2,1)S(1)} %reshape.928), channel_id=1, replica_groups=mesh['dp'=4,'rows'=8] {'rows'}, dimensions={0}, use_global_device_ids=true | all-gather | bytes 9216 | tf_op jit(solution)/shard_map/all_gather | solution.py:324
  84.9 9.6 %all-gather.3 = bf16[8,1,512]{2,1,0:T(2,128)(2,1)S(1)} all-gather(bf16[1,1,512]{2,1,0:T(2,128)(2,1)S(1)} %reshape.930), channel_id=1, replica_groups=mesh['dp'=4,'rows'=8] {'rows'}, dimensions={0}, use_global_device_ids=true | all-gather | bytes 9216 | tf_op jit(solution)/shard_map/all_gather | solution.py:324
  103.3 6.0 all-to-all-done.1
  111.7 9.1 %gather_fusion.2 = bf16[2048,256]{1,0:T(8,128)(2,1)} fusion(bf16[3136,256]{1,0:T(8,128)(2,1)S(1)} %reshape.855, s32[2048]{0:T(1024)S(1)} %broadcast_clamp_fusion), kind=kCustom, calls=%fused_computation.2 | custom fusion | bytes 2105344 | tf_op jit(solution)/shard_map/gather | solution.py:290
  140.4 3.5 convolution_convert_fusion.7
  153.7 3.4 convolution_convert_fusion.5
  159.5 6.6 add_reduce_fusion.1
  166.0 15.9 %all-gather.9.cloned.1.call-done = bf16[1,1,4096,256]{3,2,1,0:T(8,128)(2,1)} async-done(((bf16[1,1,512,256]{3,2,1,0:T(8,128)(2,1)}), bf16[1,1,4096,256]{3,2,1,0:T(8,128)(2,1)}) %all-gather.9.cloned.1.call-update) | async-done | bytes 2097168 | tf_op jit(solution)/shard_map/all_gather | solution.py:323
  181.9 3.1 add_reduce_fusion
  186.0 6.0 select_reduce_fusion
  192.6 7.5 %fusion.1 = (bf16[512,4096]{1,0:T(8,128)(2,1)S(1)}, bf16[512,4096]{1,0:T(8,128)(2,1)}) fusion(f32[512,4096]{1,0:T(8,128)S(1)} %copy-done.4, f32[512]{0:T(512)S(1)} %copy-done.85, s32[512]{0:T(512)S(1)} %copy-done.75, f32[512]{0:T(512)S(1)} %get-tuple-element.194, f32[4096]{0:T(1024)S(1)} %bitcast.256, f32[512]{0:T(512)S(1)} %copy-done.84, ...), kind=kLoop, calls=%fused_computation.10 | loop fusion | flops 25165824 | bytes 25208832 | tf_op jit(solution)/shard_map/while/body/eval_jaxpr/convert_element_type | solution.py:24
  204.8 4.2 fusion.29
  231.3 6.0 multiply_reduce_fusion.1
  247.2 6.4 fusion.45
  257.9 5.7 fusion.44
  272.9 43.5 %reduce-scatter.5.cloned.1.call-done = bf16[512,256]{1,0:T(8,128)(2,1)} async-done(((bf16[4096,256]{1,0:T(8,128)(2,1)}), bf16[512,256]{1,0:T(8,128)(2,1)}) %reduce-scatter.5.cloned.1.call-update) | async-done | bytes 262160 | tf_op jit(solution)/shard_map/reduce_scatter | solution.py:332
  320.2 11.5 %scatter_custom_fusion.1 = f32[3136,256]{1,0:T(8,128)} fusion(s32[2048]{0:T(1024)} %bitcast.292, f32[2048,256]{1,0:T(8,128)} %bitcast.248, f32[]{:T(128)} %constant.63.clone.1), kind=kCustom, calls=%fused_computation.75 | custom fusion | bytes 3211776 | tf_op jit(solution)/shard_map/scatter | solution.py:352
  331.7 4.2 reshape.867
  335.9 4.7 all-to-all-start.2
  357.5 187.0 %all-reduce.4.cloned.1.call-done = (f32[256,1536]{1,0:T(8,128)}, f32[512,256]{1,0:T(8,128)}, f32[256,1024]{1,0:T(8,128)}, f32[1024,256]{1,0:T(8,128)}, f32[512,256]{1,0:T(8,128)}) async-done(((f32[256,1536]{1,0:T(8,128)}, f32[512,256]{1,0:T(8,128)}, f32[256,1024]{1,0:T(8,128)}, f32[1024,256]{1,0:T(8,128)}, f32[512,256]{1,0:T(8,128)}), (f32[256,1536]{1,0:T(8,128)}, f32[512,256]{1,0:T(8,128)}, ...) | async-done | bytes 4718608 | tf_op jit(solution)/shard_map/psum | solution.py:360
  551.5 4.3 reshape.921
  555.8 27.8 %scatter_custom_fusion.2 = f32[6272,256]{1,0:T(8,128)} fusion(s32[3136]{0:T(1024)S(1)} %fusion.76, f32[3136,256]{1,0:T(8,128)} %reshape.921, f32[]{:T(128)} %constant.63.clone.1), kind=kCustom, calls=%fused_computation.40 | custom fusion | flops 802816 | bytes 6423040 | tf_op jit(solution)/shard_map/scatter-add | solution.py:358
  583.7 5.2 multiply_reduce_fusion.2
  589.6 38.1 %all-reduce = (f32[]{:T(128)}, f32[3,256]{1,0:T(4,128)S(1)}, f32[]{:T(128)}, f32[]{:T(128)}) all-reduce(f32[]{:T(128)} %multiply_reduce_fusion.2, f32[3,256]{1,0:T(4,128)S(1)} %maximum_add_fusion, f32[]{:T(128)S(6)} %add.535, f32[]{:T(128)} %fusion.83), channel_id=1, replica_groups=mesh['dp'=4,'rows'=8] {'dp','rows'}, use_global_device_ids=true, to_apply=%region_31.32 | all-reduce | flops 771 | bytes 6168 | tf_op jit(solution)/shard_map/psum | solution.py:373
  648.3 13.5 %multiply_subtract_fusion = (f32[6272,256]{1,0:T(8,128)}, f32[6272,256]{1,0:T(8,128)}, f32[6272,256]{1,0:T(8,128)}) fusion(f32[6272,256]{1,0:T(8,128)} %param.31, f32[6272,256]{1,0:T(8,128)S(1)} %bitcast.228, f32[]{:T(128)S(6)} %div.216, f32[6272,256]{1,0:T(8,128)} %param.38, f32[6272,256]{1,0:T(8,128)} %param.45), kind=kLoop, calls=%fused_computation.31 | loop fusion | flops 25690112 | bytes 44957700 | tf_op jit(solution)/shard_map/sub | solution.py:233
  (369 shorter events, 145.3 us)
Async XLA Ops:
  30.7 20.9 %copy-start.94 = (s32[2048,1]{0,1:T(1,128)}, s32[2048,1]{0,1:T(1,128)S(1)}, u32[]{:S(2)}) copy-start(s32[2048,1]{0,1:T(1,128)S(1)} %compare_select_fusion.2) | copy-start | bytes 24580
  39.5 14.4 %all-to-all-start = ((s32[32,1,98]{2,1,0:T(1,128)}), s32[32,1,98]{2,1,0:T(1,128)S(1)}, u32[]{:S(2)}, u32[]{:S(2)}) async-start(s32[32,1,98]{2,1,0:T(1,128)} %all_to_all.14), calls=%async_computation | async-start | bytes 32768 | tf_op jit(solution)/shard_map/all_to_all | solution.py:211
  65.2 29.4 %copy-start.57 = (f32[512,256]{1,0:T(8,128)S(1)}, f32[512,256]{1,0:T(8,128)}, u32[]{:S(2)}) copy-start(f32[512,256]{1,0:T(8,128)} %param.33) | copy-start | bytes 1572868
  65.2 44.1 %all-to-all-start.1 = ((bf16[32,98,256]{2,1,0:T(8,128)(2,1)}), bf16[32,98,256]{2,1,0:T(8,128)(2,1)}, u32[]{:S(2)}, u32[]{:S(2)}) async-start(bf16[32,98,256]{2,1,0:T(8,128)(2,1)} %reshape.886), calls=%async_computation.1 | async-start | bytes 3407872 | tf_op jit(solution)/shard_map/all_to_all | solution.py:216
  68.9 29.8 %copy-start.21 = (f32[256,1536]{1,0:T(8,128)S(1)}, f32[256,1536]{1,0:T(8,128)}, u32[]{:S(2)}) copy-start(f32[256,1536]{1,0:T(8,128)} %param.32) | copy-start | bytes 4718596
  68.9 90.5 %all-gather.7.cloned.1.call-start = ((), (), s32[]{:S(2)}) async-start(), calls=%async_computation.7 | async-start | bytes 2359296 | tf_op jit(solution)/shard_map/all_gather | solution.py:323
  124.1 57.8 %all-gather.9.cloned.1.call-start = ((), (), s32[]{:S(2)}) async-start(), calls=%async_computation.8 | async-start | bytes 2359296 | tf_op jit(solution)/shard_map/all_gather | solution.py:323
  145.1 126.0 %reduce-scatter.3.cloned.1.call-start = ((), (), s32[]{:S(2)}) async-start(), calls=%async_computation.5 | async-start | bytes 2359296 | tf_op jit(solution)/shard_map/reduce_scatter | solution.py:332
  157.6 61.0 %copy-start.6 = (f32[512,256]{1,0:T(8,128)}, f32[512,256]{1,0:T(8,128)S(1)}, u32[]{:S(2)}) copy-start(f32[512,256]{1,0:T(8,128)S(1)} %get-tuple-element.179) | copy-start | bytes 1572868
  159.4 6.6 copy-start.92
  159.4 52.2 %copy-start.50 = (f32[512,256]{1,0:T(8,128)}, f32[512,256]{1,0:T(8,128)S(1)}, u32[]{:S(2)}) copy-start(f32[512,256]{1,0:T(8,128)S(1)} %get-tuple-element.181) | copy-start | bytes 1572868
  186.0 6.0 copy-start.89
  186.0 6.7 copy-start.84
  186.0 6.7 copy-start.85
  192.6 9.5 %copy-start.52 = (f32[512,256]{1,0:T(8,128)S(1)}, f32[512,256]{1,0:T(8,128)}, u32[]{:S(2)}) copy-start(f32[512,256]{1,0:T(8,128)} %get-tuple-element.175) | copy-start | bytes 1572868
  212.0 6.5 copy-start.46
  212.0 6.5 copy-start.48
  213.6 6.5 slice-start.2
  229.7 86.7 %reduce-scatter.5.cloned.1.call-start = ((), (), s32[]{:S(2)}) async-start(), calls=%async_computation.6 | async-start | bytes 2359296 | tf_op jit(solution)/shard_map/reduce_scatter | solution.py:332
  231.3 6.1 copy-start.37
  231.3 6.1 slice-start
  231.3 6.4 slice-start.1
  335.9 215.6 %all-to-all-start.2 = ((f32[32,98,256]{2,1,0:T(8,128)}), f32[32,98,256]{2,1,0:T(8,128)}, u32[]{:S(2)}, u32[]{:S(2)}) async-start(f32[32,98,256]{2,1,0:T(8,128)} %reshape.867), calls=%async_computation.4 | async-start | bytes 6815744 | tf_op jit(solution)/shard_map/all_to_all | solution.py:221
  340.6 203.8 %all-reduce.4.cloned.1.call-start = ((), (), s32[]{:S(2)}) async-start(), calls=%async_computation.9 | async-start | bytes 9437184 | tf_op jit(solution)/shard_map/psum | solution.py:360
  544.4 6.1 copy-start.23
  583.6 49.3 %copy-start.83 = (f32[3,256]{1,0:T(4,128)S(1)}, f32[3,256]{1,0:T(4,128)}, u32[]{:S(2)}) copy-start(f32[3,256]{1,0:T(4,128)} %param.37) | copy-start | bytes 9220
  583.6 49.3 %copy-start.95 = (f32[3,256]{1,0:T(4,128)S(1)}, f32[3,256]{1,0:T(4,128)}, u32[]{:S(2)}) copy-start(f32[3,256]{1,0:T(4,128)} %param.44) | copy-start | bytes 9220
  583.6 49.3 %copy-start.96 = (f32[3,256]{1,0:T(4,128)S(1)}, f32[3,256]{1,0:T(4,128)}, u32[]{:S(2)}) copy-start(f32[3,256]{1,0:T(4,128)} %param.51) | copy-start | bytes 9220
  583.6 49.9 %copy-start.60 = (f32[512,256]{1,0:T(8,128)S(1)}, f32[512,256]{1,0:T(8,128)}, u32[]{:S(2)}) copy-start(f32[512,256]{1,0:T(8,128)} %get-tuple-element.108) | copy-start | bytes 1572868
  588.8 47.6 %copy-start.58 = (f32[512,256]{1,0:T(8,128)S(1)}, f32[512,256]{1,0:T(8,128)}, u32[]{:S(2)}) copy-start(f32[512,256]{1,0:T(8,128)} %param.33) | copy-start | bytes 1572868
  642.1 6.2 slice-start.4
  648.3 13.5 %copy-start.1 = (s32[200704]{0:T(1024)S(1)}, s32[200704]{0:T(1024)}, u32[]{:S(2)}) copy-start(s32[200704]{0:T(1024)} %param.30) | copy-start | bytes 2408452
  (84 other events, 233.7 us)
Sparse Core Ops, SparseCore 0:
  124.2 27.2 all-gather.6
  154.0 27.8 all-gather.8
  229.8 41.2 reduce-scatter.2
  275.2 41.2 reduce-scatter.4
  353.6 190.7 all-reduce.3
where the time goes:
time: 677 us; the launch traced here: 670 us
  waiting for transfers between devices  256 us (38%)
  other arithmetic  130 us (19%)
  matrix products  91.7 us (14%)
  local copies, waits for them, and re-layouts  90.1 us (13%)
  blocking collectives  62.3 us (9%)
  between operations  22.5 us (3%)
  starting transfers between devices  16.6 us (2%)
    psum x1, waiting for transfers between devices, local(): lax.psum((running[0], running[1], running[2], running[3], grad_positions,...  187 us
    reduce_scatter x2, waiting for transfers between devices, local(): lax.psum_scatter(inner_rows(grad_logits, query_low).astype(jnp.bfloat16),...  45.2 us
    psum x1, blocking collectives, local(): table_square = lax.psum(jnp.sum(table_grad * table_grad), ('dp', 'rows'))  38.1 us
    scatter-add x1, other arithmetic, local(): table_grad = jnp.zeros((rows_here, width), jnp.float32).at[received.resha...  27.8 us
    sub x7, other arithmetic, adam_step(): return (weight - rate * (stepped + decay * weight), first_new, second_new)  26 us
    all_gather x2, blocking collectives, local(): lax.all_gather(bias_low, 'rows', axis=0, tiled=True)  24.2 us
    convert_element_type x9, other arithmetic, rounded(): return values.astype(jnp.bfloat16)  22.7 us
    unnamed x219, local copies, waits for them, and re-layouts  19.1 us
  transfers between devices with their start and end apart: 8, of which 6 were waited for; matrix products, arithmetic and copies ran while one was open for 16% of the time, Pallas kernels for 0%

commit v1 on v0

--- a/solution.py
+++ b/solution.py
@@ -1,10 +1,15 @@
+import functools
 import math
 
 import jax
 import jax.numpy as jnp
 from jax import lax
+from jax.experimental import pallas as pl
+from jax.experimental.pallas import tpu as pltpu
 from jax.sharding import PartitionSpec as P
 
+MESH = pl.DeviceIdType.MESH
+VMEM = pl.BlockSpec(memory_space=pltpu.VMEM)
 HEADS = 8
 STEP = 10
 
@@ -231,6 +236,263 @@
         / (jnp.sqrt(second_new / (1.0 - BETA_TWO**STEP)) + ADAM_EPS)
     )
     return (weight - rate * (stepped + decay * weight), first_new, second_new)
+
+
+def reduce_rows(total_rows, devices):
+    unit = 16 * devices
+    return -(-total_rows // unit) * unit
+
+
+def tail_kernel(dp_count, row_count, padded, capacity, qkv, out, up, down, pos, outgoing, incoming, gathered, square,
+                acc, low, recv0, recv1, recv2, send_a, recv_a, send_r, recv_r):
+    devices = dp_count * row_count
+    dp = lax.axis_index("dp")
+    row = lax.axis_index("rows")
+    me = dp * row_count + row
+    bits = row_count.bit_length() - 1
+    barrier = pltpu.get_barrier_semaphore()
+
+    def place(k):
+        other = lax.rem(me + k, devices)
+        return other, (other // row_count, lax.rem(other, row_count))
+
+    def greet(k, carry):
+        other, where = place(k)
+        pl.semaphore_signal(barrier, inc=1, device_id=where, device_id_type=MESH)
+        return carry
+
+    lax.fori_loop(1, devices, greet, 0)
+    width = 256
+    at = 0
+    for ref in (qkv, up):
+        for c in range(ref.shape[1] // width):
+            acc[pl.ds(at, ref.shape[0]), :] = ref[:, pl.ds(c * width, width)]
+            at += ref.shape[0]
+    for ref in (out, down, pos):
+        acc[pl.ds(at, ref.shape[0]), :] = ref[...]
+        at += ref.shape[0]
+    if at < padded:
+        acc[pl.ds(at, padded - at), :] = jnp.zeros((padded - at, width), jnp.float32)
+    pl.semaphore_wait(barrier, devices - 1)
+
+    def a2a_send(k):
+        other, where = place(k)
+        return pltpu.make_async_remote_copy(
+            outgoing.at[other], incoming.at[me], send_a.at[k], recv_a.at[me], device_id=where, device_id_type=MESH)
+
+    def a2a_recv(k):
+        other, where = place(k)
+        return pltpu.make_async_remote_copy(
+            outgoing.at[other], incoming.at[other], send_a.at[k], recv_a.at[other], device_id=where, device_id_type=MESH)
+
+    def partner(bit):
+        step = 1 << bit
+        mine = lax.rem(row // step, 2)
+        return mine, (dp, row + step - 2 * step * mine)
+
+    half = padded // 2
+    units = padded // (16 * devices)
+    part_rows = [((units + 1) // 2) * 16 * (devices // 2), (units // 2) * 16 * (devices // 2)]
+    orders = [list(range(1, bits)), list(range(bits - 1, 0, -1))]
+    al = lambda v: pl.multiple_of(v, 16)
+
+    mine, where = partner(0)
+    low[pl.ds(al((1 - mine) * half), half), :] = acc[pl.ds(al((1 - mine) * half), half), :].astype(jnp.bfloat16)
+    first = pltpu.make_async_remote_copy(low.at[pl.ds(al((1 - mine) * half), half)], recv0, send_r.at[0], recv_r.at[0],
+                                         device_id=where, device_id_type=MESH)
+    first.start()
+    lax.fori_loop(1, devices, lambda k, c: (a2a_send(k).start(), c)[1], 0)
+    incoming[me] = outgoing[me]
+    first.wait_recv()
+    base = mine * half
+    pending = [first]
+    starts = [base, base + part_rows[0]]
+    sizes = list(part_rows)
+    offs = [0, sizes[0]]
+    live = [p for p in range(2) if part_rows[p] > 0]
+    acc[pl.ds(al(base), half), :] = acc[pl.ds(al(base), half), :] + recv0[...].astype(jnp.float32)
+    sem = 1
+    scratch_at = 0
+    history = []
+    for step in range(bits - 1):
+        copies = []
+        for p in live:
+            bit = orders[p][step]
+            mine, where = partner(bit)
+            size = sizes[p] // 2
+            keep = starts[p] + mine * size
+            give = starts[p] + (1 - mine) * size
+            low[pl.ds(al(give), size), :] = acc[pl.ds(al(give), size), :].astype(jnp.bfloat16)
+            landing = recv1.at[pl.ds(scratch_at, size)]
+            copy = pltpu.make_async_remote_copy(low.at[pl.ds(al(give), size)], landing, send_r.at[sem], recv_r.at[sem],
+                                                device_id=where, device_id_type=MESH)
+            copy.start()
+            copies.append((p, copy, keep, size, scratch_at, where))
+            sem += 1
+            scratch_at += size
+        for p, copy, keep, size, off, where in copies:
+            copy.wait_recv()
+            acc[pl.ds(al(keep), size), :] = acc[pl.ds(al(keep), size), :] + recv1[pl.ds(off, size), :].astype(jnp.float32)
+            history.append((p, keep, size, where))
+            starts[p], sizes[p] = keep, size
+            pending.append(copy)
+    copies = []
+    off = 0
+    final = {}
+    for p in live:
+        size = sizes[p] // dp_count
+        for k in range(1, dp_count):
+            other = lax.rem(dp + k, dp_count)
+            give = starts[p] + other * size
+            low[pl.ds(al(give), size), :] = acc[pl.ds(al(give), size), :].astype(jnp.bfloat16)
+            copy = pltpu.make_async_remote_copy(low.at[pl.ds(al(give), size)], recv2.at[pl.ds(off, size)], send_r.at[sem], recv_r.at[sem],
+                                                device_id=(other, row), device_id_type=MESH)
+            copy.start()
+            copies.append((p, copy, off, size))
+            sem += 1
+            off += size
+        final[p] = (starts[p] + dp * size, size)
+    for p, copy, off, size in copies:
+        copy.wait_recv()
+        at, size = final[p]
+        acc[pl.ds(al(at), size), :] = acc[pl.ds(al(at), size), :] + recv2[pl.ds(off, size), :].astype(jnp.float32)
+        pending.append(copy)
+    total = jnp.zeros((1, width), jnp.float32)
+    for p in live:
+        at, size = final[p]
+        mine_low = acc[pl.ds(al(at), size), :]
+        total = total + jnp.sum(mine_low * mine_low, axis=0, keepdims=True)
+        gathered[pl.ds(al(at), size), :] = mine_low.astype(jnp.bfloat16)
+    square[...] = jnp.broadcast_to(total, square.shape)
+
+    copies = []
+    for p in live:
+        at, size = final[p]
+        for k in range(1, dp_count):
+            other = lax.rem(dp + k, dp_count)
+            copy = pltpu.make_async_remote_copy(gathered.at[pl.ds(al(at), size)], gathered.at[pl.ds(al(at), size)], send_r.at[sem], recv_r.at[sem],
+                                                device_id=(other, row), device_id_type=MESH)
+            copy.start()
+            copies.append((p, copy, k, sem))
+            sem += 1
+    for p, copy, k, s in copies:
+        at, size = final[p]
+        source = lax.rem(dp + dp_count - k, dp_count)
+        land = starts[p] + source * size
+        pltpu.make_async_remote_copy(gathered.at[pl.ds(al(at), size)], gathered.at[pl.ds(al(land), size)], send_r.at[s], recv_r.at[s],
+                                     device_id=(source, row), device_id_type=MESH).wait_recv()
+        pending.append(copy)
+    for step in range(bits - 2, -1, -1):
+        copies = []
+        for p in live:
+            bit = orders[p][step]
+            mine, where = partner(bit)
+            size = sizes[p]
+            at = starts[p]
+            copy = pltpu.make_async_remote_copy(gathered.at[pl.ds(al(at), size)], gathered.at[pl.ds(al(at), size)], send_r.at[sem], recv_r.at[sem],
+                                                device_id=where, device_id_type=MESH)
+            copy.start()
+            copies.append((p, copy, sem, mine, size, where))
+            sem += 1
+        for p, copy, s, mine, size, where in copies:
+            bottom = starts[p] - mine * size
+            land = bottom + (1 - mine) * size
+            pltpu.make_async_remote_copy(gathered.at[pl.ds(al(land), size)], gathered.at[pl.ds(al(land), size)], send_r.at[s], recv_r.at[s],
+                                         device_id=where, device_id_type=MESH).wait_recv()
+            starts[p], sizes[p] = bottom, 2 * size
+            pending.append(copy)
+    mine, where = partner(0)
+    last = pltpu.make_async_remote_copy(gathered.at[pl.ds(al(mine * half), half)], gathered.at[pl.ds(al(mine * half), half)], send_r.at[sem], recv_r.at[sem],
+                                        device_id=where, device_id_type=MESH)
+    last.start()
+    pltpu.make_async_remote_copy(gathered.at[pl.ds(al((1 - mine) * half), half)], gathered.at[pl.ds(al((1 - mine) * half), half)], send_r.at[sem], recv_r.at[sem],
+                                 device_id=where, device_id_type=MESH).wait_recv()
+    sem += 1
+    pending.append(last)
+    lax.fori_loop(1, devices, lambda k, c: (a2a_recv(k).wait_recv(), c)[1], 0)
+    for copy in pending:
+        copy.wait_send()
+    lax.fori_loop(1, devices, lambda k, c: (a2a_send(k).wait_send(), c)[1], 0)
+
+
+def tail_exchange(dp_count, row_count, qkv, out, up, down, pos, outgoing):
+    devices = dp_count * row_count
+    capacity = outgoing.shape[1]
+    width = out.shape[1]
+    rows = sum(a.size for a in (qkv, out, up, down, pos)) // width
+    padded = reduce_rows(rows, devices)
+    bits = row_count.bit_length() - 1
+    sems = 2 + 4 * bits + 4 * dp_count + 8
+    return pl.pallas_call(
+        functools.partial(tail_kernel, dp_count, row_count, padded, capacity),
+        out_shape=(jax.ShapeDtypeStruct(outgoing.shape, jnp.bfloat16), jax.ShapeDtypeStruct((padded, width), jnp.bfloat16),
+                   jax.ShapeDtypeStruct((8, width), jnp.float32)),
+        in_specs=[VMEM] * 6, out_specs=(VMEM,) * 3,
+        scratch_shapes=[
+            pltpu.VMEM((padded, width), jnp.float32),
+            pltpu.VMEM((padded, width), jnp.bfloat16),
+            pltpu.VMEM((padded // 2, width), jnp.bfloat16),
+            pltpu.VMEM((padded // 2, width), jnp.bfloat16),
+            pltpu.VMEM((padded // row_count, width), jnp.bfloat16),
+            pltpu.SemaphoreType.DMA((devices,)), pltpu.SemaphoreType.DMA((devices,)),
+            pltpu.SemaphoreType.DMA((sems,)), pltpu.SemaphoreType.DMA((sems,)),
+        ],
+        name="tail_exchange",
+        compiler_params=pltpu.CompilerParams(collective_id=3, has_side_effects=True, vmem_limit_bytes=56 * 2**20),
+    )(qkv, out, up, down, pos, outgoing)
+
+
+def small_kernel(dp_count, row_count, part, summed, by_row, by_dp, send_sem, recv_sem):
+    dp = lax.axis_index("dp")
+    row = lax.axis_index("rows")
+    barrier = pltpu.get_barrier_semaphore()
+    row_places = [lax.rem(row + k, row_count) for k in range(1, row_count)]
+    dp_places = [lax.rem(dp + k, dp_count) for k in range(1, dp_count)]
+    for other in row_places:
+        pl.semaphore_signal(barrier, inc=1, device_id=(dp, other), device_id_type=MESH)
+    for other in dp_places:
+        pl.semaphore_signal(barrier, inc=1, device_id=(other, row), device_id_type=MESH)
+    pl.semaphore_wait(barrier, row_count + dp_count - 2)
+
+    def spread(source, landing, mine, others, where, base):
+        sends = []
+        for k, other in enumerate(others):
+            copy = pltpu.make_async_remote_copy(
+                source, landing.at[mine], send_sem.at[base + k], recv_sem.at[base + mine],
+                device_id=where(other), device_id_type=MESH,
+            )
+            copy.start()
+            sends.append(copy)
+        landing[mine] = source[...]
+        for other in others:
+            pltpu.make_async_remote_copy(
+                source, landing.at[other], send_sem.at[base], recv_sem.at[base + other],
+                device_id=where(other), device_id_type=MESH,
+            ).wait_recv()
+        for copy in sends:
+            copy.wait_send()
+
+    spread(part, by_row, row, row_places, lambda other: (dp, other), 0)
+    summed[...] = jnp.sum(by_row[...], axis=0)
+    spread(summed, by_dp, dp, dp_places, lambda other: (other, row), row_count)
+    summed[...] = jnp.sum(by_dp[...], axis=0)
+
+
+def small_sum(dp_count, row_count, part):
+    return pl.pallas_call(
+        functools.partial(small_kernel, dp_count, row_count),
+        out_shape=jax.ShapeDtypeStruct(part.shape, part.dtype),
+        in_specs=[VMEM],
+        out_specs=VMEM,
+        scratch_shapes=[
+            pltpu.VMEM((row_count,) + part.shape, part.dtype),
+            pltpu.VMEM((dp_count,) + part.shape, part.dtype),
+            pltpu.SemaphoreType.DMA((row_count + dp_count,)),
+            pltpu.SemaphoreType.DMA((row_count + dp_count,)),
+        ],
+        name="small_sum",
+        compiler_params=pltpu.CompilerParams(collective_id=4, has_side_effects=True),
+    )(part)
 
 
 def local(
@@ -267,6 +529,8 @@
     tokens = histories * length
     requests = 2 * micro * tokens
     capacity = 3 * (requests + devices) // (2 * devices) + 1
+    capacity = -(-capacity // 16) * 16
+    dp_count, row_count = lax.axis_size("dp"), lax.axis_size("rows")
     position = jnp.arange(length, dtype=jnp.int32)
     valid_pos = (position[None, None, :] < lengths[:, :, None]).reshape(micro, tokens)
     wanted = jnp.stack([item_ids, targets]).reshape(requests)
@@ -349,33 +613,50 @@
     target_part = jnp.stack(target_grads)
     row_grads = jnp.concatenate([jnp.stack(embed_grads), target_part]).reshape(requests, width)
     outgoing = (
-        jnp.zeros((devices * capacity, width), jnp.float32).at[slot_of].set(row_grads, mode="drop")
-    )
-    incoming = send_grads(outgoing.reshape(devices, capacity, width))
+        jnp.zeros((devices * capacity, width), jnp.bfloat16)
+        .at[slot_of]
+        .set(rounded(row_grads), mode="drop")
+    )
+    incoming, gathered, square = tail_exchange(
+        dp_count,
+        row_count,
+        running[0],
+        running[1],
+        running[2],
+        running[3],
+        grad_positions,
+        outgoing.reshape(devices, capacity, width),
+    )
     table_grad = (
         jnp.zeros((rows_here, width), jnp.float32)
         .at[received.reshape(-1)]
-        .add(incoming.reshape(-1, width))
-    )
-    summed = lax.psum(
-        (
-            running[0],
-            running[1],
-            running[2],
-            running[3],
-            grad_positions,
-            grad_gains,
-            loss_local,
-            jnp.sum(valid_pos.astype(jnp.float32)),
-        ),
-        ("dp", "rows"),
-    )
-    table_square = lax.psum(jnp.sum(table_grad * table_grad), ("dp", "rows"))
-    gradients = (table_grad, summed[0], summed[1], summed[2], summed[3], summed[4], summed[5])
-    square_total = table_square
-    for which_one in range(1, 7):
-        square_total = square_total + jnp.sum(gradients[which_one] * gradients[which_one])
-    grad_norm = jnp.sqrt(square_total)
+        .add(incoming.reshape(-1, width).astype(jnp.float32))
+    )
+    own_square = jnp.sum(table_grad * table_grad) + jnp.sum(square[0])
+    scalars = jnp.stack([loss_local, jnp.sum(valid_pos.astype(jnp.float32)), own_square])
+    part = jnp.concatenate(
+        [grad_gains.reshape(-1), jnp.pad(scalars, (0, 1024 - grad_gains.size - 3))]
+    ).reshape(8, 128)
+    small = small_sum(dp_count, row_count, part).reshape(-1)
+    sum_gains = small[: grad_gains.size].reshape(grad_gains.shape)
+    sum_loss, sum_count, square_total = (small[grad_gains.size + k] for k in range(3))
+    gathered = gathered.astype(jnp.float32)
+    place = 0
+    blocks = []
+    for like in (qkv_weight, up_weight):
+        count = like.shape[1] // width
+        piece = gathered[place : place + count * like.shape[0]]
+        blocks.append(
+            jnp.concatenate(
+                [piece[c * like.shape[0] : (c + 1) * like.shape[0]] for c in range(count)], axis=1
+            )
+        )
+        place += count * like.shape[0]
+    for like in (out_weight, down_weight, positions):
+        blocks.append(gathered[place : place + like.shape[0]])
+        place += like.shape[0]
+    gradients = (table_grad, blocks[0], blocks[2], blocks[1], blocks[3], blocks[4], sum_gains)
+    grad_norm = jnp.sqrt(square_total + jnp.sum(sum_gains * sum_gains))
     factor = CLIP / jnp.maximum(grad_norm, CLIP)
     weights = (item_table, qkv_weight, out_weight, up_weight, down_weight, positions, gains)
     firsts = (
@@ -431,8 +712,8 @@
         updated[4][2],
         updated[5][2],
         updated[6][2],
-        summed[6],
-        summed[7],
+        sum_loss,
+        sum_count,
         grad_norm,
     )
 

time: 677 us -> 516 us (0.76)
  waiting for transfers between devices: 256 us -> 65.9 us
  Pallas kernels: 0 us -> 91.3 us
  blocking collectives: 62.3 us -> 25.7 us
  local copies, waits for them, and re-layouts: 90.1 us -> 78.1 us
    psum x1 -> x0, waiting for transfers between devices: 187 us -> none  [local(): lax.psum((running[0], running[1], running[2], running[3], grad_positions,...]
    pallas_call x0 -> x2, Pallas kernels: none -> 91.3 us  [the longest x1 80.6 us: tail_exchange(): pl.pallas_call(functools.partial(tail_kernel, dp_count, row_count, padded...]
    psum x1 -> x0, blocking collectives: 38.1 us -> none  [local(): table_square = lax.psum(jnp.sum(table_grad * table_grad), ('dp', 'rows'))]
    reshape x3 -> x0, local copies, waits for them, and re-layouts: 10.9 us -> none  [the longest x1 4.3 us: local(): incoming.reshape(-1, width)]
    reduce_sum x7 -> x3, other arithmetic: 13.6 us -> 8.21 us  [the longest x2 6.93 us: local(): own_square = jnp.sum(table_grad * table_grad) + jnp.sum(square[0])]
    unnamed x219 -> x192, local copies, waits for them, and re-layouts: 19.1 us -> 14.8 us
    sub x7 -> x6, other arithmetic: 26 us -> 29.5 us  [adam_step(): return (weight - rate * (stepped + decay * weight), first_new, second_new)]
  transfers between devices with their start and end apart: 8 -> 6, of which waited for: 6 -> 4; matrix products, arithmetic and copies ran while one was open for 16% -> 18% of each run, Pallas kernels for 0% -> 0%
where the time goes in v1:
time: 516 us; the launch traced here: 510 us
  other arithmetic  131 us (25%)
  Pallas kernels  91.3 us (18%)
  matrix products  86.1 us (17%)
  local copies, waits for them, and re-layouts  78.1 us (15%)
  waiting for transfers between devices  65.9 us (13%)
  blocking collectives  25.7 us (5%)
  between operations  20.5 us (4%)
  starting transfers between devices  11.6 us (2%)
    pallas_call x1, Pallas kernels, tail_exchange(): pl.pallas_call(functools.partial(tail_kernel, dp_count, row_count, padded...  80.6 us
    reduce_scatter x2, waiting for transfers between devices, local(): lax.psum_scatter(inner_rows(grad_logits, query_low).astype(jnp.bfloat16),...  40.9 us
    sub x6, other arithmetic, adam_step(): return (weight - rate * (stepped + decay * weight), first_new, second_new)  29.5 us
    scatter-add x1, other arithmetic, local(): table_grad = jnp.zeros((rows_here, width), jnp.float32).at[received.resha...  28.7 us
    all_gather x2, blocking collectives, local(): lax.all_gather(bias_low, 'rows', axis=0, tiled=True)  25.7 us
    convert_element_type x9, other arithmetic, rounded(): return values.astype(jnp.bfloat16)  24.2 us
    dot_general x10, matrix products, inner_cols(): lax.dot_general(first_op, second_op, (((1,), (1,)), ((), ())), preferred_...  18.8 us
    all_gather x2, waiting for transfers between devices, local(): lax.all_gather(fetched[1, micro_index], 'rows', axis=0, tiled=True)  16.8 us
  transfers between devices with their start and end apart: 6, of which 4 were waited for; matrix products, arithmetic and copies ran while one was open for 18% of the time, Pallas kernels for 0%

profile of v1, /device:TPU:0, one launch (start us, length us, event | category | flops | bytes accessed | tf_op | source)
XLA Modules:
  0.0 509.7 jit_solution(4663301289282585202)
XLA Ops:
  8.8 11.8 %gather_fusion = s32[2048]{0:T(1024)S(1)} fusion(s32[200704]{0:T(1024)S(1)} %copy-done, s32[2048]{0:T(1024)S(1)} %broadcast_clamp_fusion.1), kind=kCustom, calls=%fused_computation | custom fusion | bytes 24576 | tf_op jit(solution)/shard_map/gather | solution.py:538
  20.7 9.1 %reduce-window.6 = s32[32,16,128]{2,1,0:T(8,128)S(1)} reduce-window(s32[32,16,128]{2,1,0:T(8,128)S(1)} %fusion.68, s32[]{:T(128)} %constant.64.clone.1), window={size=1x1x128 pad=0_0x0_0x127_0}, to_apply=%region_0.1 | reduce-window | flops 8323072 | bytes 524292 | tf_op jit(solution)/shard_map/reduce-window
  30.7 8.1 %scatter_custom_fusion = s32[3584]{0:T(1024)S(1)} fusion(s32[2048]{0:T(1024)S(1)} %bitcast.306, s32[2048]{0:T(1024)S(1)} %get-tuple-element.154, s32[]{:T(128)} %constant.64.clone.1), kind=kCustom, calls=%fused_computation.229 | custom fusion | bytes 14340 | tf_op jit(solution)/shard_map/scatter | solution.py:548
  39.5 7.3 %all-to-all-start = ((s32[32,1,112]{2,1,0:T(1,128)}), s32[32,1,112]{2,1,0:T(1,128)S(1)}, u32[]{:S(2)}, u32[]{:S(2)}) async-start(s32[32,1,112]{2,1,0:T(1,128)} %all_to_all.11), calls=%async_computation | async-start | bytes 32768 | tf_op jit(solution)/shard_map/all_to_all | solution.py:216
  46.8 4.8 convert_element_type.206
  53.9 11.4 %gather_fusion.1 = bf16[3584,256]{1,0:T(8,128)(2,1)} fusion(bf16[6272,256]{1,0:T(8,128)(2,1)} %convert_element_type.206, s32[4096]{0:T(1024)S(1)} %pad_clamp_fusion), kind=kCustom, calls=%fused_computation.1 | custom fusion | bytes 3684352 | tf_op jit(solution)/shard_map/gather | solution.py:551
  65.4 3.6 all-to-all-start.1
  69.7 16.1 %all-gather.3 = bf16[8,1,512]{2,1,0:T(2,128)(2,1)S(1)} all-gather(bf16[1,1,512]{2,1,0:T(2,128)(2,1)S(1)} %reshape.944), channel_id=1, replica_groups=mesh['dp'=4,'rows'=8] {'rows'}, dimensions={0}, use_global_device_ids=true | all-gather | bytes 9216 | tf_op jit(solution)/shard_map/all_gather | solution.py:588
  85.8 9.6 %all-gather.2 = bf16[8,1,512]{2,1,0:T(2,128)(2,1)S(1)} all-gather(bf16[1,1,512]{2,1,0:T(2,128)(2,1)S(1)} %reshape.942), channel_id=1, replica_groups=mesh['dp'=4,'rows'=8] {'rows'}, dimensions={0}, use_global_device_ids=true | all-gather | bytes 9216 | tf_op jit(solution)/shard_map/all_gather | solution.py:588
  106.3 5.9 %all-to-all-done.1 = bf16[32,112,256]{2,1,0:T(8,128)(2,1)S(1)} async-done(((bf16[32,112,256]{2,1,0:T(8,128)(2,1)}), bf16[32,112,256]{2,1,0:T(8,128)(2,1)S(1)}, u32[]{:S(2)}, u32[]{:S(2)}) %all-to-all-start.1) | async-done | bytes 1835040 | tf_op jit(solution)/shard_map/all_to_all | solution.py:221
  112.2 9.0 %gather_fusion.2 = bf16[2048,256]{1,0:T(8,128)(2,1)} fusion(bf16[3584,256]{1,0:T(8,128)(2,1)S(1)} %bitcast.237, s32[2048]{0:T(1024)S(1)} %broadcast_clamp_fusion), kind=kCustom, calls=%fused_computation.2 | custom fusion | bytes 2105344 | tf_op jit(solution)/shard_map/gather | solution.py:554
  140.8 3.5 convolution_convert_fusion.5
  153.3 3.4 convolution_convert_fusion.7
  159.4 6.3 %add_reduce_fusion = (f32[512]{0:T(512)S(1)}, f32[512,4096]{1,0:T(8,128)}) fusion(f32[4096]{0:T(1024)S(1)} %bitcast.266, bf16[1,1,4096,256]{3,2,1,0:T(8,128)(2,1)} %all-gather.9.cloned.1.call-done, f32[512,256]{1,0:T(8,128)} %get-tuple-element.185, f32[512]{0:T(512)S(1)} %fusion.92, f32[256]{0:T(256)S(1)} %bitcast.290), kind=kOutput, calls=%fused_computation.28 | convolution fusion | flops 1078328832 | bytes 11031552 | tf_op jit(solution)/shard_map/while/body/eval_jaxpr/dot_general | solution.py:43
  165.7 16.8 %all-gather.7.cloned.1.call-done = bf16[1,1,4096,256]{3,2,1,0:T(8,128)(2,1)} async-done(((bf16[1,1,512,256]{3,2,1,0:T(8,128)(2,1)}), bf16[1,1,4096,256]{3,2,1,0:T(8,128)(2,1)}) %all-gather.7.cloned.1.call-update) | async-done | bytes 2097168 | tf_op jit(solution)/shard_map/all_gather | solution.py:587
  182.5 3.3 add_reduce_fusion.1
  186.7 6.0 %select_reduce_fusion = (f32[512]{0:T(512)S(1)}, f32[512]{0:T(512)S(1)}, f32[512]{0:T(512)S(1)}, f32[512]{0:T(512)S(1)}) fusion(f32[512,4096]{1,0:T(8,128)S(1)} %copy-done.4, f32[4096]{0:T(1024)S(1)} %bitcast.267, s32[512]{0:T(512)S(1)} %iota_add_fusion, f32[512]{0:T(512)S(1)} %get-tuple-element.186, f32[512]{0:T(512)S(1)} %get-tuple-element.194, ...), kind=kLoop, calls=%fused_computation.13 | loop fusion | flops 23066624 | bytes 16824320 | tf_op jit(solution)/shard_map/while/body/eval_jaxpr/reduce_sum | solution.py:194
  193.9 7.5 %fusion.3 = (bf16[512,4096]{1,0:T(8,128)(2,1)S(1)}, bf16[512,4096]{1,0:T(8,128)(2,1)}) fusion(f32[512,4096]{1,0:T(8,128)S(1)} %copy-done.4, f32[512]{0:T(512)S(1)} %convert_element_type.250, f32[512]{0:T(512)S(1)} %get-tuple-element.128, f32[4096]{0:T(1024)S(1)} %bitcast.268, s32[512]{0:T(512)S(1)} %iota_add_fusion, f32[512]{0:T(512)S(1)} %convert_element_type.228, ...), kind=kLoop, calls=%fused_computation.12 | loop fusion | flops 25165824 | bytes 25208832 | tf_op jit(solution)/shard_map/while/body/eval_jaxpr/convert_element_type | solution.py:29
  206.1 4.3 fusion.30
  223.7 3.4 multiply_reduce_fusion.1
  235.2 5.5 %multiply_reduce_fusion = (f32[8,512]{1,0:T(8,128)S(1)}, f32[8,512,512]{1,2,0:T(8,128)S(1)}) fusion(f32[8,512,512]{1,2,0:T(8,128)} %copy-done.2, f32[8,512]{1,0:T(8,128)S(1)} %log_add_fusion, pred[512,512]{0,1:T(8,128)(4,1)S(1)} %fusion.47, bf16[512,8,64]{0,2,1:T(8,128)(2,1)S(1)} %bitcast.255, bf16[1,512,3,8,64]{1,4,3,2,0:T(8,128)(2,1)S(1)} %bitcast.242), kind=kOutput, calls=%fused_computation.16 | convolution fusion | flops 278917120 | bytes 18120704 | tf_op jit(solution)/shard_map/sqhe,skhe->shqk/dot_general | solution.py:93
  254.5 6.4 %fusion.44 = bf16[1,512,1,8,64]{1,4,3,2,0:T(8,128)(2,1)} fusion(bf16[512,8,64]{0,2,1:T(8,128)(2,1)S(1)} %bitcast.256, f32[8,512,512]{1,2,0:T(8,128)} %copy-done.2, f32[8,512]{1,0:T(8,128)S(1)} %log_add_fusion, pred[512,512]{0,1:T(8,128)(4,1)S(1)} %fusion.47), kind=kOutput, calls=%fused_computation.105 | convolution fusion | flops 277086208 | bytes 9715712 | tf_op jit(solution)/shard_map/shqk,sqhe->skhe/dot_general | solution.py:96
  279.4 40.9 %reduce-scatter.3.cloned.1.call-done = bf16[512,256]{1,0:T(8,128)(2,1)} async-done(((bf16[4096,256]{1,0:T(8,128)(2,1)}), bf16[512,256]{1,0:T(8,128)(2,1)}) %reduce-scatter.3.cloned.1.call-update) | async-done | bytes 262160 | tf_op jit(solution)/shard_map/reduce_scatter | solution.py:596
  321.4 11.1 %scatter_custom_fusion.1 = bf16[3584,256]{1,0:T(8,128)(2,1)} fusion(s32[2048]{0:T(1024)} %bitcast.307, bf16[2048,256]{1,0:T(8,128)(2,1)S(1)} %bitcast.264, bf16[]{:T(256)} %constant.72.clone.1), kind=kCustom, calls=%fused_computation.122 | custom fusion | bytes 1835520 | tf_op jit(solution)/shard_map/scatter | solution.py:618
  332.5 80.6 %tail_exchange.1 = (bf16[32,112,256]{2,1,0:T(8,128)(2,1)}, bf16[4608,256]{1,0:T(8,128)(2,1)}, f32[8,256]{1,0:T(8,128)}) custom-call(f32[256,1536]{1,0:T(8,128)} %convolution_add_fusion.qkv, f32[512,256]{1,0:T(8,128)} %convolution_add_fusion.5.out, f32[256,1024]{1,0:T(8,128)} %convolution_add_fusion.2.up, f32[1024,256]{1,0:T(8,128)} %convolution_add_fusion.1.down, ...), custom_call_target="tpu_custom_call" | custom-call | tf_op jit(solution)/shard_map/tail_exchange/pallas_call | solution.py:426
  419.3 28.7 %scatter_custom_fusion.2 = f32[6272,256]{1,0:T(8,128)} fusion(s32[3584]{0:T(1024)S(1)} %fusion.79, bf16[3584,256]{1,0:T(8,128)(2,1)} %bitcast.263, f32[]{:T(128)} %constant.74.clone.1), kind=kCustom, calls=%fused_computation.40 | custom fusion | flops 1835008 | bytes 8257540 | tf_op jit(solution)/shard_map/scatter-add | solution.py:633
  448.0 5.2 %multiply_reduce_fusion.2 = f32[]{:T(128)} fusion(f32[6272,256]{1,0:T(8,128)} %scatter_custom_fusion.2), kind=kLoop, calls=%fused_computation.33 | loop fusion | flops 3211263 | bytes 6422532 | tf_op jit(solution)/shard_map/reduce_sum | solution.py:635
  455.8 10.7 %small_sum.1 = f32[8,128]{1,0:T(8,128)} custom-call(f32[8,128]{1,0:T(8,128)} %maximum_bitcast_fusion.part), custom_call_target="tpu_custom_call" | custom-call | tf_op jit(solution)/shard_map/small_sum/pallas_call | solution.py:482
  471.2 4.2 multiply_subtract_fusion.2
  476.1 13.9 %multiply_subtract_fusion = (f32[6272,256]{1,0:T(8,128)}, f32[6272,256]{1,0:T(8,128)}, f32[6272,256]{1,0:T(8,128)}) fusion(f32[6272,256]{1,0:T(8,128)} %param.31, f32[6272,256]{1,0:T(8,128)S(1)} %copy-done.5, f32[]{:T(128)S(6)} %div.216, f32[6272,256]{1,0:T(8,128)} %param.38, f32[6272,256]{1,0:T(8,128)} %param.45), kind=kLoop, calls=%fused_computation.31 | loop fusion | flops 25690112 | bytes 44957700 | tf_op jit(solution)/shard_map/sub | solution.py:238
  490.7 5.1 multiply_subtract_fusion.1
  495.9 3.5 multiply_subtract_fusion.4
  (334 shorter events, 122.5 us)
Async XLA Ops:
  30.7 20.9 %copy-start.84 = (s32[2048,1]{0,1:T(1,128)}, s32[2048,1]{0,1:T(1,128)S(1)}, u32[]{:S(2)}) copy-start(s32[2048,1]{0,1:T(1,128)S(1)} %compare_select_fusion.2) | copy-start | bytes 24580
  39.5 14.4 %all-to-all-start = ((s32[32,1,112]{2,1,0:T(1,128)}), s32[32,1,112]{2,1,0:T(1,128)S(1)}, u32[]{:S(2)}, u32[]{:S(2)}) async-start(s32[32,1,112]{2,1,0:T(1,128)} %all_to_all.11), calls=%async_computation | async-start | bytes 32768 | tf_op jit(solution)/shard_map/all_to_all | solution.py:216
  65.4 30.1 %copy-start.58 = (f32[512,256]{1,0:T(8,128)S(1)}, f32[512,256]{1,0:T(8,128)}, u32[]{:S(2)}) copy-start(f32[512,256]{1,0:T(8,128)} %param.33) | copy-start | bytes 1572868
  65.4 46.8 %all-to-all-start.1 = ((bf16[32,112,256]{2,1,0:T(8,128)(2,1)}), bf16[32,112,256]{2,1,0:T(8,128)(2,1)S(1)}, u32[]{:S(2)}, u32[]{:S(2)}) async-start(bf16[32,112,256]{2,1,0:T(8,128)(2,1)} %bitcast.250), calls=%async_computation.1 | async-start | bytes 3670016 | tf_op jit(solution)/shard_map/all_to_all | solution.py:221
  69.0 90.4 %all-gather.9.cloned.1.call-start = ((), (), s32[]{:S(2)}) async-start(), calls=%async_computation.7 | async-start | bytes 2359296 | tf_op jit(solution)/shard_map/all_gather | solution.py:587
  97.5 7.1 %copy-start.77 = (f32[3,256]{1,0:T(4,128)S(1)}, f32[3,256]{1,0:T(4,128)}, u32[]{:S(2)}) copy-start(f32[3,256]{1,0:T(4,128)} %param.37) | copy-start | bytes 9220
  104.8 48.5 %copy-start.17 = (pred[512,512]{0,1:T(8,128)(4,1)}, pred[512,512]{0,1:T(8,128)(4,1)S(1)}, u32[]{:S(2)}) copy-start(pred[512,512]{0,1:T(8,128)(4,1)S(1)} %fusion.48) | copy-start | bytes 786436
  124.6 57.9 %all-gather.7.cloned.1.call-start = ((), (), s32[]{:S(2)}) async-start(), calls=%async_computation.6 | async-start | bytes 2359296 | tf_op jit(solution)/shard_map/all_gather | solution.py:587
  144.7 74.3 %copy-start.9 = (f32[512,256]{1,0:T(8,128)}, f32[512,256]{1,0:T(8,128)S(1)}, u32[]{:S(2)}) copy-start(f32[512,256]{1,0:T(8,128)S(1)} %get-tuple-element.183) | copy-start | bytes 1572868
  144.7 134.7 %reduce-scatter.5.cloned.1.call-start = ((), (), s32[]{:S(2)}) async-start(), calls=%async_computation.5 | async-start | bytes 2359296 | tf_op jit(solution)/shard_map/reduce_scatter | solution.py:596
  147.9 5.4 %copy-start.3 = (f32[8,512,512]{1,2,0:T(8,128)}, f32[8,512,512]{1,2,0:T(8,128)S(1)}, u32[]{:S(2)}) copy-start(f32[8,512,512]{1,2,0:T(8,128)S(1)} %get-tuple-element.189) | copy-start | bytes 25165828
  157.2 61.8 %copy-start.7 = (f32[512,256]{1,0:T(8,128)}, f32[512,256]{1,0:T(8,128)S(1)}, u32[]{:S(2)}) copy-start(f32[512,256]{1,0:T(8,128)S(1)} %get-tuple-element.191) | copy-start | bytes 1572868
  186.6 6.0 %copy-start.81 = (pred[512]{0:T(512)(128)(4,1)S(1)}, pred[512]{0:T(512)(128)(4,1)}, u32[]{:S(2)}) copy-start(pred[512]{0:T(512)(128)(4,1)} %copy-done.80) | copy-start | bytes 1540
  186.6 6.6 %copy-start.79 = (pred[512]{0:T(512)(128)(4,1)S(1)}, pred[512]{0:T(512)(128)(4,1)}, u32[]{:S(2)}) copy-start(pred[512]{0:T(512)(128)(4,1)} %copy-done.78) | copy-start | bytes 1540
  193.9 9.5 %copy-start.50 = (f32[512,256]{1,0:T(8,128)S(1)}, f32[512,256]{1,0:T(8,128)}, u32[]{:S(2)}) copy-start(f32[512,256]{1,0:T(8,128)} %get-tuple-element.185) | copy-start | bytes 1572868
  212.9 6.1 %copy-start.44 = (f32[512,256]{1,0:T(8,128)}, f32[512,256]{1,0:T(8,128)S(1)}, u32[]{:S(2)}) copy-start(f32[512,256]{1,0:T(8,128)S(1)} %get-tuple-element.172) | copy-start | bytes 1572868
  212.9 6.1 %copy-start.46 = (f32[512,256]{1,0:T(8,128)}, f32[512,256]{1,0:T(8,128)S(1)}, u32[]{:S(2)}) copy-start(f32[512,256]{1,0:T(8,128)S(1)} %get-tuple-element.173) | copy-start | bytes 1572868
  214.6 6.0 %slice-start.2 = ((s8[8388608]{0:T(1024)(128)(4,1)}), s8[4194304]{0:T(1024)(128)(4,1)S(1)}, s32[]{:S(2)}) async-start(s8[8388608]{0:T(1024)(128)(4,1)} %bitcast.235), calls=%async_computation.10 | async-start | bytes 8388608
  233.5 86.7 %reduce-scatter.3.cloned.1.call-start = ((), (), s32[]{:S(2)}) async-start(), calls=%async_computation.4 | async-start | bytes 2359296 | tf_op jit(solution)/shard_map/reduce_scatter | solution.py:596
  235.1 5.5 %copy-start.34 = (bf16[512,512]{0,1:T(8,128)(2,1)}, bf16[512,512]{0,1:T(8,128)(2,1)S(1)}, u32[]{:S(2)}) copy-start(bf16[512,512]{0,1:T(8,128)(2,1)S(1)} %convolution_convert_fusion.8) | copy-start | bytes 1572868
  235.1 9.1 %slice-start = ((s8[8388608]{0:T(1024)(128)(4,1)}), s8[4194304]{0:T(1024)(128)(4,1)S(1)}, s32[]{:S(2)}) async-start(s8[8388608]{0:T(1024)(128)(4,1)} %bitcast.233), calls=%async_computation.8 | async-start | bytes 8388608
  235.2 5.5 %copy-start.52 = (bf16[1,512,1,8,64]{1,4,3,2,0:T(8,128)(2,1)S(1)}, bf16[1,512,1,8,64]{1,4,3,2,0:T(8,128)(2,1)}, u32[]{:S(2)}) copy-start(bf16[1,512,1,8,64]{1,4,3,2,0:T(8,128)(2,1)} %fusion.41) | copy-start | bytes 1572868
  235.2 5.5 %copy-start.53 = (bf16[1,512,1,8,64]{1,4,3,2,0:T(8,128)(2,1)S(1)}, bf16[1,512,1,8,64]{1,4,3,2,0:T(8,128)(2,1)}, u32[]{:S(2)}) copy-start(bf16[1,512,1,8,64]{1,4,3,2,0:T(8,128)(2,1)} %fusion.42) | copy-start | bytes 1572868
  235.2 5.5 %copy-start.71 = (bf16[1,512,1,8,64]{1,4,3,2,0:T(8,128)(2,1)S(1)}, bf16[1,512,1,8,64]{1,4,3,2,0:T(8,128)(2,1)}, u32[]{:S(2)}) copy-start(bf16[1,512,1,8,64]{1,4,3,2,0:T(8,128)(2,1)} %fusion.43) | copy-start | bytes 1572868
  235.2 9.1 %slice-start.1 = ((s8[8388608]{0:T(1024)(128)(4,1)}), s8[4194304]{0:T(1024)(128)(4,1)S(1)}, s32[]{:S(2)}) async-start(s8[8388608]{0:T(1024)(128)(4,1)} %bitcast.233), calls=%async_computation.9 | async-start | bytes 8388608
  277.5 42.7 %copy-start.64 = (bf16[1,512,256]{2,1,0:T(8,128)(2,1)S(1)}, bf16[1,512,256]{2,1,0:T(8,128)(2,1)}, u32[]{:S(2)}) copy-start(bf16[1,512,256]{2,1,0:T(8,128)(2,1)} %get-tuple-element.164) | copy-start | bytes 786436
  448.0 23.2 %copy-start.32 = (f32[1024,256]{1,0:T(8,128)S(1)}, f32[1024,256]{1,0:T(8,128)}, u32[]{:S(2)}) copy-start(f32[1024,256]{1,0:T(8,128)} %param.35) | copy-start | bytes 3145732
  476.1 13.9 %copy-start.85 = (f32[3,256]{1,0:T(4,128)S(1)}, f32[3,256]{1,0:T(4,128)}, u32[]{:S(2)}) copy-start(f32[3,256]{1,0:T(4,128)} %param.44) | copy-start | bytes 9220
  476.1 13.9 %copy-start.86 = (f32[3,256]{1,0:T(4,128)S(1)}, f32[3,256]{1,0:T(4,128)}, u32[]{:S(2)}) copy-start(f32[3,256]{1,0:T(4,128)} %param.51) | copy-start | bytes 9220
  476.1 14.5 %copy-start.23 = (f32[256,1536]{1,0:T(8,128)S(1)}, f32[256,1536]{1,0:T(8,128)}, u32[]{:S(2)}) copy-start(f32[256,1536]{1,0:T(8,128)} %param.32) | copy-start | bytes 4718596
  490.6 5.1 %copy-start.61 = (f32[512,256]{1,0:T(8,128)S(1)}, f32[512,256]{1,0:T(8,128)}, u32[]{:S(2)}) copy-start(f32[512,256]{1,0:T(8,128)} %param.36) | copy-start | bytes 1572868
  490.6 5.1 %copy-start.72 = (f32[512,256]{1,0:T(8,128)S(1)}, f32[512,256]{1,0:T(8,128)}, u32[]{:S(2)}) copy-start(f32[512,256]{1,0:T(8,128)} %param.43) | copy-start | bytes 1572868
  (66 other events, 176.2 us)
Sparse Core Ops, SparseCore 0:
  124.7 27.3 all-gather.8
  154.5 27.8 all-gather.6
  233.6 41.2 reduce-scatter.4
  279.0 41.2 reduce-scatter.2

commit v2 on v1

--- a/solution.py
+++ b/solution.py
@@ -212,21 +212,6 @@
     return (loss_part, block_out[0].reshape(tokens, -1), block_out[1].reshape(tokens))
 
 
-def send_requests(asked_rows):
-    moved = lax.all_to_all(asked_rows, ("dp", "rows"), split_axis=0, concat_axis=0, tiled=True)
-    return moved
-
-
-def send_replies(found_rows):
-    moved = lax.all_to_all(found_rows, ("dp", "rows"), split_axis=0, concat_axis=0, tiled=True)
-    return moved
-
-
-def send_grads(row_terms):
-    moved = lax.all_to_all(row_terms, ("dp", "rows"), split_axis=0, concat_axis=0, tiled=True)
-    return moved
-
-
 def adam_step(weight, gradient, first, second, rate, decay):
     first_new = BETA_ONE * first + (1.0 - BETA_ONE) * gradient
     second_new = BETA_TWO * second + (1.0 - BETA_TWO) * gradient * gradient
@@ -243,8 +228,8 @@
     return -(-total_rows // unit) * unit
 
 
-def tail_kernel(dp_count, row_count, padded, capacity, qkv, out, up, down, pos, outgoing, incoming, gathered, square,
-                acc, low, recv0, recv1, recv2, send_a, recv_a, send_r, recv_r):
+def tail_kernel(dp_count, row_count, padded, capacity, qkv, out, up, down, pos, row_grads, slots, incoming, gathered, square,
+                outgoing, acc, low, recv0, recv1, recv2, send_a, recv_a, send_r, recv_r):
     devices = dp_count * row_count
     dp = lax.axis_index("dp")
     row = lax.axis_index("rows")
@@ -301,8 +286,21 @@
     first = pltpu.make_async_remote_copy(low.at[pl.ds(al((1 - mine) * half), half)], recv0, send_r.at[0], recv_r.at[0],
                                          device_id=where, device_id_type=MESH)
     first.start()
-    lax.fori_loop(1, devices, lambda k, c: (a2a_send(k).start(), c)[1], 0)
-    incoming[me] = outgoing[me]
+    slot_row = jnp.concatenate([slots[c : c + 1, :] for c in range(slots.shape[0])], axis=1)
+    slot_index = lax.broadcasted_iota(jnp.int32, (capacity, slot_row.shape[1]), 0).astype(jnp.float32)
+
+    def arrange(other):
+        pick = one_hot(slot_index == slot_row - (other * capacity).astype(jnp.float32))
+        return jnp.dot(pick, row_grads[...], preferred_element_type=jnp.float32).astype(jnp.bfloat16)
+
+    def send_rows(k, carry):
+        other, where = place(k)
+        outgoing[other] = arrange(other)
+        a2a_send(k).start()
+        return carry
+
+    lax.fori_loop(1, devices, send_rows, 0)
+    incoming[me] = arrange(me)
     first.wait_recv()
     base = mine * half
     pending = [first]
@@ -415,9 +413,8 @@
     lax.fori_loop(1, devices, lambda k, c: (a2a_send(k).wait_send(), c)[1], 0)
 
 
-def tail_exchange(dp_count, row_count, qkv, out, up, down, pos, outgoing):
+def tail_exchange(dp_count, row_count, capacity, qkv, out, up, down, pos, row_grads, slots):
     devices = dp_count * row_count
-    capacity = outgoing.shape[1]
     width = out.shape[1]
     rows = sum(a.size for a in (qkv, out, up, down, pos)) // width
     padded = reduce_rows(rows, devices)
@@ -425,10 +422,11 @@
     sems = 2 + 4 * bits + 4 * dp_count + 8
     return pl.pallas_call(
         functools.partial(tail_kernel, dp_count, row_count, padded, capacity),
-        out_shape=(jax.ShapeDtypeStruct(outgoing.shape, jnp.bfloat16), jax.ShapeDtypeStruct((padded, width), jnp.bfloat16),
+        out_shape=(jax.ShapeDtypeStruct((devices, capacity, width), jnp.bfloat16), jax.ShapeDtypeStruct((padded, width), jnp.bfloat16),
                    jax.ShapeDtypeStruct((8, width), jnp.float32)),
-        in_specs=[VMEM] * 6, out_specs=(VMEM,) * 3,
+        in_specs=[VMEM] * 7, out_specs=(VMEM,) * 3,
         scratch_shapes=[
+            pltpu.VMEM((devices, capacity, width), jnp.bfloat16),
             pltpu.VMEM((padded, width), jnp.float32),
             pltpu.VMEM((padded, width), jnp.bfloat16),
             pltpu.VMEM((padded // 2, width), jnp.bfloat16),
@@ -439,7 +437,227 @@
         ],
         name="tail_exchange",
         compiler_params=pltpu.CompilerParams(collective_id=3, has_side_effects=True, vmem_limit_bytes=56 * 2**20),
-    )(qkv, out, up, down, pos, outgoing)
+    )(qkv, out, up, down, pos, row_grads, slots)
+
+
+def other_device(k, dp_count, row_count):
+    devices = dp_count * row_count
+    me = lax.axis_index("dp") * row_count + lax.axis_index("rows")
+    other = lax.rem(me + k, devices)
+    return other, (other // row_count, lax.rem(other, row_count))
+
+
+def one_hot(flags):
+    return jnp.where(flags, 1.0, 0.0).astype(jnp.bfloat16)
+
+
+def lookup_kernel(dp_count, row_count, capacity, used, wanted, item_row, table_hbm, fetched, slots, received,
+                  table, pieces, slot_col, asked, ask, got, stage, ready, landed, asked_here,
+                  table_sem, local_sem, send_q, recv_q, send_a, recv_a):
+    devices = dp_count * row_count
+    me = lax.axis_index("dp") * row_count + lax.axis_index("rows")
+    rows_here = table.shape[0]
+    events = wanted.shape[0]
+    chunk = 256
+    barrier = pltpu.get_barrier_semaphore()
+    load_table = pltpu.make_async_copy(table_hbm, table, table_sem)
+    load_table.start()
+
+    def greet(k, carry):
+        other, where = other_device(k, dp_count, row_count)
+        pl.semaphore_signal(barrier, inc=1, device_id=where, device_id_type=MESH)
+        return carry
+
+    lax.fori_loop(1, devices, greet, 0)
+
+    whole_rows = item_row.shape[0]
+    lanes = item_row.shape[1]
+    pieces[pl.ds(whole_rows, pieces.shape[0] - whole_rows), :] = jnp.zeros(
+        (pieces.shape[0] - whole_rows, 3 * lanes), jnp.bfloat16
+    )
+    part = 224
+    def cut(c, carry):
+        at = pl.multiple_of(c * part, 16)
+        values = item_row[pl.ds(at, part), :]
+        for digit in range(3):
+            piece = jnp.bitwise_and(jnp.right_shift(values, 8 * digit), 255)
+            pieces[pl.ds(at, part), digit * lanes : (digit + 1) * lanes] = piece.astype(jnp.float32).astype(jnp.bfloat16)
+        return carry
+    lax.fori_loop(0, whole_rows // part, cut, 0)
+
+    lane = lax.broadcasted_iota(jnp.int32, (chunk, lanes), 1)
+    lane_f = lane.astype(jnp.float32)
+    wide = lax.broadcasted_iota(jnp.int32, (chunk, pieces.shape[0]), 1)
+    below = one_hot(
+        lax.broadcasted_iota(jnp.int32, (chunk, chunk), 1) < lax.broadcasted_iota(jnp.int32, (chunk, chunk), 0)
+    )
+    diagonal = lax.broadcasted_iota(jnp.int32, (chunk, chunk), 1) == lax.broadcasted_iota(jnp.int32, (chunk, chunk), 0)
+    asked[...] = jnp.zeros_like(asked)
+
+    def route(c, counts):
+        at = pl.multiple_of(c * chunk, chunk)
+        ids = wanted[pl.ds(at, chunk), :]
+        high = jnp.right_shift(ids, 7)
+        low = jnp.bitwise_and(ids, 127)
+        found = jnp.dot(one_hot(wide == high), pieces[...], preferred_element_type=jnp.float32)
+        value = found[:, :lanes] + 256.0 * found[:, lanes : 2 * lanes] + 65536.0 * found[:, 2 * lanes :]
+        row = jnp.sum(jnp.where(lane == low, value, 0.0), axis=1, keepdims=True)
+        owner = jnp.floor((row + 0.5) * (1.0 / rows_here))
+        local = row - owner * rows_here
+        live = ids >= 0
+        owned = jnp.logical_and(lane_f == owner, live)
+        owned_low = one_hot(owned)
+        before = jnp.dot(below, owned_low, preferred_element_type=jnp.float32) + counts
+        rank = jnp.sum(jnp.where(owned, before, 0.0), axis=1, keepdims=True)
+        slot = jnp.where(live, owner * capacity + rank, -1.0)
+        slot_col[pl.ds(at, chunk), :] = slot
+        slots[pl.ds(c, 1), :] = jnp.sum(jnp.where(diagonal, slot, 0.0), axis=0, keepdims=True)
+        local_high = jnp.floor(local * (1.0 / 128))
+        local_low = local - 128.0 * local_high
+        at_rank = lane_f == rank
+        both = jnp.concatenate(
+            [jnp.where(at_rank, local_high, 0.0), jnp.where(at_rank, local_low, 0.0)], axis=1
+        ).astype(jnp.bfloat16)
+        asked[...] += lax.dot_general(owned_low, both, (((0,), (0,)), ((), ())), preferred_element_type=jnp.float32)
+        return counts + jnp.sum(jnp.where(owned, 1.0, 0.0), axis=0, keepdims=True)
+
+    lax.fori_loop(0, events // chunk, route, jnp.zeros((1, lanes), jnp.float32))
+    rows_asked = (128.0 * asked[:, :lanes] + asked[:, lanes:]).astype(jnp.int32)
+    for d in range(devices):
+        ask[d] = rows_asked[d : d + 1, :]
+    pl.semaphore_wait(barrier, devices - 1)
+
+    def query(k, at_other):
+        other, where = other_device(k, dp_count, row_count)
+        return pltpu.make_async_remote_copy(
+            ask.at[other], got.at[other if at_other else me], send_q.at[k], recv_q.at[other if at_other else me],
+            device_id=where, device_id_type=MESH,
+        )
+
+    def answer(k, at_other):
+        other, where = other_device(k, dp_count, row_count)
+        place = pl.multiple_of((other if at_other else me) * capacity, 16)
+        return pltpu.make_async_remote_copy(
+            ready.at[k], landed.at[pl.ds(place, capacity)], send_a.at[k], recv_a.at[other if at_other else me],
+            device_id=where, device_id_type=MESH,
+        )
+
+    lax.fori_loop(1, devices, lambda k, c: (query(k, False).start(), c)[1], 0)
+    got[me] = ask[me]
+    stage[...] = jnp.zeros_like(stage)
+    load_table.wait()
+    lax.fori_loop(1, devices, lambda k, c: (query(k, True).wait_recv(), c)[1], 0)
+    received[...] = jnp.clip(got[...], 0, rows_here - 1)
+    to_scalars = pltpu.make_async_copy(received, asked_here, local_sem)
+    to_scalars.start()
+    to_scalars.wait()
+
+    def gather(source):
+        def some(c, carry):
+            at = pl.multiple_of(c * 8, 8)
+            for j in range(8):
+                row = asked_here[source, 0, at + j]
+                stage[pl.ds(at + j, 1), :] = table[pl.ds(row, 1), :]
+            return carry
+        lax.fori_loop(0, used // 8, some, 0)
+        return stage[...].astype(jnp.bfloat16)
+
+    def reply(k, carry):
+        other, where = other_device(k, dp_count, row_count)
+        ready[k] = gather(other)
+        answer(k, False).start()
+        return carry
+
+    lax.fori_loop(1, devices, reply, 0)
+    landed[pl.ds(pl.multiple_of(me * capacity, 16), capacity), :] = gather(me)
+    lax.fori_loop(1, devices, lambda k, c: (answer(k, True).wait_recv(), c)[1], 0)
+
+    slot_lane = lax.broadcasted_iota(jnp.int32, (chunk, devices * capacity), 1).astype(jnp.float32)
+
+    def settle(c, carry):
+        at = pl.multiple_of(c * chunk, chunk)
+        pick = one_hot(slot_lane == slot_col[pl.ds(at, chunk), :])
+        fetched[pl.ds(at, chunk), :] = jnp.dot(pick, landed[...], preferred_element_type=jnp.float32).astype(jnp.bfloat16)
+        return carry
+
+    lax.fori_loop(0, events // chunk, settle, 0)
+    lax.fori_loop(1, devices, lambda k, c: (query(k, False).wait_send(), c)[1], 0)
+    lax.fori_loop(1, devices, lambda k, c: (answer(k, False).wait_send(), c)[1], 0)
+
+
+def lookup(dp_count, row_count, capacity, used, wanted, item_row, item_table):
+    devices = dp_count * row_count
+    events = wanted.shape[0]
+    lanes = 128
+    width = item_table.shape[1]
+    blocks = item_row.shape[0] // lanes
+    return pl.pallas_call(
+        functools.partial(lookup_kernel, dp_count, row_count, capacity, used),
+        out_shape=(
+            jax.ShapeDtypeStruct((events, width), jnp.bfloat16),
+            jax.ShapeDtypeStruct((events // 256, 256), jnp.float32),
+            jax.ShapeDtypeStruct((devices, 1, lanes), jnp.int32),
+        ),
+        in_specs=[VMEM, VMEM, pl.BlockSpec(memory_space=pl.ANY)],
+        out_specs=(VMEM,) * 3,
+        scratch_shapes=[
+            pltpu.VMEM(item_table.shape, jnp.float32),
+            pltpu.VMEM((-(-blocks // lanes) * lanes, 3 * lanes), jnp.bfloat16),
+            pltpu.VMEM((events, 1), jnp.float32),
+            pltpu.VMEM((lanes, 2 * lanes), jnp.float32),
+            pltpu.VMEM((devices, 1, lanes), jnp.int32),
+            pltpu.VMEM((devices, 1, lanes), jnp.int32),
+            pltpu.VMEM((capacity, width), jnp.float32),
+            pltpu.VMEM((devices, capacity, width), jnp.bfloat16),
+            pltpu.VMEM((devices * capacity, width), jnp.bfloat16),
+            pltpu.SMEM((devices, 1, lanes), jnp.int32),
+            pltpu.SemaphoreType.DMA,
+            pltpu.SemaphoreType.DMA,
+            pltpu.SemaphoreType.DMA((devices,)),
+            pltpu.SemaphoreType.DMA((devices,)),
+            pltpu.SemaphoreType.DMA((devices,)),
+            pltpu.SemaphoreType.DMA((devices,)),
+        ],
+        name="lookup",
+        compiler_params=pltpu.CompilerParams(collective_id=2, has_side_effects=True, vmem_limit_bytes=56 * 2**20),
+    )(wanted, item_row.reshape(-1, lanes), item_table)
+
+
+def table_kernel(received, incoming, grads, square):
+    tile, width = grads.shape
+    step = pl.program_id(0)
+    rows = lax.broadcasted_iota(jnp.int32, (tile, received.shape[1]), 0) + step * tile
+    grad = jnp.dot(one_hot(rows == received[...]), incoming[...], preferred_element_type=jnp.float32)
+    grads[...] = grad
+
+    @pl.when(step == 0)
+    def start():
+        square[...] = jnp.zeros_like(square)
+
+    square[...] += jnp.broadcast_to(jnp.sum(grad * grad, axis=0, keepdims=True), square.shape)
+
+
+def table_gradient(rows_here, received, incoming):
+    width = incoming.shape[1]
+    tile = 224
+    return pl.pallas_call(
+        table_kernel,
+        grid=(rows_here // tile,),
+        out_shape=(
+            jax.ShapeDtypeStruct((rows_here, width), jnp.float32),
+            jax.ShapeDtypeStruct((8, width), jnp.float32),
+        ),
+        in_specs=[
+            pl.BlockSpec(received.shape, lambda i: (0, 0)),
+            pl.BlockSpec(incoming.shape, lambda i: (0, 0)),
+        ],
+        out_specs=(
+            pl.BlockSpec((tile, width), lambda i: (i, 0)),
+            pl.BlockSpec((8, width), lambda i: (0, 0)),
+        ),
+        name="table_gradient",
+        compiler_params=pltpu.CompilerParams(vmem_limit_bytes=40 * 2**20),
+    )(received, incoming)
 
 
 def small_kernel(dp_count, row_count, part, summed, by_row, by_dp, send_sem, recv_sem):
@@ -529,31 +747,18 @@
     tokens = histories * length
     requests = 2 * micro * tokens
     capacity = 3 * (requests + devices) // (2 * devices) + 1
+    used = -(-capacity // 8) * 8
     capacity = -(-capacity // 16) * 16
     dp_count, row_count = lax.axis_size("dp"), lax.axis_size("rows")
     position = jnp.arange(length, dtype=jnp.int32)
     valid_pos = (position[None, None, :] < lengths[:, :, None]).reshape(micro, tokens)
-    wanted = jnp.stack([item_ids, targets]).reshape(requests)
-    live_request = jnp.concatenate([valid_pos.reshape(-1), valid_pos.reshape(-1)])
-    table_rows = item_row[wanted]
-    owner_of = table_rows // rows_here
-    choose = (
-        (owner_of[:, None] == jnp.arange(devices, dtype=jnp.int32)[None, :]) & live_request[:, None]
-    ).astype(jnp.int32)
-    earlier = jnp.sum((jnp.cumsum(choose, axis=0) - choose) * choose, axis=1)
-    slot_of = jnp.where(live_request, owner_of * capacity + earlier, devices * capacity)
-    asked_rows = (
-        jnp.zeros((devices * capacity,), jnp.int32)
-        .at[slot_of]
-        .set(table_rows % rows_here, mode="drop")
-    )
-    received = send_requests(asked_rows.reshape(devices, capacity))
-    replies = send_replies(rounded(item_table)[received]).reshape(devices * capacity, width)
-    fetched = jnp.where(
-        live_request[:, None],
-        replies[jnp.minimum(slot_of, devices * capacity - 1)],
-        jnp.zeros((), jnp.bfloat16),
-    )
+    wanted = jnp.where(
+        valid_pos.reshape(1, -1), jnp.stack([item_ids, targets]).reshape(2, micro * tokens), -1
+    ).reshape(requests, 1)
+    fetched, slots, received = lookup(
+        dp_count, row_count, capacity, used, wanted, item_row, item_table
+    )
+    received = received[:, 0, :capacity].reshape(1, devices * capacity)
     fetched = fetched.reshape(2, micro, tokens, width)
     matrices = (rounded(qkv_weight), rounded(out_weight), rounded(up_weight), rounded(down_weight))
     scaling = math.sqrt(width)
@@ -612,27 +817,22 @@
         embed_grads.append(scaling * grad_embedded)
     target_part = jnp.stack(target_grads)
     row_grads = jnp.concatenate([jnp.stack(embed_grads), target_part]).reshape(requests, width)
-    outgoing = (
-        jnp.zeros((devices * capacity, width), jnp.bfloat16)
-        .at[slot_of]
-        .set(rounded(row_grads), mode="drop")
-    )
     incoming, gathered, square = tail_exchange(
         dp_count,
         row_count,
+        capacity,
         running[0],
         running[1],
         running[2],
         running[3],
         grad_positions,
-        outgoing.reshape(devices, capacity, width),
-    )
-    table_grad = (
-        jnp.zeros((rows_here, width), jnp.float32)
-        .at[received.reshape(-1)]
-        .add(incoming.reshape(-1, width).astype(jnp.float32))
-    )
-    own_square = jnp.sum(table_grad * table_grad) + jnp.sum(square[0])
+        rounded(row_grads),
+        slots,
+    )
+    table_grad, table_square = table_gradient(
+        rows_here, received, incoming.reshape(devices * capacity, width)
+    )
+    own_square = jnp.sum(table_square[0] + square[0])
     scalars = jnp.stack([loss_local, jnp.sum(valid_pos.astype(jnp.float32)), own_square])
     part = jnp.concatenate(
         [grad_gains.reshape(-1), jnp.pad(scalars, (0, 1024 - grad_gains.size - 3))]

time: 516 us -> 472 us (0.915)
  Pallas kernels: 91.3 us -> 170 us
  other arithmetic: 131 us -> 80.3 us
  local copies, waits for them, and re-layouts: 78.1 us -> 32.9 us
  waiting for transfers between devices: 65.9 us -> 50.3 us
  starting transfers between devices: 11.6 us -> 0.68 us
    pallas_call x0 -> x2, Pallas kernels: none -> 73.9 us  [the longest x1 56.4 us: lookup(): pl.pallas_call(functools.partial(lookup_kernel, dp_count, row_count, capa...]
    gather x3 -> x0, local copies, waits for them, and re-layouts: 32.3 us -> none  [the longest x1 11.8 us: local(): table_rows = item_row[wanted]]
    scatter-add x1 -> x0, other arithmetic: 28.7 us -> none  [local(): table_grad = jnp.zeros((rows_here, width), jnp.float32).at[received.resha...]
    scatter x2 -> x0, local copies, waits for them, and re-layouts: 19.1 us -> none  [the longest x1 11.1 us: local(): outgoing = jnp.zeros((devices * capacity, width), jnp.bfloat16).at[slot_o...]
    all_gather x2, waiting for transfers between devices: 16.8 us -> 0.02 us  [local(): lax.all_gather(fetched[1, micro_index], 'rows', axis=0, tiled=True)]
    all_to_all x2 -> x0, starting transfers between devices: 10.9 us -> none  [the longest x1 7.3 us: send_requests(): lax.all_to_all(asked_rows, ('dp', 'rows'), split_axis=0, concat_axis=0, t...]
    another operation x4 -> x0, other arithmetic: 10.1 us -> none
    convert_element_type x9 -> x8, other arithmetic: 24.2 us -> 14.9 us  [rounded(): return values.astype(jnp.bfloat16)]
  transfers between devices with their start and end apart: 6 -> 4, of which waited for: 4 -> 2; matrix products, arithmetic and copies ran while one was open for 18% -> 18% of each run, Pallas kernels for 0% -> 0%
where the time goes in v2:
time: 472 us; the launch traced here: 464 us
  Pallas kernels  170 us (36%)
  matrix products  84.5 us (18%)
  other arithmetic  80.3 us (17%)
  waiting for transfers between devices  50.3 us (11%)
  local copies, waits for them, and re-layouts  32.9 us (7%)
  blocking collectives  25.7 us (5%)
  between operations  19.1 us (4%)
    pallas_call x1, Pallas kernels, tail_exchange(): pl.pallas_call(functools.partial(tail_kernel, dp_count, row_count, padded...  83.7 us
    pallas_call x1, Pallas kernels, lookup(): pl.pallas_call(functools.partial(lookup_kernel, dp_count, row_count, capa...  56.4 us
    reduce_scatter x2, waiting for transfers between devices, local(): lax.psum_scatter(inner_rows(grad_logits, query_low).astype(jnp.bfloat16),...  49.5 us
    sub x6, other arithmetic, adam_step(): return (weight - rate * (stepped + decay * weight), first_new, second_new)  29.1 us
    all_gather x2, blocking collectives, local(): lax.all_gather(bias_low, 'rows', axis=0, tiled=True)  25.7 us
    unnamed x219, local copies, waits for them, and re-layouts  22.4 us
    dot_general x10, matrix products, inner_cols(): lax.dot_general(first_op, second_op, (((1,), (1,)), ((), ())), preferred_...  18.7 us
    pallas_call x1, Pallas kernels, table_gradient(): pl.pallas_call(table_kernel, grid=(rows_here // tile,), out_shape=(jax.Sh...  17.5 us
  transfers between devices with their start and end apart: 4, of which 2 were waited for; matrix products, arithmetic and copies ran while one was open for 18% of the time, Pallas kernels for 0%

profile of v2, /device:TPU:0, one launch (start us, length us, event | category | flops | bytes accessed | tf_op | source)
XLA Modules:
  0.0 463.9 jit_solution(11117937870073213986)
XLA Ops:
  10.1 56.4 %lookup.1 = (bf16[2048,256]{1,0:T(8,128)(2,1)}, f32[8,256]{1,0:T(8,128)}, s32[32,1,128]{2,1,0:T(1,128)}) custom-call(s32[2048,1]{1,0:T(8,128)} %bitcast.214, s32[1568,128]{1,0:T(8,128)} %bitcast.225, f32[6272,256]{1,0:T(8,128)} %table_hbm.1), custom_call_target="tpu_custom_call" | custom-call | tf_op jit(solution)/shard_map/lookup/pallas_call | solution.py:594
  78.3 2.6 copy.87
  89.1 2.4 convolution_convert_fusion.5
  95.2 4.7 %fusion.5 = (f32[8,512]{1,0:T(8,128)S(1)}, f32[8,512,512]{1,2,0:T(8,128)}) fusion(pred[512,512]{0,1:T(8,128)(4,1)S(1)} %copy-done.18, bf16[1,512,3,8,64]{1,4,3,2,0:T(8,128)(2,1)S(1)} %bitcast.207), kind=kOutput, calls=%fused_computation.27 | convolution fusion | flops 274722816 | bytes 9715712 | tf_op jit(solution)/shard_map/sqhe,skhe->shqk/dot_general | solution.py:67
  101.1 17.1 %all-gather.3 = bf16[8,1,512]{2,1,0:T(2,128)(2,1)S(1)} all-gather(bf16[1,1,512]{2,1,0:T(2,128)(2,1)S(1)} %reshape.639), channel_id=1, replica_groups=mesh['dp'=4,'rows'=8] {'rows'}, dimensions={0}, use_global_device_ids=true | all-gather | bytes 9216 | tf_op jit(solution)/shard_map/all_gather | solution.py:793
  118.2 8.6 %all-gather.2 = bf16[8,1,512]{2,1,0:T(2,128)(2,1)S(1)} all-gather(bf16[1,1,512]{2,1,0:T(2,128)(2,1)S(1)} %reshape.637), channel_id=1, replica_groups=mesh['dp'=4,'rows'=8] {'rows'}, dimensions={0}, use_global_device_ids=true | all-gather | bytes 9216 | tf_op jit(solution)/shard_map/all_gather | solution.py:793
  127.0 5.3 %exponential_reduce_fusion.3 = f32[8,512]{1,0:T(8,128)S(1)} fusion(f32[8,512,512]{1,2,0:T(8,128)} %get-tuple-element.191, f32[8,512]{1,0:T(8,128)S(1)} %get-tuple-element.190, pred[512,512]{0,1:T(8,128)(4,1)S(1)} %copy-done.18), kind=kLoop, calls=%fused_computation.20 | loop fusion | flops 8384512 | bytes 8683520 | tf_op jit(solution)/shard_map/reduce_sum | solution.py:81
  132.7 3.5 convolution_convert_fusion.7
  139.3 6.4 %add_reduce_fusion = (f32[512]{0:T(512)S(1)}, f32[512,4096]{1,0:T(8,128)}) fusion(f32[4096]{0:T(1024)S(1)} %bitcast.226, bf16[1,1,4096,256]{3,2,1,0:T(8,128)(2,1)} %all-gather.9.cloned.1.call-done, f32[512,256]{1,0:T(8,128)} %get-tuple-element.187, f32[512]{0:T(512)S(1)} %fusion.76, f32[256]{0:T(256)S(1)} %bitcast.247), kind=kOutput, calls=%fused_computation.22 | convolution fusion | flops 1078328832 | bytes 11031552 | tf_op jit(solution)/shard_map/while/body/eval_jaxpr/dot_general | solution.py:43
  145.7 3.1 add_reduce_fusion.1
  149.7 5.8 %select_reduce_fusion = (f32[512]{0:T(512)S(1)}, f32[512]{0:T(512)S(1)}, f32[512]{0:T(512)S(1)}, f32[512]{0:T(512)S(1)}) fusion(f32[512,4096]{1,0:T(8,128)S(1)} %copy-done.4, f32[4096]{0:T(1024)S(1)} %bitcast.227, s32[512]{0:T(512)S(1)} %iota_add_fusion, f32[512]{0:T(512)S(1)} %get-tuple-element.188, f32[512]{0:T(512)S(1)} %get-tuple-element.196, ...), kind=kLoop, calls=%fused_computation.7 | loop fusion | flops 23066624 | bytes 16824320 | tf_op jit(solution)/shard_map/while/body/eval_jaxpr/reduce_sum | solution.py:194
  156.8 7.7 %fusion.3 = (bf16[512,4096]{1,0:T(8,128)(2,1)S(1)}, bf16[512,4096]{1,0:T(8,128)(2,1)}) fusion(f32[512,4096]{1,0:T(8,128)S(1)} %copy-done.4, f32[512]{0:T(512)S(1)} %copy-done.85, f32[512]{0:T(512)S(1)} %get-tuple-element.138, f32[4096]{0:T(1024)S(1)} %bitcast.228, s32[512]{0:T(512)S(1)} %iota_add_fusion, f32[512]{0:T(512)S(1)} %copy-done.86, ...), kind=kLoop, calls=%fused_computation.6 | loop fusion | flops 25165824 | bytes 25208832 | tf_op jit(solution)/shard_map/while/body/eval_jaxpr/convert_element_type | solution.py:29
  166.5 2.7 convolution_convert_fusion
  169.3 4.3 fusion.27
  183.6 3.1 fusion.40
  186.8 3.3 multiply_reduce_fusion.1
  190.1 2.7 multiply_convert_fusion.1
  198.2 5.5 %multiply_reduce_fusion = (f32[8,512]{1,0:T(8,128)S(1)}, f32[8,512,512]{1,2,0:T(8,128)S(1)}) fusion(f32[8,512,512]{1,2,0:T(8,128)} %copy-done.2, f32[8,512]{1,0:T(8,128)S(1)} %log_add_fusion, pred[512,512]{0,1:T(8,128)(4,1)S(1)} %fusion.44, bf16[512,8,64]{0,2,1:T(8,128)(2,1)S(1)} %bitcast.215, bf16[1,512,3,8,64]{1,4,3,2,0:T(8,128)(2,1)S(1)} %bitcast.203), kind=kOutput, calls=%fused_computation.10 | convolution fusion | flops 278917120 | bytes 18120704 | tf_op jit(solution)/shard_map/sqhe,skhe->shqk/dot_general | solution.py:93
  206.4 2.8 multiply_convert_fusion
  214.1 2.7 convolution_convert_fusion.1
  216.9 6.4 %fusion.41 = bf16[1,512,1,8,64]{1,4,3,2,0:T(8,128)(2,1)} fusion(bf16[512,8,64]{0,2,1:T(8,128)(2,1)S(1)} %bitcast.216, f32[8,512,512]{1,2,0:T(8,128)} %copy-done.2, f32[8,512]{1,0:T(8,128)S(1)} %log_add_fusion, pred[512,512]{0,1:T(8,128)(4,1)S(1)} %fusion.44), kind=kOutput, calls=%fused_computation.95 | convolution fusion | flops 277086208 | bytes 9715712 | tf_op jit(solution)/shard_map/shqk,sqhe->skhe/dot_general | solution.py:96
  228.0 2.6 fusion.57
  241.9 4.2 reduce-scatter.5.cloned.1.call-done
  246.1 45.3 %reduce-scatter.3.cloned.1.call-done = bf16[512,256]{1,0:T(8,128)(2,1)} async-done(((bf16[4096,256]{1,0:T(8,128)(2,1)}), bf16[512,256]{1,0:T(8,128)(2,1)}) %reduce-scatter.3.cloned.1.call-update) | async-done | bytes 262160 | tf_op jit(solution)/shard_map/reduce_scatter | solution.py:801
  293.5 83.7 %tail_exchange.1 = (bf16[32,112,256]{2,1,0:T(8,128)(2,1)}, bf16[4608,256]{1,0:T(8,128)(2,1)}, f32[8,256]{1,0:T(8,128)}) custom-call(f32[256,1536]{1,0:T(8,128)} %convolution_add_fusion.qkv, f32[512,256]{1,0:T(8,128)} %convolution_add_fusion.5.out, f32[256,1024]{1,0:T(8,128)} %convolution_add_fusion.2.up, f32[1024,256]{1,0:T(8,128)} %convolution_add_fusion.1.down, ...), custom_call_target="tpu_custom_call" | custom-call | tf_op jit(solution)/shard_map/tail_exchange/pallas_call | solution.py:423
  385.7 17.5 %table_gradient.1 = (f32[6272,256]{1,0:T(8,128)S(1)}, f32[8,256]{1,0:T(8,128)S(1)}) custom-call(s32[1,3584]{1,0:T(1,128)S(1)} %reshape_squeeze.2.received, bf16[3584,256]{1,0:T(8,128)(2,1)S(1)} %bitcast.194), custom_call_target="tpu_custom_call" | custom-call | tf_op jit(solution)/shard_map/table_gradient/pallas_call | solution.py:643
  403.1 2.7 copy-done
  409.1 12.7 %small_sum.1 = f32[8,128]{1,0:T(8,128)} custom-call(f32[8,128]{1,0:T(8,128)} %maximum_bitcast_fusion.part), custom_call_target="tpu_custom_call" | custom-call | tf_op jit(solution)/shard_map/small_sum/pallas_call | solution.py:700
  426.6 3.9 multiply_subtract_fusion.2
  431.1 5.1 %multiply_subtract_fusion.1 = (f32[256,1536]{1,0:T(8,128)}, f32[256,1536]{1,0:T(8,128)}, f32[256,1536]{1,0:T(8,128)}) fusion(f32[256,1536]{1,0:T(8,128)S(1)} %copy-done.26, f32[256,1536]{1,0:T(8,128)S(1)} %copy-done.39, f32[]{:T(128)S(6)} %div.186, f32[256,1536]{1,0:T(8,128)} %param.39, f32[256,1536]{1,0:T(8,128)} %param.46), kind=kLoop, calls=%fused_computation.70 | loop fusion | flops 6291456 | bytes 11010052 | tf_op jit(solution)/shard_map/sub | solution.py:223
  436.3 13.6 %multiply_subtract_fusion = (f32[6272,256]{1,0:T(8,128)}, f32[6272,256]{1,0:T(8,128)}, f32[6272,256]{1,0:T(8,128)}) fusion(f32[6272,256]{1,0:T(8,128)} %table_hbm.1, f32[6272,256]{1,0:T(8,128)S(1)} %bitcast.193, f32[]{:T(128)S(6)} %div.186, f32[6272,256]{1,0:T(8,128)} %param.38, f32[6272,256]{1,0:T(8,128)} %param.45), kind=kLoop, calls=%fused_computation.25 | loop fusion | flops 25690112 | bytes 44957700 | tf_op jit(solution)/shard_map/sub | solution.py:223
  450.0 3.7 multiply_subtract_fusion.4
  (326 shorter events, 92.6 us)
Async XLA Ops:
  7.2 131.6 %all-gather.9.cloned.1.call-start = ((), (), s32[]{:S(2)}) async-start(), calls=%async_computation.5 | async-start | bytes 2359296 | tf_op jit(solution)/shard_map/all_gather | solution.py:792
  10.1 59.9 %copy-start.95 = (s32[2,1]{0,1:T(1,128)S(1)}, s32[2,1]{0,1:T(1,128)}, u32[]{:S(2)}) copy-start(s32[2,1]{0,1:T(1,128)} %param.28) | copy-start | bytes 28
  10.1 62.5 %copy-start.98 = (f32[2,1,512]{2,1,0:T(1,128)S(1)}, f32[2,1,512]{2,1,0:T(1,128)}, u32[]{:S(2)}) copy-start(f32[2,1,512]{2,1,0:T(1,128)} %param.29) | copy-start | bytes 12292
  10.1 62.5 %copy-start.84 = (f32[3,256]{1,0:T(4,128)S(1)}, f32[3,256]{1,0:T(4,128)}, u32[]{:S(2)}) copy-start(f32[3,256]{1,0:T(4,128)} %param.37) | copy-start | bytes 9220
  66.5 7.1 %copy-start.64 = (f32[512,256]{1,0:T(8,128)S(1)}, f32[512,256]{1,0:T(8,128)}, u32[]{:S(2)}) copy-start(f32[512,256]{1,0:T(8,128)} %param.33) | copy-start | bytes 1572868
  66.5 7.9 %copy-start.36 = (f32[256,1024]{1,0:T(8,128)S(1)}, f32[256,1024]{1,0:T(8,128)}, u32[]{:S(2)}) copy-start(f32[256,1024]{1,0:T(8,128)} %param.34) | copy-start | bytes 3145732
  66.6 7.9 %copy-start.34 = (f32[1024,256]{1,0:T(8,128)S(1)}, f32[1024,256]{1,0:T(8,128)}, u32[]{:S(2)}) copy-start(f32[1024,256]{1,0:T(8,128)} %param.35) | copy-start | bytes 3145732
  68.6 77.1 %all-gather.7.cloned.1.call-start = ((), (), s32[]{:S(2)}) async-start(), calls=%async_computation.4 | async-start | bytes 2359296 | tf_op jit(solution)/shard_map/all_gather | solution.py:792
  69.3 176.7 %reduce-scatter.5.cloned.1.call-start = ((), (), s32[]{:S(2)}) async-start(), calls=%async_computation.3 | async-start | bytes 2359296 | tf_op jit(solution)/shard_map/reduce_scatter | solution.py:801
  72.7 27.3 %copy-start.89 = (pred[512]{0:T(512)(128)(4,1)}, pred[512]{0:T(512)(128)(4,1)S(1)}, u32[]{:S(2)}) copy-start(pred[512]{0:T(512)(128)(4,1)S(1)} %get-tuple-element.112) | copy-start | bytes 1540
  72.7 27.8 %copy-start.87 = (pred[512]{0:T(512)(128)(4,1)}, pred[512]{0:T(512)(128)(4,1)S(1)}, u32[]{:S(2)}) copy-start(pred[512]{0:T(512)(128)(4,1)S(1)} %get-tuple-element.113) | copy-start | bytes 1540
  92.3 89.8 %copy-start.6 = (f32[512,256]{1,0:T(8,128)}, f32[512,256]{1,0:T(8,128)S(1)}, u32[]{:S(2)}) copy-start(f32[512,256]{1,0:T(8,128)S(1)} %get-tuple-element.185) | copy-start | bytes 1572868
  94.4 32.5 %copy-start.91 = (f32[512]{0:T(512)}, f32[512]{0:T(512)S(1)}, u32[]{:S(2)}) copy-start(f32[512]{0:T(512)S(1)} %get-tuple-element.186) | copy-start | bytes 6148
  138.8 36.9 %copy-start.54 = (f32[512,256]{1,0:T(8,128)}, f32[512,256]{1,0:T(8,128)S(1)}, u32[]{:S(2)}) copy-start(f32[512,256]{1,0:T(8,128)S(1)} %get-tuple-element.195) | copy-start | bytes 1572868
  149.7 6.5 %copy-start.88 = (pred[512]{0:T(512)(128)(4,1)S(1)}, pred[512]{0:T(512)(128)(4,1)}, u32[]{:S(2)}) copy-start(pred[512]{0:T(512)(128)(4,1)} %copy-done.87) | copy-start | bytes 1540
  149.7 7.1 %copy-start.85 = (f32[512]{0:T(512)S(1)}, f32[512]{0:T(512)}, u32[]{:S(2)}) copy-start(f32[512]{0:T(512)} %convert_element_type.230) | copy-start | bytes 6148
  149.7 7.1 %copy-start.86 = (f32[512]{0:T(512)S(1)}, f32[512]{0:T(512)}, u32[]{:S(2)}) copy-start(f32[512]{0:T(512)} %convert_element_type.208) | copy-start | bytes 6148
  156.8 9.7 %copy-start.56 = (f32[512,256]{1,0:T(8,128)S(1)}, f32[512,256]{1,0:T(8,128)}, u32[]{:S(2)}) copy-start(f32[512,256]{1,0:T(8,128)} %get-tuple-element.187) | copy-start | bytes 1572868
  196.6 94.8 %reduce-scatter.3.cloned.1.call-start = ((), (), s32[]{:S(2)}) async-start(), calls=%async_computation.2 | async-start | bytes 2359296 | tf_op jit(solution)/shard_map/reduce_scatter | solution.py:801
  198.2 8.2 %slice-start.2 = ((s8[8388608]{0:T(1024)(128)(4,1)}), s8[4194304]{0:T(1024)(128)(4,1)S(1)}, s32[]{:S(2)}) async-start(s8[8388608]{0:T(1024)(128)(4,1)} %bitcast.195), calls=%async_computation.8 | async-start | bytes 8388608
  198.2 8.1 %slice-start.3 = ((s8[8388608]{0:T(1024)(128)(4,1)}), s8[4194304]{0:T(1024)(128)(4,1)S(1)}, s32[]{:S(2)}) async-start(s8[8388608]{0:T(1024)(128)(4,1)} %bitcast.195), calls=%async_computation.9 | async-start | bytes 8388608
  240.0 51.4 %copy-start.72 = (bf16[1,512,256]{2,1,0:T(8,128)(2,1)S(1)}, bf16[1,512,256]{2,1,0:T(8,128)(2,1)}, u32[]{:S(2)}) copy-start(bf16[1,512,256]{2,1,0:T(8,128)(2,1)} %get-tuple-element.168) | copy-start | bytes 786436
  381.3 49.2 %copy-start.96 = (f32[3,256]{1,0:T(4,128)S(1)}, f32[3,256]{1,0:T(4,128)}, u32[]{:S(2)}) copy-start(f32[3,256]{1,0:T(4,128)} %param.44) | copy-start | bytes 9220
  381.3 49.2 %copy-start.97 = (f32[3,256]{1,0:T(4,128)S(1)}, f32[3,256]{1,0:T(4,128)}, u32[]{:S(2)}) copy-start(f32[3,256]{1,0:T(4,128)} %param.51) | copy-start | bytes 9220
  381.4 45.2 %copy-start.35 = (f32[1024,256]{1,0:T(8,128)S(1)}, f32[1024,256]{1,0:T(8,128)}, u32[]{:S(2)}) copy-start(f32[1024,256]{1,0:T(8,128)} %param.35) | copy-start | bytes 3145732
  381.4 45.2 %copy-start.69 = (f32[1024,256]{1,0:T(8,128)S(1)}, f32[1024,256]{1,0:T(8,128)}, u32[]{:S(2)}) copy-start(f32[1024,256]{1,0:T(8,128)} %param.42) | copy-start | bytes 3145732
  426.6 9.6 %slice-start = ((s8[6422528]{0:T(1024)(128)(4,1)}), s8[4194304]{0:T(1024)(128)(4,1)S(1)}, s32[]{:S(2)}) async-start(s8[6422528]{0:T(1024)(128)(4,1)} %bitcast.192), calls=%async_computation.6 | async-start | bytes 8388608
  436.2 13.7 %copy-start.65 = (f32[512,256]{1,0:T(8,128)S(1)}, f32[512,256]{1,0:T(8,128)}, u32[]{:S(2)}) copy-start(f32[512,256]{1,0:T(8,128)} %param.33) | copy-start | bytes 1572868
  436.2 13.7 %copy-start.67 = (f32[512,256]{1,0:T(8,128)S(1)}, f32[512,256]{1,0:T(8,128)}, u32[]{:S(2)}) copy-start(f32[512,256]{1,0:T(8,128)} %param.36) | copy-start | bytes 1572868
  436.2 13.7 %copy-start.80 = (f32[512,256]{1,0:T(8,128)S(1)}, f32[512,256]{1,0:T(8,128)}, u32[]{:S(2)}) copy-start(f32[512,256]{1,0:T(8,128)} %param.43) | copy-start | bytes 1572868
  436.3 13.7 %copy-start.81 = (f32[512,256]{1,0:T(8,128)S(1)}, f32[512,256]{1,0:T(8,128)}, u32[]{:S(2)}) copy-start(f32[512,256]{1,0:T(8,128)} %param.50) | copy-start | bytes 1572868
  436.3 13.7 %copy-start.82 = (f32[512,256]{1,0:T(8,128)S(1)}, f32[512,256]{1,0:T(8,128)}, u32[]{:S(2)}) copy-start(f32[512,256]{1,0:T(8,128)} %param.47) | copy-start | bytes 1572868
  (77 other events, 221.8 us)
Sparse Core Ops, SparseCore 0:
  68.7 44.4 all-gather.8
  115.7 27.9 all-gather.6
  196.7 49.3 reduce-scatter.4
  250.1 41.2 reduce-scatter.2

commit v3 on v2

--- a/solution.py
+++ b/solution.py
@@ -660,6 +660,544 @@
     )(received, incoming)
 
 
+def dot_nn(first_op, second_op):
+    return jnp.dot(first_op, second_op, preferred_element_type=jnp.float32)
+
+
+def dot_nt(first_op, second_op):
+    return lax.dot_general(
+        first_op, second_op, (((1,), (1,)), ((), ())), preferred_element_type=jnp.float32
+    )
+
+
+def dot_tn(first_op, second_op):
+    return lax.dot_general(
+        first_op, second_op, (((0,), (0,)), ((), ())), preferred_element_type=jnp.float32
+    )
+
+
+def inverse_rms(values):
+    return lax.rsqrt(jnp.mean(values * values, axis=-1, keepdims=True) + NORM_EPS)
+
+
+def rms_back(values, gain_row, grad):
+    scale = inverse_rms(values)
+    grad_scaled = grad * gain_row
+    inner = jnp.mean(values * grad_scaled, axis=-1, keepdims=True)
+    gain_part = jnp.sum(grad * values * scale, axis=0, keepdims=True)
+    return scale * grad_scaled - values * (scale * scale * scale * inner), gain_part
+
+
+def subsets(bits):
+    found = [()]
+    for bit in bits:
+        found = found + [one + (bit,) for one in found]
+    return found
+
+
+def flip(index, bits):
+    for bit in bits:
+        step = 1 << bit
+        index = index + step - 2 * step * lax.rem(index // step, 2)
+    return index
+
+
+def layer_kernel(row_count, lengths, items, targets, correction, qkv_hbm, out_hbm, up_hbm, down_hbm, positions, gains,
+                 grad_qkv, grad_out, grad_up, grad_down, grad_positions, row_grads, small,
+                 qkv_low, out_low, up_low, down_low, embedded, hidden_one, joined, probs_top, probs_low, attended,
+                 middle, hidden_two, slope, active, output, query, cand, bias, cand_grads, landing, logits,
+                 grad_logits, highest, scores, grad_scores, grad_middle_low, grad_attended, part_k, part_v,
+                 load_sem, send_b, recv_b, send_g, recv_g, send_s, recv_s):
+    micro = 2
+    tokens = positions.shape[0]
+    half = tokens // 2
+    width = positions.shape[1]
+    inner = out_low.shape[0]
+    bits = row_count.bit_length() - 1
+    dp = lax.axis_index("dp")
+    row = lax.axis_index("rows")
+    bf = jnp.bfloat16
+    barrier = pltpu.get_barrier_semaphore()
+    for k in range(1, row_count):
+        pl.semaphore_signal(
+            barrier, inc=1, device_id=(dp, lax.rem(row + k, row_count)), device_id_type=MESH
+        )
+    ff = up_low.shape[1]
+    loads = [
+        (qkv_hbm, 0, 0, 3 * inner, qkv_low),
+        (up_hbm, 0, 3 * inner, ff, up_low),
+    ]
+    at = 3 * inner + ff
+    for source, low in ((out_hbm, out_low), (down_hbm, down_low)):
+        for k in range(source.shape[0] // width):
+            loads.append((source, k * width, at, width, low))
+            at += width
+    copies = []
+    for k, (source, first, at, count, low) in enumerate(loads):
+        copy = pltpu.make_async_copy(
+            source.at[pl.ds(first, width)], logits.at[:, pl.ds(at, count)], load_sem.at[k]
+        )
+        copy.start()
+        copies.append(copy)
+
+    column = lax.broadcasted_iota(jnp.int32, (1, tokens), 1)
+    for m in range(micro):
+        own_bias = jnp.where(
+            column < lengths[m], (-correction[m : m + 1, :]).astype(bf).astype(jnp.float32), MASKED
+        )
+        bias[row, m : m + 1, :] = own_bias.astype(bf).astype(jnp.float32)
+        cand[m, pl.ds(pl.multiple_of(row * tokens, tokens), tokens), :] = targets[m * tokens : (m + 1) * tokens, :]
+    pl.semaphore_wait(barrier, row_count - 1)
+
+    pending = []
+    for k in range(1, row_count):
+        copy = pltpu.make_async_remote_copy(
+            bias.at[row], bias.at[row], send_b.at[k], recv_b.at[row],
+            device_id=(dp, lax.rem(row + k, row_count)), device_id_type=MESH,
+        )
+        copy.start()
+        pending.append(copy)
+
+    orders = [list(range(1, bits)) + [0], list(range(bits - 1, 0, -1)) + [0]]
+    block_of = lambda ref, m, owner: ref.at[m, pl.ds(pl.multiple_of(owner * tokens, tokens), tokens)]
+    gather_steps = []
+    count = 0
+    for step in range(bits):
+        here = []
+        for m in range(micro):
+            for mask in subsets(orders[m][:step]):
+                here.append((m, orders[m][step], mask, count))
+                count += 1
+        gather_steps.append(here)
+
+    def gather_start(step):
+        for m, bit, mask, sem in gather_steps[step]:
+            mine = flip(row, mask)
+            copy = pltpu.make_async_remote_copy(
+                block_of(cand, m, mine), block_of(cand, m, mine), send_g.at[sem], recv_g.at[sem],
+                device_id=(dp, flip(row, (bit,))), device_id_type=MESH,
+            )
+            copy.start()
+            pending.append(copy)
+
+    def gather_wait(step):
+        for m, bit, mask, sem in gather_steps[step]:
+            theirs = flip(flip(row, (bit,)), mask)
+            pltpu.make_async_remote_copy(
+                block_of(cand, m, theirs), block_of(cand, m, theirs), send_g.at[sem], recv_g.at[sem],
+                device_id=(dp, flip(row, (bit,))), device_id_type=MESH,
+            ).wait_recv()
+
+    gather_start(0)
+
+    scatter_orders = [[0] + list(range(1, bits)), [0] + list(range(bits - 1, 0, -1))]
+    scatter_steps = []
+    count = 0
+    for m in range(micro):
+        levels = []
+        for step in range(bits):
+            bit = scatter_orders[m][step]
+            levels.append([(bit, mask, count + i) for i, mask in enumerate(subsets(scatter_orders[m][step + 1 :]))])
+            count += len(levels[-1])
+        scatter_steps.append(levels)
+
+    def scatter_start(m, step):
+        for bit, mask, sem in scatter_steps[m][step]:
+            there = flip(row, (bit,))
+            copy = pltpu.make_async_remote_copy(
+                block_of(cand_grads, m, flip(there, mask)), landing.at[sem], send_s.at[sem], recv_s.at[sem],
+                device_id=(dp, there), device_id_type=MESH,
+            )
+            copy.start()
+            pending.append(copy)
+
+    def scatter_wait(m, step):
+        for bit, mask, sem in scatter_steps[m][step]:
+            there = flip(row, (bit,))
+            pltpu.make_async_remote_copy(
+                block_of(cand_grads, m, flip(row, mask)), landing.at[sem], send_s.at[sem], recv_s.at[sem],
+                device_id=(dp, there), device_id_type=MESH,
+            ).wait_recv()
+            base = flip(row, mask) * tokens
+            last = step == bits - 1
+
+            def add(c, carry):
+                at = pl.multiple_of(base + c * 64, 64)
+                near = pl.multiple_of(c * 64, 64)
+                total = cand_grads[m, pl.ds(at, 64), :].astype(jnp.float32) + landing[sem, pl.ds(near, 64), :].astype(jnp.float32)
+                if last:
+                    row_grads[pl.ds(pl.multiple_of((micro + m) * tokens + c * 64, 64), 64), :] = total.astype(bf)
+                else:
+                    cand_grads[m, pl.ds(at, 64), :] = total.astype(bf)
+                return carry
+
+            lax.fori_loop(0, tokens // 64, add, 0)
+
+    for copy, (source, first, at, count, low) in zip(copies, loads):
+        copy.wait()
+    for source, first, at, count, low in loads:
+        low[pl.ds(first, width), :] = logits[:, pl.ds(at, count)].astype(bf)
+
+    chunks = micro * 2
+    gain_one, gain_two, gain_three = gains[0:1, :], gains[1:2, :], gains[2:3, :]
+    scaling = math.sqrt(width)
+
+    def project(c, carry):
+        at = pl.multiple_of(c * half, half)
+        near = pl.multiple_of(lax.rem(c, 2) * half, half)
+        values = scaling * items[pl.ds(at, half), :].astype(jnp.float32) + positions[pl.ds(near, half), :]
+        embedded[pl.ds(at, half), :] = values
+        normed = (values * inverse_rms(values) * gain_one).astype(bf)
+        hidden_one[pl.ds(at, half), :] = normed
+        joined[pl.ds(at, half), :inner] = (dot_nn(normed, qkv_low[:, :inner]).astype(bf) * bf(0.125))
+        joined[pl.ds(at, half), inner:] = dot_nn(normed, qkv_low[:, inner:]).astype(bf)
+        return carry
+
+    lax.fori_loop(0, chunks, project, 0)
+    gather_wait(0)
+    gather_start(1)
+
+    lane = lax.broadcasted_iota(jnp.int32, (1, 128), 1)
+    head_mask = [jnp.where(lane < 64, 1.0, 0.0).astype(bf), jnp.where(lane < 64, 0.0, 1.0).astype(bf)]
+    pairs = inner // 128
+    sub = 32
+
+    def attend(m):
+        masked_row = jnp.where(column < lengths[m], 0.0, MASKED)
+        base = m * tokens
+
+        def pair(hp, carry):
+            lanes = [pl.ds(pl.multiple_of(k * inner + hp * 128, 128), 128) for k in range(3)]
+            keys = joined[base : base + tokens, lanes[1]]
+            values = joined[base : base + tokens, lanes[2]]
+            for rb in range(2):
+                first = base + rb * half
+                span = (rb + 1) * half
+                probs = probs_low if rb else probs_top
+                queries = joined[first : first + half, lanes[0]]
+                for h in range(2):
+                    scores[h, :, :span] = dot_nt(queries * head_mask[h], keys[:span])
+                for h in range(2):
+                    for s in range(half // sub):
+                        value = scores[h, s * sub : (s + 1) * sub, :span] + masked_row[:, :span]
+                        allowed = (
+                            lax.broadcasted_iota(jnp.int32, (sub, half), 1)
+                            <= lax.broadcasted_iota(jnp.int32, (sub, half), 0) + s * sub
+                        )
+                        corner = jnp.where(allowed, value[:, rb * half :], MASKED)
+                        value = jnp.concatenate([value[:, :half], corner], axis=1) if rb else corner
+                        value = jnp.exp(value - jnp.max(value, axis=1, keepdims=True))
+                        value = value * (1.0 / jnp.sum(value, axis=1, keepdims=True))
+                        probs[m * 2 * pairs + hp * 2 + h, s * sub : (s + 1) * sub, :] = value.astype(bf)
+                total = dot_nn(probs[m * 2 * pairs + hp * 2], values[:span] * head_mask[0]) + dot_nn(
+                    probs[m * 2 * pairs + hp * 2 + 1], values[:span] * head_mask[1]
+                )
+                attended[first : first + half, pl.ds(pl.multiple_of(hp * 128, 128), 128)] = total.astype(bf)
+            return carry
+
+        lax.fori_loop(0, pairs, pair, 0)
+
+    attend(0)
+    gather_wait(1)
+    for step in range(2, bits):
+        gather_start(step)
+        if step < bits - 1:
+            gather_wait(step)
+    attend(1)
+
+    gelu_scale = math.sqrt(2.0 / math.pi)
+
+    def feed(c, carry):
+        at = pl.multiple_of(c * half, half)
+        values = embedded[pl.ds(at, half), :] + dot_nn(attended[pl.ds(at, half), :], out_low[...])
+        middle[pl.ds(at, half), :] = values
+        normed = (values * inverse_rms(values) * gain_two).astype(bf)
+        hidden_two[pl.ds(at, half), :] = normed
+        logits[:, :ff] = dot_nn(normed, up_low[...])
+
+        def bend(s, carry):
+            for part in range(2):
+                near = pl.multiple_of(s * 32 + part * 16, 16)
+                there = pl.multiple_of(at + s * 32 + part * 16, 16)
+                upward = logits[pl.ds(near, 16), :ff]
+                square = upward * upward
+                bent = jnp.tanh(gelu_scale * upward * (1.0 + 0.044715 * square))
+                active[pl.ds(there, 16), :] = (0.5 * upward * (1.0 + bent)).astype(bf)
+                slope[pl.ds(there, 16), :] = 0.5 * (1.0 + bent) + 0.5 * gelu_scale * upward * (1.0 - bent * bent) * (
+                    1.0 + 3.0 * 0.044715 * square
+                )
+            return carry
+
+        lax.fori_loop(0, half // 32, bend, 0)
+        values = values + dot_nn(active[pl.ds(at, half), :], down_low[...])
+        output[pl.ds(at, half), :] = values
+        query[pl.ds(at, half), :] = (values * inverse_rms(values) * gain_three).astype(bf)
+        return carry
+
+    lax.fori_loop(0, chunks, feed, 0)
+    gather_wait(bits - 1)
+    for k in range(1, row_count):
+        other = lax.rem(row + k, row_count)
+        pltpu.make_async_remote_copy(
+            bias.at[other], bias.at[other], send_b.at[k], recv_b.at[other],
+            device_id=(dp, other), device_id_type=MESH,
+        ).wait_recv()
+
+    block = 512
+    blocks = row_count * tokens // block
+    fine = 16
+
+    def loss_of(m):
+        length = lengths[m]
+
+        def one_half(rh, carry):
+            first = pl.multiple_of(m * tokens + rh * half, half)
+            queries = query[pl.ds(first, half), :]
+            highest[...] = jnp.full_like(highest, -3.0e38)
+
+            def score(j, carry):
+                at = pl.multiple_of(j * block, block)
+                value = dot_nt(queries, cand[m, pl.ds(at, block), :]) + bias[j, m : m + 1, :]
+                logits[:, pl.ds(at, block)] = value
+                top = jnp.maximum(
+                    jnp.maximum(value[:, :128], value[:, 128:256]), jnp.maximum(value[:, 256:384], value[:, 384:])
+                )
+                highest[...] = jnp.maximum(highest[...], top)
+                return carry
+
+            lax.fori_loop(0, blocks, score, 0)
+
+            def soften(s, carry):
+                near = pl.multiple_of(s * fine, fine)
+                place = rh * half + s * fine
+                own_at = pl.multiple_of(row * tokens + (place // 128) * 128, 128)
+                hit = lax.broadcasted_iota(jnp.int32, (fine, 128), 1) == lax.broadcasted_iota(
+                    jnp.int32, (fine, 128), 0
+                ) + lax.rem(place, 128)
+                valid = jnp.where(
+                    lax.broadcasted_iota(jnp.int32, (fine, 1), 0) + place < length, 1.0, 0.0
+                )
+                top = jnp.max(highest[pl.ds(near, fine), :], axis=1, keepdims=True)
+                own_logit = jnp.sum(
+                    jnp.where(hit, logits[pl.ds(near, fine), pl.ds(own_at, 128)], 0.0), axis=1, keepdims=True
+                )
+                total = jnp.zeros((fine, 128), jnp.float32)
+                for j in range(blocks):
+                    value = jnp.exp(logits[pl.ds(near, fine), j * block : (j + 1) * block] - top)
+                    logits[pl.ds(near, fine), j * block : (j + 1) * block] = value
+                    total = total + ((value[:, :128] + value[:, 128:256]) + (value[:, 256:384] + value[:, 384:]))
+                total = jnp.sum(total, axis=1, keepdims=True)
+                share = valid / total
+                there = pl.multiple_of(place, fine)
+                for j in range(blocks):
+                    grad_logits[pl.ds(there, fine), j * block : (j + 1) * block] = (
+                        logits[pl.ds(near, fine), j * block : (j + 1) * block] * share
+                    ).astype(bf)
+                own = logits[pl.ds(near, fine), pl.ds(own_at, 128)] * share - jnp.where(hit, valid, 0.0)
+                grad_logits[pl.ds(there, fine), pl.ds(own_at, 128)] = own.astype(bf)
+                return carry + valid * (top + jnp.log(total) - own_logit)
+
+            loss = lax.fori_loop(0, half // fine, soften, jnp.zeros((fine, 1), jnp.float32))
+            small[3:4, :] += jnp.broadcast_to(jnp.sum(loss, axis=0, keepdims=True), (1, width))
+            grad_query = dot_nn(grad_logits[pl.ds(pl.multiple_of(rh * half, half), half), :], cand[m])
+            grad, gain_part = rms_back(output[pl.ds(first, half), :], gain_three, grad_query)
+            output[pl.ds(first, half), :] = grad
+            small[2:3, :] += gain_part
+            return carry
+
+        lax.fori_loop(0, 2, one_half, 0)
+
+        def to_targets(j, carry):
+            at = pl.multiple_of(j * block, block)
+            cand_grads[m, pl.ds(at, block), :] = dot_tn(
+                grad_logits[:, pl.ds(at, block)], query[m * tokens : (m + 1) * tokens, :]
+            ).astype(bf)
+            return carry
+
+        lax.fori_loop(0, blocks, to_targets, 0)
+        scatter_start(m, 0)
+        small[4:5, :] += jnp.broadcast_to(
+            jnp.sum(jnp.where(column < length, 1.0, 0.0), axis=1, keepdims=True), (1, width)
+        )
+
+    small[...] = jnp.zeros_like(small)
+    loss_of(0)
+    loss_of(1)
+    scatter_wait(0, 0)
+    if bits > 1:
+        scatter_start(0, 1)
+
+    query[...] = output[...].astype(bf)
+    for k in range(ff // width):
+        grad_down[k * width : (k + 1) * width, :] = dot_tn(active[:, k * width : (k + 1) * width], query[...])
+    scatter_wait(1, 0)
+    if bits > 1:
+        scatter_start(1, 1)
+
+    def feed_back(c, carry):
+        at = pl.multiple_of(c * half, half)
+        branch = query[pl.ds(at, half), :]
+        for k in range(ff // width):
+            active[pl.ds(at, half), k * width : (k + 1) * width] = (
+                dot_nt(branch, down_low[k * width : (k + 1) * width, :])
+                * slope[pl.ds(at, half), k * width : (k + 1) * width]
+            ).astype(bf)
+        grad_hidden = dot_nt(active[pl.ds(at, half), :], up_low[...])
+        grad, gain_part = rms_back(middle[pl.ds(at, half), :], gain_two, grad_hidden)
+        small[1:2, :] += gain_part
+        grad = grad + output[pl.ds(at, half), :]
+        output[pl.ds(at, half), :] = grad
+        grad_low = grad.astype(bf)
+        grad_middle_low[pl.ds(at, half), :] = grad_low
+        grad_attended[pl.ds(at, half), :] = dot_nt(grad_low, out_low[...]).astype(bf)
+        return carry
+
+    lax.fori_loop(0, chunks, feed_back, 0)
+    grad_up[...] = dot_tn(hidden_two[...], active[...])
+    grad_out[...] = dot_tn(attended[...], grad_middle_low[...])
+    for step in range(1, bits - 1):
+        for m in range(micro):
+            scatter_wait(m, step)
+            scatter_start(m, step + 1)
+
+    def attend_back(m):
+        base = m * tokens
+
+        def pair(hp, carry):
+            lanes = [pl.ds(pl.multiple_of(k * inner + hp * 128, 128), 128) for k in range(3)]
+            here = pl.ds(pl.multiple_of(hp * 128, 128), 128)
+            keys = joined[base : base + tokens, lanes[1]]
+            values = joined[base : base + tokens, lanes[2]]
+            for rb in (1, 0):
+                first = base + rb * half
+                span = (rb + 1) * half
+                probs = probs_low if rb else probs_top
+                queries = joined[first : first + half, lanes[0]]
+                upper = grad_attended[first : first + half, here]
+                for h in range(2):
+                    scores[h, :, :span] = dot_nt(upper * head_mask[h], values[:span])
+                for h in range(2):
+                    for s in range(half // sub):
+                        chance = probs[m * 2 * pairs + hp * 2 + h, s * sub : (s + 1) * sub, :].astype(jnp.float32)
+                        grad = scores[h, s * sub : (s + 1) * sub, :span]
+                        inner_sum = jnp.sum(chance * grad, axis=1, keepdims=True)
+                        grad_scores[h, s * sub : (s + 1) * sub, :span] = (chance * (grad - inner_sum)).astype(bf)
+                total_q = dot_nn(grad_scores[0, :, :span], keys[:span] * head_mask[0]) + dot_nn(
+                    grad_scores[1, :, :span], keys[:span] * head_mask[1]
+                )
+                total_k = dot_tn(grad_scores[0, :, :span], queries * head_mask[0]) + dot_tn(
+                    grad_scores[1, :, :span], queries * head_mask[1]
+                )
+                total_v = dot_tn(probs[m * 2 * pairs + hp * 2], upper * head_mask[0]) + dot_tn(
+                    probs[m * 2 * pairs + hp * 2 + 1], upper * head_mask[1]
+                )
+                joined[first : first + half, lanes[0]] = (total_q * 0.125).astype(bf)
+                if rb:
+                    part_k[...] = total_k
+                    part_v[...] = total_v
+                else:
+                    part_k[:half, :] += total_k
+                    part_v[:half, :] += total_v
+            joined[base : base + tokens, lanes[1]] = part_k[...].astype(bf)
+            joined[base : base + tokens, lanes[2]] = part_v[...].astype(bf)
+            return carry
+
+        lax.fori_loop(0, pairs, pair, 0)
+
+    attend_back(0)
+    attend_back(1)
+
+    def project_back(c, carry):
+        at = pl.multiple_of(c * half, half)
+        near = pl.multiple_of(lax.rem(c, 2) * half, half)
+        grad_hidden = dot_nt(joined[pl.ds(at, half), :], qkv_low[...])
+        grad, gain_part = rms_back(embedded[pl.ds(at, half), :], gain_one, grad_hidden)
+        small[0:1, :] += gain_part
+        grad = grad + output[pl.ds(at, half), :]
+        grad_positions[pl.ds(near, half), :] += grad
+        row_grads[pl.ds(at, half), :] = (scaling * grad).astype(bf)
+        return carry
+
+    grad_positions[...] = jnp.zeros_like(grad_positions)
+    lax.fori_loop(0, chunks, project_back, 0)
+    for k in range(3 * inner // 512):
+        grad_qkv[:, k * 512 : (k + 1) * 512] = dot_tn(hidden_one[...], joined[:, k * 512 : (k + 1) * 512])
+    for m in range(micro):
+        if bits > 1:
+            scatter_wait(m, bits - 1)
+    for copy in pending:
+        copy.wait_send()
+
+
+def layer(row_count, lengths, items, targets, correction, matrices, positions, gains):
+    qkv, out, up, down = matrices
+    tokens, width = positions.shape
+    half = tokens // 2
+    inner, ff = out.shape[0], up.shape[1]
+    events = 2 * tokens
+    group = row_count * tokens
+    bf, f32 = jnp.bfloat16, jnp.float32
+    pairs = inner // 128
+    bits = row_count.bit_length() - 1
+    hops = 2 * (row_count - 1)
+    sems = lambda count: pltpu.SemaphoreType.DMA((count,))
+    hbm = pl.BlockSpec(memory_space=pl.ANY)
+    return pl.pallas_call(
+        functools.partial(layer_kernel, row_count),
+        out_shape=(
+            jax.ShapeDtypeStruct(qkv.shape, f32),
+            jax.ShapeDtypeStruct(out.shape, f32),
+            jax.ShapeDtypeStruct(up.shape, f32),
+            jax.ShapeDtypeStruct(down.shape, f32),
+            jax.ShapeDtypeStruct(positions.shape, f32),
+            jax.ShapeDtypeStruct((2 * events, width), bf),
+            jax.ShapeDtypeStruct((8, width), f32),
+        ),
+        in_specs=[pl.BlockSpec(memory_space=pltpu.SMEM), VMEM, VMEM, VMEM, hbm, hbm, hbm, hbm, VMEM, VMEM],
+        out_specs=(VMEM,) * 7,
+        scratch_shapes=[
+            pltpu.VMEM(qkv.shape, bf),
+            pltpu.VMEM(out.shape, bf),
+            pltpu.VMEM(up.shape, bf),
+            pltpu.VMEM(down.shape, bf),
+            pltpu.VMEM((events, width), f32),
+            pltpu.VMEM((events, width), bf),
+            pltpu.VMEM((events, 3 * inner), bf),
+            pltpu.VMEM((4 * pairs, half, half), bf),
+            pltpu.VMEM((4 * pairs, half, tokens), bf),
+            pltpu.VMEM((events, inner), bf),
+            pltpu.VMEM((events, width), f32),
+            pltpu.VMEM((events, width), bf),
+            pltpu.VMEM((events, ff), f32),
+            pltpu.VMEM((events, ff), bf),
+            pltpu.VMEM((events, width), f32),
+            pltpu.VMEM((events, width), bf),
+            pltpu.VMEM((2, group, width), bf),
+            pltpu.VMEM((row_count, 2, tokens), f32),
+            pltpu.VMEM((2, group, width), bf),
+            pltpu.VMEM((hops, tokens, width), bf),
+            pltpu.VMEM((half, group), f32),
+            pltpu.VMEM((tokens, group), bf),
+            pltpu.VMEM((half, 128), f32),
+            pltpu.VMEM((2, half, tokens), f32),
+            pltpu.VMEM((2, half, tokens), bf),
+            pltpu.VMEM((events, width), bf),
+            pltpu.VMEM((events, inner), bf),
+            pltpu.VMEM((tokens, 128), f32),
+            pltpu.VMEM((tokens, 128), f32),
+            sems(2 + (inner + ff) // width),
+            sems(row_count),
+            sems(row_count),
+            sems(hops),
+            sems(hops),
+            sems(hops),
+            sems(hops),
+        ],
+        name="layer",
+        compiler_params=pltpu.CompilerParams(collective_id=5, has_side_effects=True, vmem_limit_bytes=60 * 2**20),
+    )(lengths, items, targets, correction, qkv, out, up, down, positions, gains)
+
+
 def small_kernel(dp_count, row_count, part, summed, by_row, by_dp, send_sem, recv_sem):
     dp = lax.axis_index("dp")
     row = lax.axis_index("rows")
@@ -711,6 +1249,71 @@
         name="small_sum",
         compiler_params=pltpu.CompilerParams(collective_id=4, has_side_effects=True),
     )(part)
+
+
+def grouped_layer(fetched, valid_pos, lengths, correction, weights, positions, gains):
+    qkv_weight, out_weight, up_weight, down_weight = weights
+    micro, tokens = valid_pos.shape
+    histories = lengths.shape[1]
+    length, width = positions.shape
+    matrices = (rounded(qkv_weight), rounded(out_weight), rounded(up_weight), rounded(down_weight))
+    scaling = math.sqrt(width)
+    offset = lax.axis_index("rows") * tokens
+    running = [
+        jnp.zeros_like(qkv_weight),
+        jnp.zeros_like(out_weight),
+        jnp.zeros_like(up_weight),
+        jnp.zeros_like(down_weight),
+    ]
+    grad_positions = jnp.zeros_like(positions)
+    grad_gains = jnp.zeros_like(gains)
+    loss_local = jnp.zeros((), jnp.float32)
+    embed_grads = []
+    target_grads = []
+    for micro_index in range(micro):
+        lengths_here = lengths[micro_index]
+        valid_here = valid_pos[micro_index].astype(jnp.float32)
+        embedded = scaling * fetched[0, micro_index].astype(jnp.float32) + jnp.tile(
+            positions, (histories, 1)
+        )
+        output, saved_state = layer_forward(embedded, lengths_here, matrices, gains, HEADS)
+        normed_three, back_three = jax.vjp(rms_norm, output, gains[2])
+        query_low = rounded(normed_three)
+        bias_low = jnp.where(
+            valid_pos[micro_index],
+            rounded(-correction[micro_index].reshape(-1)),
+            jnp.asarray(MASKED, jnp.bfloat16),
+        )
+        candidates, cand_bias = (
+            lax.all_gather(fetched[1, micro_index], "rows", axis=0, tiled=True),
+            lax.all_gather(bias_low, "rows", axis=0, tiled=True),
+        )
+        loss_part, grad_logits, log_total = candidate_loss(
+            query_low, candidates, cand_bias, valid_here, offset
+        )
+        loss_local = loss_local + loss_part
+        grad_output, gain_three = back_three(matmul(grad_logits, candidates))
+        target_grads.append(
+            lax.psum_scatter(
+                inner_rows(grad_logits, query_low).astype(jnp.bfloat16),
+                "rows",
+                scatter_dimension=0,
+                tiled=True,
+            ).astype(jnp.float32)
+        )
+        grad_embedded, grad_layer, gain_pair = layer_backward(
+            grad_output, saved_state, lengths_here, matrices, HEADS
+        )
+        for which_one in range(4):
+            running[which_one] = running[which_one] + grad_layer[which_one]
+        grad_positions = grad_positions + jnp.sum(
+            grad_embedded.reshape(histories, length, width), axis=0
+        )
+        grad_gains = grad_gains + jnp.stack([gain_pair[0], gain_pair[1], gain_three])
+        embed_grads.append(scaling * grad_embedded)
+    target_part = jnp.stack(target_grads)
+    row_grads = jnp.concatenate([jnp.stack(embed_grads), target_part]).reshape(-1, width)
+    return running, grad_positions, rounded(row_grads), grad_gains, loss_local
 
 
 def local(
@@ -760,63 +1363,32 @@
     )
     received = received[:, 0, :capacity].reshape(1, devices * capacity)
     fetched = fetched.reshape(2, micro, tokens, width)
-    matrices = (rounded(qkv_weight), rounded(out_weight), rounded(up_weight), rounded(down_weight))
-    scaling = math.sqrt(width)
-    offset = lax.axis_index("rows") * tokens
-    running = [
-        jnp.zeros_like(qkv_weight),
-        jnp.zeros_like(out_weight),
-        jnp.zeros_like(up_weight),
-        jnp.zeros_like(down_weight),
-    ]
-    grad_positions = jnp.zeros_like(positions)
-    grad_gains = jnp.zeros_like(gains)
-    loss_local = jnp.zeros((), jnp.float32)
-    embed_grads = []
-    target_grads = []
-    for micro_index in range(micro):
-        lengths_here = lengths[micro_index]
-        valid_here = valid_pos[micro_index].astype(jnp.float32)
-        embedded = scaling * fetched[0, micro_index].astype(jnp.float32) + jnp.tile(
-            positions, (histories, 1)
-        )
-        output, saved_state = layer_forward(embedded, lengths_here, matrices, gains, HEADS)
-        normed_three, back_three = jax.vjp(rms_norm, output, gains[2])
-        query_low = rounded(normed_three)
-        bias_low = jnp.where(
-            valid_pos[micro_index],
-            rounded(-correction[micro_index].reshape(-1)),
-            jnp.asarray(MASKED, jnp.bfloat16),
-        )
-        candidates, cand_bias = (
-            lax.all_gather(fetched[1, micro_index], "rows", axis=0, tiled=True),
-            lax.all_gather(bias_low, "rows", axis=0, tiled=True),
-        )
-        loss_part, grad_logits, log_total = candidate_loss(
-            query_low, candidates, cand_bias, valid_here, offset
-        )
-        loss_local = loss_local + loss_part
-        grad_output, gain_three = back_three(matmul(grad_logits, candidates))
-        target_grads.append(
-            lax.psum_scatter(
-                inner_rows(grad_logits, query_low).astype(jnp.bfloat16),
-                "rows",
-                scatter_dimension=0,
-                tiled=True,
-            ).astype(jnp.float32)
-        )
-        grad_embedded, grad_layer, gain_pair = layer_backward(
-            grad_output, saved_state, lengths_here, matrices, HEADS
-        )
-        for which_one in range(4):
-            running[which_one] = running[which_one] + grad_layer[which_one]
-        grad_positions = grad_positions + jnp.sum(
-            grad_embedded.reshape(histories, length, width), axis=0
-        )
-        grad_gains = grad_gains + jnp.stack([gain_pair[0], gain_pair[1], gain_three])
-        embed_grads.append(scaling * grad_embedded)
-    target_part = jnp.stack(target_grads)
-    row_grads = jnp.concatenate([jnp.stack(embed_grads), target_part]).reshape(requests, width)
+    fits = histories == 1 and micro == 2 and row_count * tokens <= 4096
+    if fits:
+        outs = layer(
+            row_count,
+            lengths.reshape(micro),
+            fetched[0].reshape(micro * tokens, width),
+            fetched[1].reshape(micro * tokens, width),
+            correction.reshape(micro, tokens),
+            (qkv_weight, out_weight, up_weight, down_weight),
+            positions,
+            gains,
+        )
+        running = outs[:4]
+        grad_positions, row_grads, small = outs[4:]
+        grad_gains, loss_local, count_local = small[:3], small[3, 0], small[4, 0]
+    else:
+        running, grad_positions, row_grads, grad_gains, loss_local = grouped_layer(
+            fetched,
+            valid_pos,
+            lengths,
+            correction,
+            (qkv_weight, out_weight, up_weight, down_weight),
+            positions,
+            gains,
+        )
+        count_local = jnp.sum(valid_pos.astype(jnp.float32))
     incoming, gathered, square = tail_exchange(
         dp_count,
         row_count,
@@ -826,14 +1398,14 @@
         running[2],
         running[3],
         grad_positions,
-        rounded(row_grads),
+        row_grads,
         slots,
     )
     table_grad, table_square = table_gradient(
         rows_here, received, incoming.reshape(devices * capacity, width)
     )
     own_square = jnp.sum(table_square[0] + square[0])
-    scalars = jnp.stack([loss_local, jnp.sum(valid_pos.astype(jnp.float32)), own_square])
+    scalars = jnp.stack([loss_local, count_local, own_square])
     part = jnp.concatenate(
         [grad_gains.reshape(-1), jnp.pad(scalars, (0, 1024 - grad_gains.size - 3))]
     ).reshape(8, 128)

time: 472 us -> 346 us (0.73); the launches traced: 464 us -> 346 us
  Pallas kernels: 170 us -> 292 us
  matrix products: 84.5 us -> 0 us
  waiting for transfers between devices: 50.3 us -> 0 us
  other arithmetic: 80.3 us -> 34.7 us
  blocking collectives: 25.7 us -> 0 us
  local copies, waits for them, and re-layouts: 32.9 us -> 15.6 us
  between operations: 19.1 us -> 3.46 us
    pallas_call x0 -> x1, Pallas kernels: none -> 110 us  [layer(): pl.pallas_call(functools.partial(layer_kernel, row_count), out_shape=(jax...]
    dot_general x42 -> x0, matrix products: 84.5 us -> none  [the longest x10 18.7 us: inner_cols(): lax.dot_general(first_op, second_op, (((1,), (1,)), ((), ())), preferred_...]
    reduce_scatter x2 -> x0, waiting for transfers between devices: 49.5 us -> none  [local(): lax.psum_scatter(inner_rows(grad_logits, query_low).astype(jnp.bfloat16),...]
    all_gather x2 -> x0, blocking collectives: 25.7 us -> none  [local(): lax.all_gather(bias_low, 'rows', axis=0, tiled=True)]
    convert_element_type x12 -> x0, other arithmetic: 16.1 us -> none  [the longest x8 14.9 us: rounded(): return values.astype(jnp.bfloat16)]
    reduce_sum x7 -> x0, other arithmetic: 15 us -> none  [the longest x2 6.98 us: attention_forward(): jnp.sum(jnp.exp(scores - highest), axis=-1, keepdims=True)]
    unnamed x219 -> x56, local copies, waits for them, and re-layouts: 22.4 us -> 10.4 us
    pallas_call x1, Pallas kernels: 83.7 us -> 93.9 us  [tail_exchange(): pl.pallas_call(functools.partial(tail_kernel, dp_count, row_count, padded...]
  transfers between devices with their start and end apart: 4 -> 0, of which waited for: 2 -> 0; matrix products, arithmetic and copies ran while one was open for 18% -> 0% of each run, Pallas kernels for 0% -> 0%
where the time goes in v3:
time: 346 us
  Pallas kernels  292 us (84%)
  other arithmetic  34.7 us (10%)
  local copies, waits for them, and re-layouts  15.6 us (5%)
  between operations  3.46 us (1%)
    pallas_call x1, Pallas kernels, layer(): pl.pallas_call(functools.partial(layer_kernel, row_count), out_shape=(jax...  110 us
    pallas_call x1, Pallas kernels, tail_exchange(): pl.pallas_call(functools.partial(tail_kernel, dp_count, row_count, padded...  93.9 us
    pallas_call x1, Pallas kernels, lookup(): pl.pallas_call(functools.partial(lookup_kernel, dp_count, row_count, capa...  56.4 us
    sub x6, other arithmetic, adam_step(): return (weight - rate * (stepped + decay * weight), first_new, second_new)  27.7 us
    pallas_call x1, Pallas kernels, table_gradient(): pl.pallas_call(table_kernel, grid=(rows_here // tile,), out_shape=(jax.Sh...  17.5 us
    pallas_call x1, Pallas kernels, small_sum(): pl.pallas_call(functools.partial(small_kernel, dp_count, row_count), out_...  14.4 us
    unnamed x56, local copies, waits for them, and re-layouts  10.4 us

profile of v3, /device:TPU:0, one launch (start us, length us, event | category | flops | bytes accessed | tf_op | source)
XLA Modules:
  0.0 345.7 jit_solution(10302116006196998672)
XLA Ops:
  0.7 0.7 iota_compare_fusion
  1.4 0.7 fusion.6
  2.1 1.3 copy.53
  3.5 56.4 %lookup.1 = (bf16[2048,256]{1,0:T(8,128)(2,1)}, f32[8,256]{1,0:T(8,128)}, s32[32,1,128]{2,1,0:T(1,128)}) custom-call(s32[2048,1]{1,0:T(8,128)} %bitcast.25, s32[1568,128]{1,0:T(8,128)} %bitcast.26, f32[6272,256]{1,0:T(8,128)} %table_hbm.1), custom_call_target="tpu_custom_call" | custom-call | tf_op jit(solution)/shard_map/lookup/pallas_call | solution.py:594
  59.9 0.8 slice_reduce_fusion
  60.8 2.2 fusion.16
  63.0 0.6 copy.55
  63.6 109.7 %layer.1 = (f32[256,1536]{1,0:T(8,128)}, f32[512,256]{1,0:T(8,128)}, f32[256,1024]{1,0:T(8,128)}, f32[1024,256]{1,0:T(8,128)}, f32[512,256]{1,0:T(8,128)}, /*index=5*/bf16[2048,256]{1,0:T(8,128)(2,1)}, f32[8,256]{1,0:T(8,128)}) custom-call(s32[2]{0:T(128)} %bitcast.33, bf16[1024,256]{1,0:T(8,128)(2,1)} %get-tuple-element.83.items, ...), custom_call_target="tpu_custom_call" | custom-call | tf_op jit(solution)/shard_map/layer/pallas_call | solution.py:1145
  173.4 93.9 %tail_exchange.1 = (bf16[32,112,256]{2,1,0:T(8,128)(2,1)}, bf16[4608,256]{1,0:T(8,128)(2,1)}, f32[8,256]{1,0:T(8,128)}) custom-call(f32[256,1536]{1,0:T(8,128)} %get-tuple-element.42.qkv, f32[512,256]{1,0:T(8,128)} %get-tuple-element.43.out, f32[256,1024]{1,0:T(8,128)} %get-tuple-element.44.up, f32[1024,256]{1,0:T(8,128)} %get-tuple-element.45.down, ...), custom_call_target="tpu_custom_call" | custom-call | tf_op jit(solution)/shard_map/tail_exchange/pallas_call | solution.py:423
  267.3 1.5 copy-done.1
  268.8 17.5 %table_gradient.1 = (f32[6272,256]{1,0:T(8,128)S(1)}, f32[8,256]{1,0:T(8,128)S(1)}) custom-call(s32[1,3584]{1,0:T(1,128)S(1)} %reshape_squeeze.2.received, bf16[3584,256]{1,0:T(8,128)(2,1)S(1)} %bitcast.24), custom_call_target="tpu_custom_call" | custom-call | tf_op jit(solution)/shard_map/table_gradient/pallas_call | solution.py:643
  286.3 2.7 copy-done
  289.0 1.3 add_reduce_fusion
  290.3 0.5 fusion.17
  290.9 2.0 select_maximum_fusion
  292.9 0.6 maximum_bitcast_fusion.part
  293.5 14.4 %small_sum.1 = f32[8,128]{1,0:T(8,128)} custom-call(f32[8,128]{1,0:T(8,128)} %maximum_bitcast_fusion.part), custom_call_target="tpu_custom_call" | custom-call | tf_op jit(solution)/shard_map/small_sum/pallas_call | solution.py:1238
  307.9 1.4 fusion.18
  309.3 1.3 multiply_reduce_fusion
  312.0 17.4 %multiply_subtract_fusion = (f32[6272,256]{1,0:T(8,128)}, f32[6272,256]{1,0:T(8,128)}, f32[6272,256]{1,0:T(8,128)}) fusion(f32[6272,256]{1,0:T(8,128)} %table_hbm.1, f32[6272,256]{1,0:T(8,128)} %copy-done, f32[]{:T(128)S(6)} %div.96, f32[6272,256]{1,0:T(8,128)} %param.38, f32[6272,256]{1,0:T(8,128)} %param.45), kind=kLoop, calls=%fused_computation.2 | loop fusion | flops 25690112 | bytes 44957700 | tf_op jit(solution)/shard_map/sub | solution.py:223
  329.4 0.4 convert_element_type.5
  330.0 0.8 copy-done.8
  330.8 0.5 copy-done.9
  331.2 0.6 copy-done.2
  331.9 3.1 multiply_subtract_fusion.1
  335.0 2.2 multiply_subtract_fusion.4
  337.3 1.1 copy-done.4
  338.4 0.3 copy-done.10
  338.7 2.2 multiply_subtract_fusion.3
  340.9 0.8 copy-done.13
  341.7 2.2 multiply_subtract_fusion.2
  343.9 0.6 add_subtract_fusion
  (54 shorter events, 0.5 us)
Async XLA Ops:
  59.9 3.1 copy-start.22
  173.3 117.0 %copy-start.23 = (f32[8,256]{1,0:T(8,128)S(1)}, f32[8,256]{1,0:T(8,128)}, u32[]{:S(2)}) copy-start(f32[8,256]{1,0:T(8,128)} %get-tuple-element.40) | copy-start | bytes 24580
  267.3 1.5 copy-start.1
  286.3 2.7 copy-start
  312.0 17.4 %copy-start.3 = (bf16[4608,256]{1,0:T(8,128)(2,1)S(1)}, bf16[4608,256]{1,0:T(8,128)(2,1)}, u32[]{:S(2)}) copy-start(bf16[4608,256]{1,0:T(8,128)(2,1)} %get-tuple-element.53) | copy-start | bytes 7077892
  329.4 1.4 copy-start.8
  329.4 1.9 copy-start.9
  329.8 2.1 copy-start.2
  331.8 3.1 copy-start.6
  331.8 3.1 copy-start.7
  331.8 3.1 copy-start.14
  331.8 3.1 copy-start.15
  331.8 3.1 copy-start.16
  331.8 3.1 copy-start.17
  334.9 2.3 copy-start.11
  337.2 1.2 copy-start.4
  337.2 1.5 copy-start.10
  338.7 2.2 copy-start.5
  338.7 2.2 copy-start.12
  338.7 3.0 copy-start.13
  341.7 2.2 copy-start.18
  341.7 2.2 copy-start.19
  341.7 2.2 copy-start.20
  341.7 2.2 copy-start.21

commit v4 on v3

--- a/solution.py
+++ b/solution.py
@@ -263,12 +263,12 @@
     def a2a_send(k):
         other, where = place(k)
         return pltpu.make_async_remote_copy(
-            outgoing.at[other], incoming.at[me], send_a.at[k], recv_a.at[me], device_id=where, device_id_type=MESH)
+            outgoing.at[other], incoming.at[k], send_a.at[k], recv_a.at[k], device_id=where, device_id_type=MESH)
 
     def a2a_recv(k):
         other, where = place(k)
         return pltpu.make_async_remote_copy(
-            outgoing.at[other], incoming.at[other], send_a.at[k], recv_a.at[other], device_id=where, device_id_type=MESH)
+            outgoing.at[other], incoming.at[k], send_a.at[k], recv_a.at[k], device_id=where, device_id_type=MESH)
 
     def partner(bit):
         step = 1 << bit
@@ -300,7 +300,7 @@
         return carry
 
     lax.fori_loop(1, devices, send_rows, 0)
-    incoming[me] = arrange(me)
+    incoming[0] = arrange(me)
     first.wait_recv()
     base = mine * half
     pending = [first]
@@ -547,9 +547,15 @@
     stage[...] = jnp.zeros_like(stage)
     load_table.wait()
     lax.fori_loop(1, devices, lambda k, c: (query(k, True).wait_recv(), c)[1], 0)
-    received[...] = jnp.clip(got[...], 0, rows_here - 1)
-    to_scalars = pltpu.make_async_copy(received, asked_here, local_sem)
+    got[...] = jnp.clip(got[...], 0, rows_here - 1)
+    to_scalars = pltpu.make_async_copy(got, asked_here, local_sem)
     to_scalars.start()
+
+    def by_distance(k, carry):
+        received[k] = got[lax.rem(me + devices - k, devices)]
+        return carry
+
+    lax.fori_loop(0, devices, by_distance, 0)
     to_scalars.wait()
 
     def gather(source):
@@ -702,12 +708,15 @@
     return index
 
 
-def layer_kernel(row_count, lengths, items, targets, correction, qkv_hbm, out_hbm, up_hbm, down_hbm, positions, gains,
-                 grad_qkv, grad_out, grad_up, grad_down, grad_positions, row_grads, small,
+def layer_kernel(dp_count, row_count, capacity, rows_here, lengths, items, targets, correction, qkv_hbm, out_hbm,
+                 up_hbm, down_hbm, positions, gains, slots, received,
+                 table_grads, gathered, summed,
                  qkv_low, out_low, up_low, down_low, embedded, hidden_one, joined, probs_top, probs_low, attended,
                  middle, hidden_two, slope, active, output, query, cand, bias, cand_grads, landing, logits,
-                 grad_logits, highest, scores, grad_scores, grad_middle_low, grad_attended, part_k, part_v,
-                 load_sem, send_b, recv_b, send_g, recv_g, send_s, recv_s):
+                 grad_logits, highest, row_grads, small, acc, got_sums, incoming, by_row, by_dp, row_small, part_k, part_v,
+                 load_sem, send_b, recv_b, send_g, recv_g, send_s, recv_s, send_r, recv_r, send_a, recv_a,
+                 send_n, recv_n, store_sem):
+    devices = dp_count * row_count
     micro = 2
     tokens = positions.shape[0]
     half = tokens // 2
@@ -718,10 +727,13 @@
     row = lax.axis_index("rows")
     bf = jnp.bfloat16
     barrier = pltpu.get_barrier_semaphore()
-    for k in range(1, row_count):
-        pl.semaphore_signal(
-            barrier, inc=1, device_id=(dp, lax.rem(row + k, row_count)), device_id_type=MESH
-        )
+
+    def greet(k, carry):
+        other, where = other_device(k, dp_count, row_count)
+        pl.semaphore_signal(barrier, inc=1, device_id=where, device_id_type=MESH)
+        return carry
+
+    lax.fori_loop(1, devices, greet, 0)
     ff = up_low.shape[1]
     loads = [
         (qkv_hbm, 0, 0, 3 * inner, qkv_low),
@@ -746,10 +758,11 @@
             column < lengths[m], (-correction[m : m + 1, :]).astype(bf).astype(jnp.float32), MASKED
         )
         bias[row, m : m + 1, :] = own_bias.astype(bf).astype(jnp.float32)
-        cand[m, pl.ds(pl.multiple_of(row * tokens, tokens), tokens), :] = targets[m * tokens : (m + 1) * tokens, :]
-    pl.semaphore_wait(barrier, row_count - 1)
+        cand[pl.ds(pl.multiple_of((m * row_count + row) * tokens, tokens), tokens), :] = targets[m * tokens : (m + 1) * tokens, :]
+    pl.semaphore_wait(barrier, devices - 1)
 
     pending = []
+    gathers = []
     for k in range(1, row_count):
         copy = pltpu.make_async_remote_copy(
             bias.at[row], bias.at[row], send_b.at[k], recv_b.at[row],
@@ -759,7 +772,7 @@
         pending.append(copy)
 
     orders = [list(range(1, bits)) + [0], list(range(bits - 1, 0, -1)) + [0]]
-    block_of = lambda ref, m, owner: ref.at[m, pl.ds(pl.multiple_of(owner * tokens, tokens), tokens)]
+    block_of = lambda ref, m, owner: ref.at[pl.ds(pl.multiple_of((m * row_count + owner) * tokens, tokens), tokens)]
     gather_steps = []
     count = 0
     for step in range(bits):
@@ -778,7 +791,7 @@
                 device_id=(dp, flip(row, (bit,))), device_id_type=MESH,
             )
             copy.start()
-            pending.append(copy)
+            gathers.append(copy)
 
     def gather_wait(step):
         for m, bit, mask, sem in gather_steps[step]:
@@ -818,17 +831,17 @@
                 block_of(cand_grads, m, flip(row, mask)), landing.at[sem], send_s.at[sem], recv_s.at[sem],
                 device_id=(dp, there), device_id_type=MESH,
             ).wait_recv()
-            base = flip(row, mask) * tokens
+            base = (m * row_count + flip(row, mask)) * tokens
             last = step == bits - 1
 
             def add(c, carry):
                 at = pl.multiple_of(base + c * 64, 64)
                 near = pl.multiple_of(c * 64, 64)
-                total = cand_grads[m, pl.ds(at, 64), :].astype(jnp.float32) + landing[sem, pl.ds(near, 64), :].astype(jnp.float32)
+                total = cand_grads[pl.ds(at, 64), :].astype(jnp.float32) + landing[sem, pl.ds(near, 64), :].astype(jnp.float32)
                 if last:
                     row_grads[pl.ds(pl.multiple_of((micro + m) * tokens + c * 64, 64), 64), :] = total.astype(bf)
                 else:
-                    cand_grads[m, pl.ds(at, 64), :] = total.astype(bf)
+                    cand_grads[pl.ds(at, 64), :] = total.astype(bf)
                 return carry
 
             lax.fori_loop(0, tokens // 64, add, 0)
@@ -876,10 +889,10 @@
                 probs = probs_low if rb else probs_top
                 queries = joined[first : first + half, lanes[0]]
                 for h in range(2):
-                    scores[h, :, :span] = dot_nt(queries * head_mask[h], keys[:span])
+                    logits[:, h * tokens : h * tokens + span] = dot_nt(queries * head_mask[h], keys[:span])
                 for h in range(2):
                     for s in range(half // sub):
-                        value = scores[h, s * sub : (s + 1) * sub, :span] + masked_row[:, :span]
+                        value = logits[s * sub : (s + 1) * sub, h * tokens : h * tokens + span] + masked_row[:, :span]
                         allowed = (
                             lax.broadcasted_iota(jnp.int32, (sub, half), 1)
                             <= lax.broadcasted_iota(jnp.int32, (sub, half), 0) + s * sub
@@ -957,7 +970,7 @@
 
             def score(j, carry):
                 at = pl.multiple_of(j * block, block)
-                value = dot_nt(queries, cand[m, pl.ds(at, block), :]) + bias[j, m : m + 1, :]
+                value = dot_nt(queries, cand[pl.ds(pl.multiple_of(m * row_count * tokens + at, block), block), :]) + bias[j, m : m + 1, :]
                 logits[:, pl.ds(at, block)] = value
                 top = jnp.maximum(
                     jnp.maximum(value[:, :128], value[:, 128:256]), jnp.maximum(value[:, 256:384], value[:, 384:])
@@ -999,7 +1012,7 @@
 
             loss = lax.fori_loop(0, half // fine, soften, jnp.zeros((fine, 1), jnp.float32))
             small[3:4, :] += jnp.broadcast_to(jnp.sum(loss, axis=0, keepdims=True), (1, width))
-            grad_query = dot_nn(grad_logits[pl.ds(pl.multiple_of(rh * half, half), half), :], cand[m])
+            grad_query = dot_nn(grad_logits[pl.ds(pl.multiple_of(rh * half, half), half), :], cand[m * row_count * tokens : (m + 1) * row_count * tokens, :])
             grad, gain_part = rms_back(output[pl.ds(first, half), :], gain_three, grad_query)
             output[pl.ds(first, half), :] = grad
             small[2:3, :] += gain_part
@@ -1009,7 +1022,7 @@
 
         def to_targets(j, carry):
             at = pl.multiple_of(j * block, block)
-            cand_grads[m, pl.ds(at, block), :] = dot_tn(
+            cand_grads[pl.ds(pl.multiple_of(m * row_count * tokens + at, block), block), :] = dot_tn(
                 grad_logits[:, pl.ds(at, block)], query[m * tokens : (m + 1) * tokens, :]
             ).astype(bf)
             return carry
@@ -1027,15 +1040,137 @@
     if bits > 1:
         scatter_start(0, 1)
 
+    def partner(bit):
+        mine = lax.rem(row // (1 << bit), 2)
+        return mine, (dp, flip(row, (bit,)))
+
+    low = cand
+    squared = {}
+    al = lambda value: pl.multiple_of(value, 16)
+
+    def summing(first, rows, sem, land):
+        half_rows = rows // 2
+        units = rows // (16 * devices)
+        sizes = [((units + 1) // 2) * 8 * devices, (units // 2) * 8 * devices]
+        parts = [p for p in range(2) if sizes[p]]
+        part_orders = [list(range(1, bits)), list(range(bits - 1, 0, -1))]
+
+        def lower(at, size):
+            low[pl.ds(al(at), size), :] = acc[pl.ds(al(at), size), :].astype(bf)
+
+        def add(at, size, off):
+            acc[pl.ds(al(at), size), :] += got_sums[pl.ds(off, size), :].astype(jnp.float32)
+
+        def send(source, at, size, target, sem, where):
+            copy = pltpu.make_async_remote_copy(
+                source.at[pl.ds(al(at), size)], target, send_r.at[sem], recv_r.at[sem],
+                device_id=where, device_id_type=MESH,
+            )
+            copy.start()
+            pending.append(copy)
+            return copy
+
+        def expect(at, size, sem, where):
+            pltpu.make_async_remote_copy(
+                gathered.at[pl.ds(al(at), size)], gathered.at[pl.ds(al(at), size)], send_r.at[sem], recv_r.at[sem],
+                device_id=where, device_id_type=MESH,
+            ).wait_recv()
+
+        mine, where = partner(0)
+        give = first + (1 - mine) * half_rows
+        lower(give, half_rows)
+        copy = send(low, give, half_rows, got_sums.at[pl.ds(land, half_rows)], sem, where)
+        yield
+        copy.wait_recv()
+        base = first + mine * half_rows
+        add(base, half_rows, land)
+        sem, land = sem + 1, land + half_rows
+        starts = [base, base + sizes[0]]
+        for step in range(bits - 1):
+            moved = []
+            for p in parts:
+                mine, where = partner(part_orders[p][step])
+                size = sizes[p] // 2
+                give = starts[p] + (1 - mine) * size
+                lower(give, size)
+                copy = send(low, give, size, got_sums.at[pl.ds(land, size)], sem, where)
+                starts[p], sizes[p] = starts[p] + mine * size, size
+                moved.append((p, copy, land))
+                sem, land = sem + 1, land + size
+            yield
+            for p, copy, at in moved:
+                copy.wait_recv()
+                add(starts[p], sizes[p], at)
+        moved = []
+        finals = {}
+        for p in parts:
+            size = sizes[p] // dp_count
+            finals[p] = starts[p] + dp * size
+            for k in range(1, dp_count):
+                other = lax.rem(dp + k, dp_count)
+                give = starts[p] + other * size
+                lower(give, size)
+                copy = send(low, give, size, got_sums.at[pl.ds(land, size)], sem, (other, row))
+                moved.append((p, copy, land, size))
+                sem, land = sem + 1, land + size
+        yield
+        for p, copy, at, size in moved:
+            copy.wait_recv()
+            add(finals[p], size, at)
+        moved = []
+        for p in parts:
+            size = sizes[p] // dp_count
+            at = finals[p]
+            done = acc[pl.ds(al(at), size), :]
+            small[5:6, :] += jnp.sum(done * done, axis=0, keepdims=True)
+            gathered[pl.ds(al(at), size), :] = done.astype(bf)
+            squared[first] = True
+            for k in range(1, dp_count):
+                other = lax.rem(dp + k, dp_count)
+                send(gathered, at, size, gathered.at[pl.ds(al(at), size)], sem, (other, row))
+                moved.append((p, k, size, sem))
+                sem += 1
+        yield
+        for p, k, size, one in moved:
+            source = lax.rem(dp + dp_count - k, dp_count)
+            expect(starts[p] + source * size, size, one, (source, row))
+        for step in range(bits - 2, -1, -1):
+            moved = []
+            for p in parts:
+                mine, where = partner(part_orders[p][step])
+                send(gathered, starts[p], sizes[p], gathered.at[pl.ds(al(starts[p]), sizes[p])], sem, where)
+                moved.append((p, mine, where, sem))
+                sem += 1
+            yield
+            for p, mine, where, one in moved:
+                bottom = starts[p] - mine * sizes[p]
+                expect(bottom + (1 - mine) * sizes[p], sizes[p], one, where)
+                starts[p], sizes[p] = bottom, 2 * sizes[p]
+        mine, where = partner(0)
+        send(gathered, first + mine * half_rows, half_rows, gathered.at[pl.ds(al(first + mine * half_rows), half_rows)], sem, where)
+        yield
+        expect(first + (1 - mine) * half_rows, half_rows, sem, where)
+
+    for copy in gathers:
+        copy.wait_send()
+    rows_early = 2 * ff + inner
+    rows_late = 3 * inner + tokens
+    sems_each = send_r.shape[0] // 2
+    early = summing(0, rows_early, 0, 0)
+    late = summing(rows_early, rows_late, sems_each, rows_early)
+
     query[...] = output[...].astype(bf)
     for k in range(ff // width):
-        grad_down[k * width : (k + 1) * width, :] = dot_tn(active[:, k * width : (k + 1) * width], query[...])
+        acc[k * width : (k + 1) * width, :] = dot_tn(active[:, k * width : (k + 1) * width], query[...])
     scatter_wait(1, 0)
     if bits > 1:
         scatter_start(1, 1)
 
-    def feed_back(c, carry):
-        at = pl.multiple_of(c * half, half)
+    grad_attended, grad_middle_low = 2 * tokens, 4 * tokens
+
+    def feed_back(c, m):
+        at = pl.multiple_of(m * tokens + c * half, half)
+        near = pl.multiple_of(c * half, half)
         branch = query[pl.ds(at, half), :]
         for k in range(ff // width):
             active[pl.ds(at, half), k * width : (k + 1) * width] = (
@@ -1048,24 +1183,30 @@
         grad = grad + output[pl.ds(at, half), :]
         output[pl.ds(at, half), :] = grad
         grad_low = grad.astype(bf)
-        grad_middle_low[pl.ds(at, half), :] = grad_low
-        grad_attended[pl.ds(at, half), :] = dot_nt(grad_low, out_low[...]).astype(bf)
-        return carry
-
-    lax.fori_loop(0, chunks, feed_back, 0)
-    grad_up[...] = dot_tn(hidden_two[...], active[...])
-    grad_out[...] = dot_tn(attended[...], grad_middle_low[...])
+        grad_logits[pl.ds(near, half), grad_middle_low + m * width : grad_middle_low + (m + 1) * width] = grad_low
+        grad_logits[pl.ds(near, half), grad_attended + m * inner : grad_attended + (m + 1) * inner] = dot_nt(
+            grad_low, out_low[...]
+        ).astype(bf)
+
+    for m in range(micro):
+        lax.fori_loop(0, 2, lambda c, carry, m=m: (feed_back(c, m), carry)[1], 0)
+    for k in range(ff // width):
+        acc[ff + k * width : ff + (k + 1) * width, :] = dot_tn(hidden_two[...], active[:, k * width : (k + 1) * width])
+    acc[2 * ff : 2 * ff + inner, :] = dot_tn(
+        attended[:tokens, :], grad_logits[:, grad_middle_low : grad_middle_low + width]
+    ) + dot_tn(attended[tokens:, :], grad_logits[:, grad_middle_low + width : grad_middle_low + 2 * width])
+    next(early, None)
     for step in range(1, bits - 1):
         for m in range(micro):
             scatter_wait(m, step)
             scatter_start(m, step + 1)
 
-    def attend_back(m):
+    def attend_back(m, begin, end):
         base = m * tokens
 
         def pair(hp, carry):
             lanes = [pl.ds(pl.multiple_of(k * inner + hp * 128, 128), 128) for k in range(3)]
-            here = pl.ds(pl.multiple_of(hp * 128, 128), 128)
+            here = pl.ds(pl.multiple_of(grad_attended + m * inner + hp * 128, 128), 128)
             keys = joined[base : base + tokens, lanes[1]]
             values = joined[base : base + tokens, lanes[2]]
             for rb in (1, 0):
@@ -1073,21 +1214,22 @@
                 span = (rb + 1) * half
                 probs = probs_low if rb else probs_top
                 queries = joined[first : first + half, lanes[0]]
-                upper = grad_attended[first : first + half, here]
+                upper = grad_logits[rb * half : (rb + 1) * half, here]
                 for h in range(2):
-                    scores[h, :, :span] = dot_nt(upper * head_mask[h], values[:span])
+                    logits[:, h * tokens : h * tokens + span] = dot_nt(upper * head_mask[h], values[:span])
                 for h in range(2):
                     for s in range(half // sub):
                         chance = probs[m * 2 * pairs + hp * 2 + h, s * sub : (s + 1) * sub, :].astype(jnp.float32)
-                        grad = scores[h, s * sub : (s + 1) * sub, :span]
+                        grad = logits[s * sub : (s + 1) * sub, h * tokens : h * tokens + span]
                         inner_sum = jnp.sum(chance * grad, axis=1, keepdims=True)
-                        grad_scores[h, s * sub : (s + 1) * sub, :span] = (chance * (grad - inner_sum)).astype(bf)
-                total_q = dot_nn(grad_scores[0, :, :span], keys[:span] * head_mask[0]) + dot_nn(
-                    grad_scores[1, :, :span], keys[:span] * head_mask[1]
+                        grad_logits[s * sub : (s + 1) * sub, h * tokens : h * tokens + span] = (
+                            chance * (grad - inner_sum)
+                        ).astype(bf)
+                pieces = [grad_logits[:half, h * tokens : h * tokens + span] for h in range(2)]
+                total_q = dot_nn(pieces[0], keys[:span] * head_mask[0]) + dot_nn(
+                    pieces[1], keys[:span] * head_mask[1]
                 )
-                total_k = dot_tn(grad_scores[0, :, :span], queries * head_mask[0]) + dot_tn(
-                    grad_scores[1, :, :span], queries * head_mask[1]
-                )
+                total_k = dot_tn(pieces[0], queries * head_mask[0]) + dot_tn(pieces[1], queries * head_mask[1])
                 total_v = dot_tn(probs[m * 2 * pairs + hp * 2], upper * head_mask[0]) + dot_tn(
                     probs[m * 2 * pairs + hp * 2 + 1], upper * head_mask[1]
                 )
@@ -1102,10 +1244,14 @@
             joined[base : base + tokens, lanes[2]] = part_v[...].astype(bf)
             return carry
 
-        lax.fori_loop(0, pairs, pair, 0)
-
-    attend_back(0)
-    attend_back(1)
+        lax.fori_loop(begin, end, pair, 0)
+
+    for m in range(micro):
+        for begin in range(0, pairs, 2):
+            attend_back(m, begin, min(begin + 2, pairs))
+            next(early, None)
+
+    place = rows_early + 3 * inner
 
     def project_back(c, carry):
         at = pl.multiple_of(c * half, half)
@@ -1114,47 +1260,162 @@
         grad, gain_part = rms_back(embedded[pl.ds(at, half), :], gain_one, grad_hidden)
         small[0:1, :] += gain_part
         grad = grad + output[pl.ds(at, half), :]
-        grad_positions[pl.ds(near, half), :] += grad
+        acc[pl.ds(pl.multiple_of(place + near, half), half), :] += grad
         row_grads[pl.ds(at, half), :] = (scaling * grad).astype(bf)
         return carry
 
-    grad_positions[...] = jnp.zeros_like(grad_positions)
+    acc[place : place + tokens, :] = jnp.zeros((tokens, width), jnp.float32)
     lax.fori_loop(0, chunks, project_back, 0)
-    for k in range(3 * inner // 512):
-        grad_qkv[:, k * 512 : (k + 1) * 512] = dot_tn(hidden_one[...], joined[:, k * 512 : (k + 1) * 512])
+    next(early, None)
+    for k in range(3 * inner // width):
+        acc[rows_early + k * width : rows_early + (k + 1) * width, :] = dot_tn(
+            hidden_one[...], joined[:, k * width : (k + 1) * width]
+        )
+    next(late, None)
     for m in range(micro):
         if bits > 1:
             scatter_wait(m, bits - 1)
+    next(early, None)
+
+    out_at = rows_early + rows_late
+    slot_row = jnp.concatenate([slots[c : c + 1, :] for c in range(slots.shape[0])], axis=1)
+    slot_index = lax.broadcasted_iota(jnp.int32, (capacity, slot_row.shape[1]), 0).astype(jnp.float32)
+
+    def arrange(other):
+        pick = one_hot(slot_index == slot_row - (other * capacity).astype(jnp.float32))
+        return dot_nn(pick, row_grads[...]).astype(bf)
+
+    def block_copy(k):
+        other, where = other_device(k, dp_count, row_count)
+        return pltpu.make_async_remote_copy(
+            cand.at[pl.ds(al(out_at + k * capacity), capacity)], incoming.at[pl.ds(al(k * capacity), capacity)],
+            send_a.at[k], recv_a.at[k], device_id=where, device_id_type=MESH,
+        )
+
+    def send_rows(k, carry):
+        other, where = other_device(k, dp_count, row_count)
+        cand[pl.ds(al(out_at + k * capacity), capacity), :] = arrange(other)
+        block_copy(k).start()
+        return carry
+
+    lax.fori_loop(1, devices // 2, send_rows, 0)
+    next(late, None)
+    next(early, None)
+    lax.fori_loop(devices // 2, devices, send_rows, 0)
+    incoming[0:capacity, :] = arrange(dp * row_count + row)
+    next(late, None)
+    next(early, None)
+
+    groups = 4
+    each = devices // groups
+    tile = 256
+    tiles = -(-rows_here // tile)
+    in_logits = logits.shape[1] // tile
+
+    def add_table(g):
+        span = each * capacity
+        ids = received[:, g * span : (g + 1) * span]
+        rows = incoming[g * span : (g + 1) * span, :]
+        near = one_hot(lax.broadcasted_iota(jnp.int32, (tile, span), 0) == jnp.bitwise_and(ids, tile - 1))
+        high = jnp.right_shift(ids, 8)
+
+        def one(t, at_row, at_lane, ref):
+            value = dot_nn(near * one_hot(high == t), rows)
+            where = (pl.ds(pl.multiple_of(at_row, tile), tile), pl.ds(pl.multiple_of(at_lane, tile), tile))
+            if g:
+                value = value + ref[where]
+            ref[where] = value
+            if g == groups - 1:
+                small[5:6, :] += jnp.sum(value * value, axis=0, keepdims=True)
+
+        def first_ones(t, carry):
+            one(t, 0, t * tile, logits)
+            return carry
+
+        def other_ones(t, carry):
+            u = t - in_logits
+            one(t, (u // (ff // tile)) * tile, lax.rem(u, ff // tile) * tile, slope)
+            return carry
+
+        lax.fori_loop(0, min(tiles, in_logits), first_ones, 0)
+        if tiles > in_logits:
+            lax.fori_loop(in_logits, tiles, other_ones, 0)
+
+    for g in range(groups):
+        lax.fori_loop(max(1, g * each), (g + 1) * each, lambda k, c: (block_copy(k).wait_recv(), c)[1], 0)
+        add_table(g)
+        next(late, None)
+        next(early, None)
+    stores = []
+    for t in range(tiles):
+        count = min(tile, rows_here - t * tile)
+        if t < in_logits:
+            source = logits.at[pl.ds(0, count), pl.ds(t * tile, tile)]
+        else:
+            u = t - in_logits
+            source = slope.at[pl.ds((u // (ff // tile)) * tile, count), pl.ds((u % (ff // tile)) * tile, tile)]
+        copy = pltpu.make_async_copy(source, table_grads.at[pl.ds(t * tile, count)], store_sem.at[t])
+        copy.start()
+        stores.append(copy)
+
+    def spread(source, zone, mine, others, where, base):
+        for k, other in enumerate(others):
+            copy = pltpu.make_async_remote_copy(
+                source, zone.at[mine], send_n.at[base + k], recv_n.at[base + mine],
+                device_id=where(other), device_id_type=MESH,
+            )
+            copy.start()
+            pending.append(copy)
+        zone[mine] = source[...]
+        for other in others:
+            pltpu.make_async_remote_copy(
+                source, zone.at[other], send_n.at[base], recv_n.at[base + other],
+                device_id=where(other), device_id_type=MESH,
+            ).wait_recv()
+        return jnp.sum(zone[...], axis=0)
+
+    spread_rows = spread(
+        small, by_row, row, [lax.rem(row + k, row_count) for k in range(1, row_count)], lambda o: (dp, o), 0
+    )
+    row_small[...] = spread_rows
+    summed[...] = spread(
+        row_small, by_dp, dp, [lax.rem(dp + k, dp_count) for k in range(1, dp_count)], lambda o: (o, row), row_count
+    )
+    for summer in (late, early):
+        for unused in summer:
+            pass
+    for copy in stores:
+        copy.wait()
+    lax.fori_loop(1, devices, lambda k, c: (block_copy(k).wait_send(), c)[1], 0)
     for copy in pending:
         copy.wait_send()
 
 
-def layer(row_count, lengths, items, targets, correction, matrices, positions, gains):
+def layer(dp_count, row_count, capacity, rows_here, lengths, items, targets, correction, matrices, positions, gains,
+          slots, received):
     qkv, out, up, down = matrices
     tokens, width = positions.shape
     half = tokens // 2
     inner, ff = out.shape[0], up.shape[1]
     events = 2 * tokens
     group = row_count * tokens
+    devices = dp_count * row_count
     bf, f32 = jnp.bfloat16, jnp.float32
     pairs = inner // 128
     bits = row_count.bit_length() - 1
     hops = 2 * (row_count - 1)
+    summed_rows = 2 * ff + 4 * inner + tokens
     sems = lambda count: pltpu.SemaphoreType.DMA((count,))
     hbm = pl.BlockSpec(memory_space=pl.ANY)
     return pl.pallas_call(
-        functools.partial(layer_kernel, row_count),
+        functools.partial(layer_kernel, dp_count, row_count, capacity, rows_here),
         out_shape=(
-            jax.ShapeDtypeStruct(qkv.shape, f32),
-            jax.ShapeDtypeStruct(out.shape, f32),
-            jax.ShapeDtypeStruct(up.shape, f32),
-            jax.ShapeDtypeStruct(down.shape, f32),
-            jax.ShapeDtypeStruct(positions.shape, f32),
-            jax.ShapeDtypeStruct((2 * events, width), bf),
+            jax.ShapeDtypeStruct((rows_here, width), f32),
+            jax.ShapeDtypeStruct((summed_rows, width), bf),
             jax.ShapeDtypeStruct((8, width), f32),
         ),
-        in_specs=[pl.BlockSpec(memory_space=pltpu.SMEM), VMEM, VMEM, VMEM, hbm, hbm, hbm, hbm, VMEM, VMEM],
-        out_specs=(VMEM,) * 7,
+        in_specs=[pl.BlockSpec(memory_space=pltpu.SMEM), VMEM, VMEM, VMEM, hbm, hbm, hbm, hbm] + [VMEM] * 4,
+        out_specs=(hbm, VMEM, VMEM),
         scratch_shapes=[
             pltpu.VMEM(qkv.shape, bf),
             pltpu.VMEM(out.shape, bf),
@@ -1172,17 +1433,21 @@
             pltpu.VMEM((events, ff), bf),
             pltpu.VMEM((events, width), f32),
             pltpu.VMEM((events, width), bf),
-            pltpu.VMEM((2, group, width), bf),
+            pltpu.VMEM((2 * group, width), bf),
             pltpu.VMEM((row_count, 2, tokens), f32),
-            pltpu.VMEM((2, group, width), bf),
+            pltpu.VMEM((2 * group, width), bf),
             pltpu.VMEM((hops, tokens, width), bf),
             pltpu.VMEM((half, group), f32),
             pltpu.VMEM((tokens, group), bf),
             pltpu.VMEM((half, 128), f32),
-            pltpu.VMEM((2, half, tokens), f32),
-            pltpu.VMEM((2, half, tokens), bf),
-            pltpu.VMEM((events, width), bf),
-            pltpu.VMEM((events, inner), bf),
+            pltpu.VMEM((2 * events, width), bf),
+            pltpu.VMEM((8, width), f32),
+            pltpu.VMEM((summed_rows, width), f32),
+            pltpu.VMEM((summed_rows, width), bf),
+            pltpu.VMEM((devices * capacity, width), bf),
+            pltpu.VMEM((row_count, 8, width), f32),
+            pltpu.VMEM((dp_count, 8, width), f32),
+            pltpu.VMEM((8, width), f32),
             pltpu.VMEM((tokens, 128), f32),
             pltpu.VMEM((tokens, 128), f32),
             sems(2 + (inner + ff) // width),
@@ -1192,10 +1457,17 @@
             sems(hops),
             sems(hops),
             sems(hops),
+            sems(2 * (4 * bits + 4 * dp_count)),
+            sems(2 * (4 * bits + 4 * dp_count)),
+            sems(devices),
+            sems(devices),
+            sems(devices),
+            sems(devices),
+            sems(-(-rows_here // 256)),
         ],
         name="layer",
-        compiler_params=pltpu.CompilerParams(collective_id=5, has_side_effects=True, vmem_limit_bytes=60 * 2**20),
-    )(lengths, items, targets, correction, qkv, out, up, down, positions, gains)
+        compiler_params=pltpu.CompilerParams(collective_id=5, has_side_effects=True, vmem_limit_bytes=62 * 2**20),
+    )(lengths, items, targets, correction, qkv, out, up, down, positions, gains, slots, received)
 
 
 def small_kernel(dp_count, row_count, part, summed, by_row, by_dp, send_sem, recv_sem):
@@ -1363,21 +1635,38 @@
     )
     received = received[:, 0, :capacity].reshape(1, devices * capacity)
     fetched = fetched.reshape(2, micro, tokens, width)
-    fits = histories == 1 and micro == 2 and row_count * tokens <= 4096
+    weights = (qkv_weight, out_weight, up_weight, down_weight, positions)
+    summed_rows = sum(one.size for one in weights) // width
+    group = row_count * tokens
+    fits = (
+        histories == 1
+        and micro == 2
+        and row_count > 1
+        and devices % 4 == 0
+        and group <= 4096
+        and summed_rows % (16 * devices) == 0
+        and summed_rows + devices * capacity <= 2 * group
+        and rows_here <= 4096 + group
+    )
     if fits:
-        outs = layer(
+        table_grad, gathered, small = layer(
+            dp_count,
             row_count,
+            capacity,
+            rows_here,
             lengths.reshape(micro),
             fetched[0].reshape(micro * tokens, width),
             fetched[1].reshape(micro * tokens, width),
             correction.reshape(micro, tokens),
-            (qkv_weight, out_weight, up_weight, down_weight),
+            weights[:4],
             positions,
             gains,
-        )
-        running = outs[:4]
-        grad_positions, row_grads, small = outs[4:]
-        grad_gains, loss_local, count_local = small[:3], small[3, 0], small[4, 0]
+            slots,
+            received,
+        )
+        sum_gains, sum_loss, sum_count = small[:3], small[3, 0], small[4, 0]
+        square_total = jnp.sum(small[5])
+        order = (3, 2, 1, 0, 4)
     else:
         running, grad_positions, row_grads, grad_gains, loss_local = grouped_layer(
             fetched,
@@ -1389,45 +1678,42 @@
             gains,
         )
         count_local = jnp.sum(valid_pos.astype(jnp.float32))
-    incoming, gathered, square = tail_exchange(
-        dp_count,
-        row_count,
-        capacity,
-        running[0],
-        running[1],
-        running[2],
-        running[3],
-        grad_positions,
-        row_grads,
-        slots,
-    )
-    table_grad, table_square = table_gradient(
-        rows_here, received, incoming.reshape(devices * capacity, width)
-    )
-    own_square = jnp.sum(table_square[0] + square[0])
-    scalars = jnp.stack([loss_local, count_local, own_square])
-    part = jnp.concatenate(
-        [grad_gains.reshape(-1), jnp.pad(scalars, (0, 1024 - grad_gains.size - 3))]
-    ).reshape(8, 128)
-    small = small_sum(dp_count, row_count, part).reshape(-1)
-    sum_gains = small[: grad_gains.size].reshape(grad_gains.shape)
-    sum_loss, sum_count, square_total = (small[grad_gains.size + k] for k in range(3))
+        incoming, gathered, square = tail_exchange(
+            dp_count,
+            row_count,
+            capacity,
+            running[0],
+            running[1],
+            running[2],
+            running[3],
+            grad_positions,
+            row_grads,
+            slots,
+        )
+        table_grad, table_square = table_gradient(
+            rows_here, received, incoming.reshape(devices * capacity, width)
+        )
+        own_square = jnp.sum(table_square[0] + square[0])
+        scalars = jnp.stack([loss_local, count_local, own_square])
+        part = jnp.concatenate(
+            [grad_gains.reshape(-1), jnp.pad(scalars, (0, 1024 - grad_gains.size - 3))]
+        ).reshape(8, 128)
+        small = small_sum(dp_count, row_count, part).reshape(-1)
+        sum_gains = small[: grad_gains.size].reshape(grad_gains.shape)
+        sum_loss, sum_count, square_total = (small[grad_gains.size + k] for k in range(3))
+        order = (0, 2, 1, 3, 4)
     gathered = gathered.astype(jnp.float32)
     place = 0
-    blocks = []
-    for like in (qkv_weight, up_weight):
+    blocks = {}
+    for which_one in order:
+        like = weights[which_one]
         count = like.shape[1] // width
         piece = gathered[place : place + count * like.shape[0]]
-        blocks.append(
-            jnp.concatenate(
-                [piece[c * like.shape[0] : (c + 1) * like.shape[0]] for c in range(count)], axis=1
-            )
+        blocks[which_one] = jnp.concatenate(
+            [piece[c * like.shape[0] : (c + 1) * like.shape[0]] for c in range(count)], axis=1
         )
         place += count * like.shape[0]
-    for like in (out_weight, down_weight, positions):
-        blocks.append(gathered[place : place + like.shape[0]])
-        place += like.shape[0]
-    gradients = (table_grad, blocks[0], blocks[2], blocks[1], blocks[3], blocks[4], sum_gains)
+    gradients = (table_grad, blocks[0], blocks[1], blocks[2], blocks[3], blocks[4], sum_gains)
     grad_norm = jnp.sqrt(square_total + jnp.sum(sum_gains * sum_gains))
     factor = CLIP / jnp.maximum(grad_norm, CLIP)
     weights = (item_table, qkv_weight, out_weight, up_weight, down_weight, positions, gains)

time: 346 us -> 314 us (0.908)
  Pallas kernels: 292 us -> 268 us
  local copies, waits for them, and re-layouts: 15.6 us -> 9.83 us
    pallas_call x4 -> x1, Pallas kernels: 236 us -> 211 us  [layer(): pl.pallas_call(functools.partial(layer_kernel, dp_count, row_count, capac...]
    unnamed x56 -> x52, local copies, waits for them, and re-layouts: 10.4 us -> 6.21 us
where the time goes in v4:
time: 314 us; the launch traced here: 313 us
  Pallas kernels  268 us (85%)
  other arithmetic  32.3 us (10%)
  local copies, waits for them, and re-layouts  9.83 us (3%)
  between operations  3.4 us (1%)
    pallas_call x1, Pallas kernels, layer(): pl.pallas_call(functools.partial(layer_kernel, dp_count, row_count, capac...  211 us
    pallas_call x1, Pallas kernels, lookup(): pl.pallas_call(functools.partial(lookup_kernel, dp_count, row_count, capa...  56.4 us
    sub x6, other arithmetic, adam_step(): return (weight - rate * (stepped + decay * weight), first_new, second_new)  27.8 us

profile of v4, /device:TPU:0, one launch (start us, length us, event | category | flops | bytes accessed | tf_op | source)
XLA Modules:
  0.0 313.0 jit_solution(12240978571152597477)
XLA Ops:
  0.7 0.7 iota_compare_fusion
  1.4 0.7 fusion.6
  2.1 1.3 copy.53
  3.5 56.4 %lookup.1 = (bf16[2048,256]{1,0:T(8,128)(2,1)}, f32[8,256]{1,0:T(8,128)}, s32[32,1,128]{2,1,0:T(1,128)}) custom-call(s32[2048,1]{1,0:T(8,128)} %bitcast.16, s32[1568,128]{1,0:T(8,128)} %bitcast.17, f32[6272,256]{1,0:T(8,128)} %table_hbm.1), custom_call_target="tpu_custom_call" | custom-call | tf_op jit(solution)/shard_map/lookup/pallas_call | solution.py:600
  59.9 0.0 copy-start.21
  59.9 2.2 fusion.16
  62.2 0.6 copy.55
  62.8 0.0 copy-done.17
  62.8 0.7 reshape_squeeze.2.received
  63.5 211.1 %layer.1 = (f32[6272,256]{1,0:T(8,128)}, bf16[4608,256]{1,0:T(8,128)(2,1)}, f32[8,256]{1,0:T(8,128)}) custom-call(s32[2]{0:T(128)} %bitcast.23, bf16[1024,256]{1,0:T(8,128)(2,1)} %get-tuple-element.65.items, bf16[1024,256]{1,0:T(8,128)(2,1)} %get-tuple-element.64.targets, f32[2,512]{1,0:T(2,128)} %bitcast.19, f32[256,1536]{1,0:T(8,128)} %qkv_hbm.1, ...), custom_call_target="tpu_custom_call" | custom-call | tf_op jit(solution)/shard_map/layer/pallas_call | solution.py:1410
  274.6 1.3 slice_reduce_fusion.1
  275.9 1.3 multiply_reduce_fusion
  278.6 17.6 %multiply_subtract_fusion = (f32[6272,256]{1,0:T(8,128)}, f32[6272,256]{1,0:T(8,128)}, f32[6272,256]{1,0:T(8,128)}) fusion(f32[6272,256]{1,0:T(8,128)} %table_hbm.1, f32[6272,256]{1,0:T(8,128)} %get-tuple-element.34, f32[]{:T(128)S(6)} %div.96, f32[6272,256]{1,0:T(8,128)} %param.38, f32[6272,256]{1,0:T(8,128)} %param.45), kind=kLoop, calls=%fused_computation.2 | loop fusion | flops 25690112 | bytes 44957700 | tf_op jit(solution)/shard_map/sub | solution.py:223
  296.2 0.0 copy-start.7
  296.2 0.4 convert_element_type.3
  296.6 0.0 copy-start
  296.8 0.8 copy-done.6
  297.6 0.5 copy-done.7
  298.1 0.6 copy-done
  298.7 0.0 copy-start.14
  298.7 0.0 copy-start.15
  298.7 3.1 multiply_subtract_fusion.1
  301.8 0.0 copy-start.9
  301.8 2.2 multiply_subtract_fusion.4
  304.0 0.1 fusion.15
  304.1 1.1 copy-done.2
  305.2 0.3 copy-done.8
  305.5 2.2 multiply_subtract_fusion.3
  307.7 0.8 copy-done.11
  308.5 2.2 multiply_subtract_fusion.2
  310.7 0.6 add_subtract_fusion
  311.4 0.5 fusion.17
  (40 shorter events, 0.3 us)
Async XLA Ops:
  59.9 2.3 copy-start.21
  59.9 2.9 copy-start.17
  278.6 17.6 %copy-start.1 = (bf16[4608,256]{1,0:T(8,128)(2,1)S(1)}, bf16[4608,256]{1,0:T(8,128)(2,1)}, u32[]{:S(2)}) copy-start(bf16[4608,256]{1,0:T(8,128)(2,1)} %get-tuple-element.35) | copy-start | bytes 7077892
  296.2 1.4 copy-start.6
  296.2 1.9 copy-start.7
  296.6 2.1 copy-start
  298.6 3.1 copy-start.4
  298.6 3.1 copy-start.5
  298.6 3.1 copy-start.12
  298.6 3.1 copy-start.13
  298.7 3.1 copy-start.14
  298.7 3.1 copy-start.15
  301.8 2.3 copy-start.9
  304.0 1.2 copy-start.2
  304.0 1.5 copy-start.8
  305.5 2.2 copy-start.3
  305.5 2.2 copy-start.10
  305.5 3.0 copy-start.11
  308.5 2.2 copy-start.16
  308.5 2.2 copy-start.18
  308.5 2.2 copy-start.19
  308.5 2.2 copy-start.20
